TPU v7x, 256 devices: a whole 4x4x8 slice. The times are simulated.
256 devices in a mesh: row: 32 (over z, x), col: 8 (over y, core).
Axes of the slice: x: 4, y: 4, z: 8, core: 2. Of those that a mesh axis runs over, the one named last changes fastest.
Arguments:
- vectors: bfloat16 [256, 65536], P('col', 'row'), may hold values from -6 to 6
- hblocks: bfloat16 [1024, 12, 4096], P('row'), may hold values from -0.15625 to 0.15625
- counts: int32 [1024], P('row'), may hold values from 3 to 12, as said below
- sources: int32 [1024, 12], P('row'), may hold values from 0 to 95, as said below
- send_rows: int32 [2048], P('row'), may hold values from 0 to 31
Outputs:
- filtered: bfloat16 [256, 65536], P('col', 'row')
- gram_matrix: float32 [256, 256], P(None, 'col')
- projected: float32 [256, 256], P(None, 'col')
Inputs may be any that keep to these rules, and one draw needn't show every extreme that they name: Blocks 0 to counts[i] - 1 of block row i are live; the rows of every device include one with 12 live blocks. `sources`: entry 0 of block row i is i's own index within its device. On every device each slot value 32 + s, s below 64, stands exactly once, at block 1 or 2 of some row. `send_rows`: entries p * 64 + q * 2 + c name block rows of device p within it.
All inputs are finite; a program needn't handle non-finite values.
Results may differ from a plain program's by a relative error of at most 0.017.
Values may be sent and summed in bfloat16 or wider, within the bound.
No kernel may reach another device: no remote copies, remote signals or barrier semaphores. Data moves between devices by JAX's collectives and lax.ppermute only.
A program may use at most 128 MiB of HBM per device.

v0:
```python
import jax
import jax.numpy as jnp
from jax import lax
from jax.sharding import PartitionSpec as P

B = 64
K = 12


center_value = 0.25
half_width = 1.5


def on_device(vectors, hblocks, counts, sources, send_rows):
    rows_here = hblocks.shape[0]
    cols_here = vectors.shape[0]
    slots = send_rows.shape[0]
    live_mask = lax.broadcasted_iota(jnp.int32, (rows_here, K), 1) < counts[:, None]
    masked = jnp.where(live_mask[:, :, None], hblocks, jnp.zeros((), jnp.bfloat16)).reshape(
        rows_here, K, B, B
    )
    flat_sources = sources.reshape(-1)
    slot_table = lax.all_gather(send_rows, "row", axis=0, tiled=True)
    device_row = lax.axis_index("row")
    capacity = slots // lax.axis_size("row")
    positions = jnp.arange(slots, dtype=jnp.int32)
    peer_index = positions // capacity
    global_rows = (
        peer_index * rows_here
        + slot_table[peer_index * slots + device_row * capacity + positions % capacity]
    )

    def apply_operator(block_vectors):
        whole_blocks = lax.all_gather(block_vectors, "row", axis=0, tiled=True)
        incoming = whole_blocks[global_rows]
        extended = jnp.concatenate([block_vectors, incoming], 0)
        picked = extended[flat_sources].reshape(rows_here, K, cols_here, B)
        upper_part = jnp.einsum(
            "ikmb,ikab->ima", picked, masked, preferred_element_type=jnp.float32
        )
        mirror = jnp.einsum(
            "ima,ikab->ikmb", block_vectors, masked, preferred_element_type=jnp.float32
        )
        spread = jax.ops.segment_sum(
            mirror.reshape(rows_here * K, cols_here, B),
            flat_sources,
            num_segments=rows_here + slots,
        )
        returned = lax.all_to_all(
            spread[rows_here:], "row", split_axis=0, concat_axis=0, tiled=True
        )
        back_sums = jax.ops.segment_sum(returned, send_rows, num_segments=rows_here)
        return upper_part + spread[:rows_here] + back_sums

    start_blocks = vectors.reshape(cols_here, rows_here, B).transpose(1, 0, 2)
    start_float = start_blocks.astype(jnp.float32)
    first_image = apply_operator(start_blocks)
    first_step = ((first_image - center_value * start_float) / half_width).astype(jnp.bfloat16)
    second_image = apply_operator(first_step)
    second_step = (
        2.0 * (second_image - center_value * first_step.astype(jnp.float32)) / half_width
        - start_float
    ).astype(jnp.bfloat16)
    image_blocks = apply_operator(second_step).astype(jnp.bfloat16)
    filtered = second_step.transpose(1, 0, 2).reshape(cols_here, rows_here * B)
    image_rows = image_blocks.transpose(1, 0, 2).reshape(cols_here, rows_here * B)
    contract = (((1,), (1,)), ((), ()))
    stacked = jnp.concatenate([filtered, image_rows], 0)
    partial_value = lax.dot_general(
        lax.all_gather(filtered, "col", axis=0, tiled=True),
        stacked,
        contract,
        preferred_element_type=jnp.float32,
    )
    partial_value = partial_value.reshape(partial_value.shape[0], 2, cols_here)
    totals = lax.psum(partial_value.astype(jnp.bfloat16), "row").astype(jnp.float32)
    return (filtered, totals[:, 0, :], totals[:, 1, :])


def solution(mesh):
    return jax.shard_map(
        on_device,
        mesh=mesh,
        in_specs=(P("col", "row"), P("row", None, None), P("row"), P("row", None), P("row")),
        out_specs=(P("col", "row"), P(None, "col"), P(None, "col")),
        check_vma=False,
    )
```

profile of v0, /device:TPU:2, one launch (start us, length us, event | category | flops | bytes accessed | tf_op | source)
XLA Modules:
  0.0 541.9 jit_solution(17651293404976288670)
XLA Ops:
  7.2 1.2 reshape.175
  8.4 0.8 copy.75
  9.2 0.8 copy.26
  10.0 0.7 iota_compare_fusion
  10.7 2.2 broadcast_select_fusion
  12.8 7.9 %reshape.178 = bf16[32,12,64,64]{3,2,0,1:T(8,128)(2,1)} reshape(bf16[32,12,4096]{2,0,1:T(8,128)(2,1)S(1)} %broadcast_select_fusion) | data formatting | bytes 6291456 | tf_op jit(solution)/shard_map/reshape | solution.py:19
  20.8 6.3 %fusion = f32[32,12,64,32]{2,3,1,0:T(8,128)} fusion(bf16[32,12,64,64]{3,2,0,1:T(8,128)(2,1)} %reshape.178, bf16[32,32,64]{2,1,0:T(8,128)(2,1)S(1)} %reshape.175), kind=kOutput, calls=%fused_computation.14 | convolution fusion | flops 100663296 | bytes 6422528 | tf_op jit(solution)/shard_map/ima,ikab->ikmb/dot_general | solution.py:41
  27.2 0.2 broadcast.194.clone
  27.4 34.4 %scatter_fusion = f32[96,32,64]{2,1,0:T(8,128)S(1)} fusion(f32[96,32,64]{2,1,0:T(8,128)S(1)} %broadcast.194.clone, s32[384]{0:T(512)S(1)} %reshape.244, f32[384,32,64]{2,1,0:T(8,128)} %bitcast.74), kind=kCustom, calls=%fused_computation.7 | custom fusion | flops 786432 | bytes 9438720 | tf_op jit(solution)/shard_map/scatter-add | solution.py:44
  61.8 1.5 reshape.308
  63.3 11.6 %all-to-all-start = ((f32[32,1,4096]{2,1,0:T(1,128)}), f32[32,1,4096]{2,1,0:T(1,128)S(1)}, u32[]{:S(2)}, u32[]{:S(2)}) async-start(f32[32,1,4096]{2,1,0:T(1,128)} %reshape.308), calls=%async_computation | async-start | bytes 1048576 | tf_op jit(solution)/shard_map/all_to_all | solution.py:49
  75.1 0.6 dynamic-slice
  76.3 0.3 dynamic-update-slice
  76.6 25.6 %all-reduce = s32[2048]{0:T(1024)S(1)} all-reduce(s32[2048]{0:T(1024)S(1)} %dynamic-update-slice), channel_id=1, replica_groups=mesh['row'=32,'col'=8] {'row'}, use_global_device_ids=true, to_apply=%add | all-reduce | flops 2048 | bytes 16384
  102.3 0.8 gather_fusion
  103.1 0.5 broadcast.225
  103.6 1.9 reduce.2
  105.5 1.4 reshape.309
  106.9 12.9 %all-gather.5.cloned.1.call-done = bf16[1024,32,64]{2,1,0:T(8,128)(2,1)} async-done(((bf16[32,32,64]{2,1,0:T(8,128)(2,1)}), bf16[1024,32,64]{2,1,0:T(8,128)(2,1)}) %all-gather.5.cloned.1.call-update) | async-done | bytes 4194320 | tf_op jit(solution)/shard_map/all_gather | solution.py:34
  119.8 4.8 gather_fusion.1
  124.6 1.2 pad_maximum_fusion
  125.8 3.2 gather_fusion.2
  129.0 5.6 %fusion.27 = f32[32,32,64]{2,1,0:T(8,128)S(1)} fusion(bf16[32,12,32,64]{3,2,1,0:T(8,128)(2,1)} %bitcast.78, bf16[32,12,64,64]{3,2,0,1:T(8,128)(2,1)} %reshape.178, f32[96,32,64]{2,1,0:T(8,128)S(1)} %scatter_fusion), kind=kOutput, calls=%fused_computation.31 | convolution fusion | flops 100728832 | bytes 5242880 | tf_op jit(solution)/shard_map/ikmb,ikab->ima/dot_general | solution.py:38
  134.6 3.2 scatter_fusion.1
  137.7 0.8 fusion.32
  138.6 0.2 all-gather.11.cloned.1.call-start
  138.8 6.4 %fusion.4 = f32[32,12,64,32]{2,3,1,0:T(8,128)} fusion(bf16[32,12,64,64]{3,2,0,1:T(8,128)(2,1)} %reshape.178, bf16[32,32,64]{2,1,0:T(8,128)(2,1)} %fusion.32), kind=kOutput, calls=%fused_computation.18 | convolution fusion | flops 100663296 | bytes 6422528 | tf_op jit(solution)/shard_map/ima,ikab->ikmb/dot_general | solution.py:41
  145.2 0.2 broadcast.194.clone.1
  145.4 34.4 %scatter_fusion.2 = f32[96,32,64]{2,1,0:T(8,128)S(1)} fusion(f32[96,32,64]{2,1,0:T(8,128)S(1)} %broadcast.194.clone.1, s32[384]{0:T(512)S(1)} %reshape.244, f32[384,32,64]{2,1,0:T(8,128)} %bitcast.75), kind=kCustom, calls=%fused_computation.9 | custom fusion | flops 786432 | bytes 9438720 | tf_op jit(solution)/shard_map/scatter-add | solution.py:44
  179.8 1.0 slice.49
  180.9 1.9 reshape.310
  182.7 30.7 %all_to_all.15 = f32[32,1,4096]{2,1,0:T(1,128)S(1)} all-to-all(f32[32,1,4096]{2,1,0:T(1,128)S(1)} %reshape.310), channel_id=1, replica_groups=mesh['row'=32,'col'=8] {'row'}, dimensions={0} | all-to-all | bytes 1048576 | tf_op jit(solution)/shard_map/all_to_all | solution.py:49
  213.4 1.9 reduce.3
  215.3 1.4 reshape.311
  216.7 27.0 %all-gather.7.cloned.1.call-done = bf16[1024,32,64]{2,1,0:T(8,128)(2,1)} async-done(((bf16[32,32,64]{2,1,0:T(8,128)(2,1)}), bf16[1024,32,64]{2,1,0:T(8,128)(2,1)}) %all-gather.7.cloned.1.call-update) | async-done | bytes 4194320 | tf_op jit(solution)/shard_map/all_gather | solution.py:34
  243.7 4.0 gather_fusion.3
  247.7 0.2 pad_maximum_fusion.1
  247.9 3.2 gather_fusion.4
  251.1 5.5 %fusion.24 = f32[32,32,64]{2,1,0:T(8,128)S(1)} fusion(bf16[32,12,32,64]{3,2,1,0:T(8,128)(2,1)} %bitcast.79, bf16[32,12,64,64]{3,2,0,1:T(8,128)(2,1)} %reshape.178, f32[96,32,64]{2,1,0:T(8,128)S(1)} %scatter_fusion.2), kind=kOutput, calls=%fused_computation.30 | convolution fusion | flops 100728832 | bytes 5242880 | tf_op jit(solution)/shard_map/ikmb,ikab->ima/dot_general | solution.py:38
  256.6 6.1 %scatter_fusion.3 = f32[32,32,64]{2,1,0:T(8,128)S(1)} fusion(f32[32,32,64]{2,1,0:T(8,128)S(1)} %fusion.24, s32[64]{0:T(128)S(1)} %copy-done.6, f32[64,32,64]{2,1,0:T(8,128)} %reshape.311), kind=kCustom, calls=%fused_computation.10 | custom fusion | flops 131072 | bytes 1573120 | tf_op jit(solution)/shard_map/scatter-add | solution.py:52
  262.7 0.9 fusion.33
  263.6 6.4 %fusion.8 = f32[32,12,64,32]{2,3,1,0:T(8,128)} fusion(bf16[32,12,64,64]{3,2,0,1:T(8,128)(2,1)} %reshape.178, bf16[32,32,64]{2,1,0:T(8,128)(2,1)} %fusion.33), kind=kOutput, calls=%fused_computation.22 | convolution fusion | flops 100663296 | bytes 6422528 | tf_op jit(solution)/shard_map/ima,ikab->ikmb/dot_general | solution.py:41
  270.0 0.2 broadcast.194
  270.2 34.4 %scatter_fusion.4 = f32[96,32,64]{2,1,0:T(8,128)S(1)} fusion(f32[96,32,64]{2,1,0:T(8,128)S(1)} %broadcast.194, s32[384]{0:T(512)S(1)} %reshape.244, f32[384,32,64]{2,1,0:T(8,128)} %bitcast.73), kind=kCustom, calls=%fused_computation.11 | custom fusion | flops 786432 | bytes 9438720 | tf_op jit(solution)/shard_map/scatter-add | solution.py:44
  304.6 1.0 slice.51
  305.7 2.7 reshape.312
  308.3 7.4 %all-to-all-start.2 = ((f32[32,1,4096]{2,1,0:T(1,128)}), f32[32,1,4096]{2,1,0:T(1,128)S(1)}, u32[]{:S(2)}, u32[]{:S(2)}) async-start(f32[32,1,4096]{2,1,0:T(1,128)} %reshape.312), calls=%async_computation.2 | async-start | bytes 1048576 | tf_op jit(solution)/shard_map/all_to_all | solution.py:49
  315.8 0.3 all-gather.9.cloned.1.call-start
  316.1 0.1 copy.32
  316.2 0.9 reshape.182
  317.1 21.8 %all-to-all-done.2 = f32[32,1,4096]{2,1,0:T(1,128)S(1)} async-done(((f32[32,1,4096]{2,1,0:T(1,128)}), f32[32,1,4096]{2,1,0:T(1,128)S(1)}, u32[]{:S(2)}, u32[]{:S(2)}) %all-to-all-start.2) | async-done | bytes 524320 | tf_op jit(solution)/shard_map/all_to_all | solution.py:49
  338.9 1.9 reduce.4
  340.8 1.4 reshape.313
  342.2 25.8 %all-gather.11.cloned.1.call-done = bf16[1024,32,64]{2,1,0:T(8,128)(2,1)} async-done(((bf16[32,32,64]{2,1,0:T(8,128)(2,1)}), bf16[1024,32,64]{2,1,0:T(8,128)(2,1)}) %all-gather.11.cloned.1.call-update) | async-done | bytes 4194320 | tf_op jit(solution)/shard_map/all_gather | solution.py:34
  368.1 4.0 gather_fusion.5
  372.1 0.2 pad_maximum_fusion.2
  372.3 3.2 gather_fusion.6
  375.5 5.6 %fusion.21 = f32[32,32,64]{2,1,0:T(8,128)S(1)} fusion(bf16[32,12,32,64]{3,2,1,0:T(8,128)(2,1)} %bitcast.77, bf16[32,12,64,64]{3,2,0,1:T(8,128)(2,1)} %reshape.178, f32[96,32,64]{2,1,0:T(8,128)S(1)} %scatter_fusion.4), kind=kOutput, calls=%fused_computation.29 | convolution fusion | flops 100728832 | bytes 5242880 | tf_op jit(solution)/shard_map/ikmb,ikab->ima/dot_general | solution.py:38
  381.1 3.2 scatter_fusion.5
  384.4 0.3 reshape.185
  384.7 10.3 %all-gather.9.cloned.1.call-done = bf16[256,2048]{1,0:T(8,128)(2,1)} async-done(((bf16[32,2048]{1,0:T(8,128)(2,1)}), bf16[256,2048]{1,0:T(8,128)(2,1)}) %all-gather.9.cloned.1.call-update) | async-done | bytes 1048592 | tf_op jit(solution)/shard_map/all_gather | solution.py:70
  395.0 1.7 convolution_convert_fusion
  396.6 138.1 %psum.7 = bf16[256,2,32]{0,2,1:T(8,128)(2,1)S(1)} all-reduce(bf16[256,2,32]{0,2,1:T(8,128)(2,1)S(1)} %bitcast.82), channel_id=1, replica_groups=mesh['row'=32,'col'=8] {'row'}, use_global_device_ids=true, to_apply=%region_6.7 | all-reduce | flops 16384 | bytes 65536 | tf_op jit(solution)/shard_map/psum | solution.py:76
  534.8 0.6 slice_bitcast_fusion
  (36 shorter events, 0.7 us)
Async XLA Ops:
  7.2 112.6 %all-gather.5.cloned.1.call-start = ((), (), s32[]{:S(2)}) async-start(), calls=%async_computation.3 | async-start | bytes 8650752 | tf_op jit(solution)/shard_map/all_gather | solution.py:34
  27.3 47.7 %copy-start.7 = (u32[256]{0:T(256)S(1)}, u32[256]{0:T(256)}, u32[]{:S(2)}) copy-start(u32[256]{0:T(256)} %constant.65) | copy-start | bytes 3076
  27.4 49.0 %copy-start.6 = (s32[64]{0:T(128)S(1)}, s32[64]{0:T(128)}, u32[]{:S(2)}) copy-start(s32[64]{0:T(128)} %param.9) | copy-start | bytes 772
  61.7 62.8 %copy-start.4 = (bf16[32,32,64]{2,0,1:T(8,128)(2,1)S(1)}, bf16[32,32,64]{2,0,1:T(8,128)(2,1)}, u32[]{:S(2)}) copy-start(bf16[32,32,64]{2,0,1:T(8,128)(2,1)} %copy.75) | copy-start | bytes 393220
  63.3 39.8 %all-to-all-start = ((f32[32,1,4096]{2,1,0:T(1,128)}), f32[32,1,4096]{2,1,0:T(1,128)S(1)}, u32[]{:S(2)}, u32[]{:S(2)}) async-start(f32[32,1,4096]{2,1,0:T(1,128)} %reshape.308), calls=%async_computation | async-start | bytes 1048576 | tf_op jit(solution)/shard_map/all_to_all | solution.py:49
  74.9 168.8 %all-gather.7.cloned.1.call-start = ((), (), s32[]{:S(2)}) async-start(), calls=%async_computation.4 | async-start | bytes 8650752 | tf_op jit(solution)/shard_map/all_gather | solution.py:34
  129.0 5.6 %copy-start.3 = (f32[64,32,64]{2,1,0:T(8,128)S(1)}, f32[64,32,64]{2,1,0:T(8,128)}, u32[]{:S(2)}) copy-start(f32[64,32,64]{2,1,0:T(8,128)} %reshape.309) | copy-start | bytes 1572868
  138.6 229.5 %all-gather.11.cloned.1.call-start = ((), (), s32[]{:S(2)}) async-start(), calls=%async_computation.6 | async-start | bytes 8650752 | tf_op jit(solution)/shard_map/all_gather | solution.py:34
  179.8 67.9 %copy-start.1 = (bf16[32,32,64]{2,1,0:T(8,128)(2,1)S(1)}, bf16[32,32,64]{2,1,0:T(8,128)(2,1)}, u32[]{:S(2)}) copy-start(bf16[32,32,64]{2,1,0:T(8,128)(2,1)} %fusion.32) | copy-start | bytes 393220
  270.2 45.9 %copy-start = (bf16[32,32,64]{2,1,0:T(8,128)(2,1)S(1)}, bf16[32,32,64]{2,1,0:T(8,128)(2,1)}, u32[]{:S(2)}) copy-start(bf16[32,32,64]{2,1,0:T(8,128)(2,1)} %fusion.33) | copy-start | bytes 393220
  308.3 30.6 %all-to-all-start.2 = ((f32[32,1,4096]{2,1,0:T(1,128)}), f32[32,1,4096]{2,1,0:T(1,128)S(1)}, u32[]{:S(2)}, u32[]{:S(2)}) async-start(f32[32,1,4096]{2,1,0:T(1,128)} %reshape.312), calls=%async_computation.2 | async-start | bytes 1048576 | tf_op jit(solution)/shard_map/all_to_all | solution.py:49
  315.8 79.2 %all-gather.9.cloned.1.call-start = ((), (), s32[]{:S(2)}) async-start(), calls=%async_computation.5 | async-start | bytes 1179648 | tf_op jit(solution)/shard_map/all_gather | solution.py:70
  375.5 5.6 %copy-start.2 = (f32[64,32,64]{2,1,0:T(8,128)S(1)}, f32[64,32,64]{2,1,0:T(8,128)}, u32[]{:S(2)}) copy-start(f32[64,32,64]{2,1,0:T(8,128)} %reshape.313) | copy-start | bytes 1572868
  375.5 19.5 %copy-start.5 = (bf16[32,2048]{1,0:T(8,128)(2,1)S(1)}, bf16[32,2048]{1,0:T(8,128)(2,1)}, u32[]{:S(2)}) copy-start(bf16[32,2048]{1,0:T(8,128)(2,1)} %reshape.182) | copy-start | bytes 393220
Sparse Core Ops, SparseCore 0:
  10.6 109.1 all-gather.4
  138.7 104.9 all-gather.6
  263.7 104.3 all-gather.10
  370.4 24.5 all-gather.8
where the time goes:
time: 549 us; the launch traced here: 542 us
  blocking collectives  194 us (35%)
  other arithmetic  127 us (23%)
  waiting for transfers between devices  97.8 us (18%)
  local copies, waits for them, and re-layouts  50.4 us (9%)
  matrix products  37.5 us (7%)
  starting transfers between devices  19.6 us (4%)
  between operations  14.8 us (3%)
    psum x1, blocking collectives, on_device(): lax.psum(partial_value.astype(jnp.bfloat16), 'row').astype(jnp.float32)  138 us
    scatter-add x3, other arithmetic, apply_operator(): jax.ops.segment_sum(mirror.reshape(rows_here * K, cols_here, B), flat_sou...  103 us
    all_gather x3, waiting for transfers between devices, apply_operator(): whole_blocks = lax.all_gather(block_vectors, 'row', axis=0, tiled=True)  65.7 us
    all_to_all x1, blocking collectives, apply_operator(): lax.all_to_all(spread[rows_here:], 'row', split_axis=0, concat_axis=0, ti...  30.7 us
    unnamed x1, blocking collectives  25.6 us
    all_to_all x2, waiting for transfers between devices, apply_operator(): lax.all_to_all(spread[rows_here:], 'row', split_axis=0, concat_axis=0, ti...  21.8 us
    dot_general x3, matrix products, apply_operator(): jnp.einsum('ima,ikab->ikmb', block_vectors, masked, preferred_element_typ...  19.2 us
    all_to_all x2, starting transfers between devices, apply_operator(): lax.all_to_all(spread[rows_here:], 'row', split_axis=0, concat_axis=0, ti...  19 us
  transfers between devices with their start and end apart: 6, of which 5 were waited for; matrix products, arithmetic and copies ran while one was open for 32% of the time, Pallas kernels for 0%

commit v1 on v0

v1 whole, which is shorter than its diff:
```python
import jax
import jax.numpy as jnp
from jax import lax
from jax.experimental import pallas as pl
from jax.experimental.pallas import tpu as pltpu
from jax.sharding import Mesh, PartitionSpec as P

B = 64
K = 12
RB = 32
MC = 32
PEERS = 32
NZ, NX, NY, NC = 8, 4, 4, 2
STEP = 8
LOCAL = ((0, 3), (4, 5), (6, 7), (8, 9), (10, 11))
LW = 128 * len(LOCAL)
center_value = 0.25
half_width = 1.5
bf16 = jnp.bfloat16
f32 = jnp.float32
VMEM_LIMIT = 40 * 1024 * 1024

NN = (((1,), (0,)), ((), ()))
NT = (((1,), (1,)), ((), ()))


def low_half(rows=MC):
    return lax.broadcasted_iota(jnp.int32, (rows, 128), 1) < B


def dot(a, b, dims):
    return lax.dot_general(a, b, dims, preferred_element_type=f32)


def store_pair(even_odd_ref, first, second, low):
    even_odd_ref[pl.ds(0, 32, stride=2), :] = jnp.where(low, first, pltpu.roll(second, B, 1))
    even_odd_ref[pl.ds(1, 32, stride=2), :] = jnp.where(low, pltpu.roll(first, B, 1), second)


def duplicate(tile, low):
    turned = pltpu.roll(tile, B, 1)
    return jnp.where(low, tile, turned), jnp.where(low, turned, tile)


def emit_picks(msg_ref, dup_ref, send_ref, low):
    for q in range(PEERS):
        msg_ref[q, 0:MC, :] = jnp.where(
            low, dup_ref[send_ref[2 * q]], dup_ref[send_ref[2 * q + 1]]
        ).astype(bf16)


def emit_mirror(msg_ref, prod_ref, inv_ref, low):
    for q in range(PEERS):
        msg_ref[q, MC : 2 * MC, :] = jnp.where(
            low, prod_ref[inv_ref[2 * q]], prod_ref[inv_ref[2 * q + 1]]
        ).astype(bf16)


def invert_slots(inv_ref, src_ref):
    for i in range(RB):
        for k in (1, 2):
            inv_ref[src_ref[i, k] - RB] = 2 * i + k - 1


def first_message_kernel(src_ref, send_ref, v_ref, hb_ref, msg_ref, wd_ref, rows_ref, pair_ref, dup_ref, prod_ref, inv_ref):
    step = pl.program_id(0)
    low = low_half()

    @pl.when(step == 0)
    def _():
        for t in range(RB // 2):
            tile = v_ref[:, 128 * t : 128 * (t + 1)].astype(f32)
            dup_ref[2 * t], dup_ref[2 * t + 1] = duplicate(tile, low)
        invert_slots(inv_ref, src_ref)
        emit_picks(msg_ref, dup_ref, send_ref, low)

    for il in range(STEP):
        for j in range(32):
            rows_ref[il, 8 * j : 8 * (j + 1), :] = hb_ref[il, 0:8, 128 * j : 128 * (j + 1)].astype(f32)
        for k in (1, 2):
            block = rows_ref[il, pl.ds(k, 32, stride=8), :]
            store_pair(pair_ref.at[2 * il + k - 1], block, block, low)
        wd_ref[il, :, 0:128] = pair_ref[2 * il].astype(bf16)
        wd_ref[il, :, 128:256] = pair_ref[2 * il + 1].astype(bf16)
    for il in range(STEP):
        i = step * STEP + il
        prod = dot(dup_ref[i][:, 0:B].astype(bf16), wd_ref[il], NN)
        prod_ref[2 * i] = prod[:, 0:128]
        prod_ref[2 * i + 1] = prod[:, 128:256]

    @pl.when(step == RB // STEP - 1)
    def _():
        emit_mirror(msg_ref, prod_ref, inv_ref, low)


def local_product(src_ref, v_ref, um_ref, y_ref, dup_ref, dupb_ref, lhs_ref, mir_ref, acc_ref):
    low = low_half()
    for t in range(RB // 2):
        tile = v_ref[:, 128 * t : 128 * (t + 1)].astype(f32)
        one, two = duplicate(tile, low)
        dup_ref[2 * t], dup_ref[2 * t + 1] = one, two
        dupb_ref[2 * t], dupb_ref[2 * t + 1] = one.astype(bf16), two.astype(bf16)

    def gather(i, _):
        for t, (k0, k1) in enumerate(LOCAL):
            j0 = i if k0 == 0 else jnp.minimum(src_ref[i, k0], RB - 1)
            j1 = jnp.minimum(src_ref[i, k1], RB - 1)
            lhs_ref[i, :, 128 * t : 128 * (t + 1)] = jnp.where(low, dup_ref[j0], dup_ref[j1]).astype(bf16)
        return 0

    lax.fori_loop(0, RB, gather, 0, unroll=4)
    for i in range(RB):
        mir_ref[i] = dot(dupb_ref[i][:, 0:B], um_ref[i], NN)
    for i in range(RB):
        acc_ref[i, :, 0:B] = dot(lhs_ref[i], um_ref[i], NT)
        acc_ref[i, :, B:128] = jnp.zeros((MC, B), f32)

    def scatter(i, _):
        for t, (k0, k1) in enumerate(LOCAL):
            j0 = i if k0 == 0 else jnp.minimum(src_ref[i, k0], RB - 1)
            j1 = jnp.minimum(src_ref[i, k1], RB - 1)
            part = mir_ref[i, :, 128 * t : 128 * (t + 1)]
            acc_ref[j0] += jnp.where(low, part, 0.0)
            acc_ref[j1] += jnp.where(low, 0.0, part)
        return 0

    lax.fori_loop(0, RB, scatter, 0, unroll=4)
    for t in range(RB // 2):
        one, two = acc_ref[2 * t], acc_ref[2 * t + 1]
        y_ref[:, 128 * t : 128 * (t + 1)] = jnp.where(
            low, one + pltpu.roll(one, B, 1), two + pltpu.roll(two, B, 1)
        )


def first_local_kernel(src_ref, counts_ref, v_ref, hb_ref, um_ref, y_ref, rows_ref, pair_ref, dup_ref, dupb_ref, lhs_ref, mir_ref, acc_ref):
    step = pl.program_id(0)
    low = low_half()
    for il in range(STEP):
        i = step * STEP + il
        count = counts_ref[i]
        for j in range(32):
            rows_ref[il, 16 * j : 16 * j + K, :] = hb_ref[il, :, 128 * j : 128 * (j + 1)].astype(f32)
        for t, (k0, k1) in enumerate(LOCAL):
            one = rows_ref[il, pl.ds(k0, 32, stride=16), :]
            two = rows_ref[il, pl.ds(k1, 32, stride=16), :]
            if k0 >= 3:
                one = jnp.where(k0 < count, one, 0.0)
            two = jnp.where(k1 < count, two, 0.0)
            pair = pair_ref.at[il * len(LOCAL) + t]
            store_pair(pair, one, two, low)
            um_ref[i, :, 128 * t : 128 * (t + 1)] = pair[...].astype(bf16)

    @pl.when(step == RB // STEP - 1)
    def _():
        local_product(src_ref, v_ref, um_ref, y_ref, dup_ref, dupb_ref, lhs_ref, mir_ref, acc_ref)


def remote_sum(src_ref, send_ref, recv_ref, wd_ref, lhs_ref, acc_ref):
    low = low_half()
    lane = lax.broadcasted_iota(jnp.int32, (MC, 128), 1) // B

    def gather(i, _):
        for k in (1, 2):
            s = src_ref[i, k] - RB
            tile = recv_ref[s // 2, 0:MC, :].astype(f32)
            lhs_ref[i, :, 128 * (k - 1) : 128 * k] = jnp.where(lane == s % 2, tile, 0.0).astype(bf16)
        return 0

    lax.fori_loop(0, RB, gather, 0, unroll=4)
    for i in range(RB):
        acc_ref[i, :, 0:B] = dot(lhs_ref[i], wd_ref[i], NT)
        acc_ref[i, :, B:128] = jnp.zeros((MC, B), f32)

    def scatter(q, _):
        tile = recv_ref[q, MC : 2 * MC, :].astype(f32)
        acc_ref[send_ref[2 * q]] += jnp.where(low, tile, 0.0)
        acc_ref[send_ref[2 * q + 1]] += jnp.where(low, 0.0, tile)
        return 0

    lax.fori_loop(0, PEERS, scatter, 0, unroll=4)


def folded(acc_ref, t, low):
    one, two = acc_ref[2 * t], acc_ref[2 * t + 1]
    return jnp.where(low, one + pltpu.roll(one, B, 1), two + pltpu.roll(two, B, 1))


def step_kernel(second, src_ref, send_ref, recv_ref, y_ref, v_ref, prev_ref, wd_ref, out_ref, msg_ref, lhs_ref, acc_ref, dup_ref, prod_ref, inv_ref):
    low = low_half()
    invert_slots(inv_ref, src_ref)
    remote_sum(src_ref, send_ref, recv_ref, wd_ref, lhs_ref, acc_ref)
    for t in range(RB // 2):
        lanes = slice(128 * t, 128 * (t + 1))
        image = folded(acc_ref, t, low) + y_ref[:, lanes]
        if second:
            tile = 2.0 * (image - center_value * prev_ref[:, lanes].astype(f32)) / half_width - v_ref[:, lanes].astype(f32)
        else:
            tile = (image - center_value * v_ref[:, lanes].astype(f32)) / half_width
        tile = tile.astype(bf16)
        out_ref[:, lanes] = tile
        dup_ref[2 * t], dup_ref[2 * t + 1] = duplicate(tile.astype(f32), low)
    emit_picks(msg_ref, dup_ref, send_ref, low)
    for i in range(RB):
        prod = dot(dup_ref[i][:, 0:B].astype(bf16), wd_ref[i], NN)
        prod_ref[2 * i] = prod[:, 0:128]
        prod_ref[2 * i + 1] = prod[:, 128:256]
    emit_mirror(msg_ref, prod_ref, inv_ref, low)


def image_kernel(src_ref, send_ref, recv_ref, y_ref, f_ref, all_ref, wd_ref, out_ref, lhs_ref, acc_ref, stack_ref):
    low = low_half()
    remote_sum(src_ref, send_ref, recv_ref, wd_ref, lhs_ref, acc_ref)
    stack_ref[0:MC, :] = f_ref[...]
    for t in range(RB // 2):
        lanes = slice(128 * t, 128 * (t + 1))
        stack_ref[MC : 2 * MC, lanes] = (folded(acc_ref, t, low) + y_ref[:, lanes]).astype(bf16)
    part = dot(stack_ref[...], all_ref[...], NT).astype(bf16)
    for z in range(NZ):
        out_ref[z] = part


def sum_z_kernel(in_ref, out_ref):
    total = in_ref[0].astype(f32)
    for z in range(1, NZ):
        total = total + in_ref[z].astype(f32)
    total = total.astype(bf16)
    for x in range(NX):
        out_ref[x] = total


def sum_x_kernel(in_ref, gram_ref, proj_ref):
    total = in_ref[0].astype(f32)
    for x in range(1, NX):
        total = total + in_ref[x].astype(f32)
    gram_ref[...] = total[0:MC, :].T
    proj_ref[...] = total[MC : 2 * MC, :].T


SMEM = pl.BlockSpec(memory_space=pltpu.SMEM)
VM = pl.BlockSpec(memory_space=pltpu.VMEM)
params = pltpu.CompilerParams(vmem_limit_bytes=VMEM_LIMIT)
shape = jax.ShapeDtypeStruct


def on_device(vectors, hblocks, counts, sources, send_rows):
    cols, width = vectors.shape
    row_axes, rows = ("z", "x"), hblocks.shape[0]
    msg_shape = shape((PEERS, 2 * MC, 128), bf16)
    wd_shape = shape((rows, B, 256), bf16)
    dup = pltpu.VMEM((rows, MC, 128), f32)
    dupb = pltpu.VMEM((rows, MC, 128), bf16)
    acc = pltpu.VMEM((rows, MC, 128), f32)
    prod = pltpu.VMEM((2 * rows, MC, 128), f32)
    inv = pltpu.SMEM((2 * PEERS,), jnp.int32)
    lhs = pltpu.VMEM((rows, MC, LW), bf16)
    lhs_remote = pltpu.VMEM((rows, MC, 256), bf16)
    mir = pltpu.VMEM((rows, MC, LW), f32)

    def whole(shape_):
        return pl.BlockSpec(shape_, lambda g: (0,) * len(shape_))

    grid_rows = pl.BlockSpec((STEP, K, B * B), lambda g: (g, 0, 0))
    message, wd = pl.pallas_call(
        first_message_kernel,
        grid=(rows // STEP,),
        out_shape=(msg_shape, wd_shape),
        in_specs=[SMEM, SMEM, whole((cols, width)), grid_rows],
        out_specs=(whole(msg_shape.shape), pl.BlockSpec((STEP, B, 256), lambda g: (g, 0, 0))),
        scratch_shapes=[
            pltpu.VMEM((STEP, 256, 128), f32),
            pltpu.VMEM((2 * STEP, B, 128), f32),
            dup,
            prod,
            inv,
        ],
        compiler_params=params,
        name="first_message",
    )(sources, send_rows, vectors, hblocks)

    def exchange(message):
        return lax.all_to_all(message, row_axes, split_axis=0, concat_axis=0, tiled=True)

    received = exchange(message)
    local_scratch = [dup, dupb, lhs, mir, acc]
    um, local = pl.pallas_call(
        first_local_kernel,
        grid=(rows // STEP,),
        out_shape=(shape((rows, B, LW), bf16), shape((cols, width), f32)),
        in_specs=[SMEM, SMEM, whole((cols, width)), grid_rows],
        out_specs=(whole((rows, B, LW)), whole((cols, width))),
        scratch_shapes=[
            pltpu.VMEM((STEP, 512, 128), f32),
            pltpu.VMEM((STEP * len(LOCAL), B, 128), f32),
        ]
        + local_scratch,
        compiler_params=params,
        name="first_local",
    )(sources, counts, vectors, hblocks)

    def local_part(block):
        return pl.pallas_call(
            local_product,
            out_shape=shape((cols, width), f32),
            in_specs=[SMEM, VM, VM],
            out_specs=VM,
            scratch_shapes=local_scratch,
            compiler_params=params,
            name="local_product",
        )(sources, block, um)

    def next_step(second, received, local, previous):
        return pl.pallas_call(
            lambda *refs: step_kernel(second, *refs),
            out_shape=(shape((cols, width), bf16), msg_shape),
            in_specs=[SMEM, SMEM] + [VM] * 5,
            out_specs=(VM, VM),
            scratch_shapes=[lhs_remote, acc, dup, prod, inv],
            compiler_params=params,
            name="second_step" if second else "first_step",
        )(sources, send_rows, received, local, vectors, previous, wd)

    first, message = next_step(False, received, local, vectors)
    received = exchange(message)
    local = local_part(first)
    filtered, message = next_step(True, received, local, first)
    received = exchange(message)
    local = local_part(filtered)
    both = lax.all_gather(filtered, "c", axis=0, tiled=True)
    everyone = lax.all_gather(both, "y", axis=0, tiled=True)
    part = pl.pallas_call(
        image_kernel,
        out_shape=shape((NZ, 2 * MC, NY * NC * MC), bf16),
        in_specs=[SMEM, SMEM] + [VM] * 5,
        out_specs=VM,
        scratch_shapes=[lhs_remote, acc, pltpu.VMEM((2 * MC, width), bf16)],
        compiler_params=params,
        name="image",
    )(sources, send_rows, received, local, filtered, everyone, wd)
    part = lax.all_to_all(part, "z", split_axis=0, concat_axis=0, tiled=True)
    part = pl.pallas_call(
        sum_z_kernel,
        out_shape=shape((NX,) + part.shape[1:], bf16),
        compiler_params=params,
        name="sum_z",
    )(part)
    part = lax.all_to_all(part, "x", split_axis=0, concat_axis=0, tiled=True)
    gram, projected = pl.pallas_call(
        sum_x_kernel,
        out_shape=(shape((NY * NC * MC, MC), f32),) * 2,
        compiler_params=params,
        name="sum_x",
    )(part)
    return filtered, gram, projected


def solution(mesh):
    axes = Mesh(mesh.devices.reshape(NZ, NX, NY, NC), ("z", "x", "y", "c"))
    row, col = ("z", "x"), ("y", "c")
    return jax.shard_map(
        on_device,
        mesh=axes,
        in_specs=(P(col, row), P(row, None, None), P(row), P(row, None), P(row)),
        out_specs=(P(col, row), P(None, col), P(None, col)),
        check_vma=False,
    )
```

time: 549 us -> 150 us (0.27); the launches traced: 542 us -> 149 us
  blocking collectives: 194 us -> 30.6 us
  other arithmetic: 127 us -> 0 us
  waiting for transfers between devices: 97.8 us -> 29.4 us
  matrix products: 37.5 us -> 0 us
  Pallas kernels: 0 us -> 28.3 us
  local copies, waits for them, and re-layouts: 50.4 us -> 23.5 us
    psum x1 -> x0, blocking collectives: 138 us -> none  [on_device(): lax.psum(partial_value.astype(jnp.bfloat16), 'row').astype(jnp.float32)]
    scatter-add x6 -> x0, other arithmetic: 116 us -> none  [the longest x3 103 us: apply_operator(): jax.ops.segment_sum(mirror.reshape(rows_here * K, cols_here, B), flat_sou...]
    all_gather x4 -> x1, waiting for transfers between devices: 76 us -> 0.69 us  [on_device(): everyone = lax.all_gather(both, 'y', axis=0, tiled=True)]
    dot_general x7 -> x0, matrix products: 37.5 us -> none  [the longest x3 19.2 us: apply_operator(): jnp.einsum('ima,ikab->ikmb', block_vectors, masked, preferred_element_typ...]
    pallas_call x0 -> x9, Pallas kernels: none -> 28.3 us  [the longest x2 8.91 us: local_part(): pl.pallas_call(local_product, out_shape=shape((cols, width), f32), in_spe...]
    unnamed x1 -> x0, blocking collectives: 25.6 us -> none
    gather x7 -> x0, local copies, waits for them, and re-layouts: 23.2 us -> none  [the longest x3 12.9 us: apply_operator(): incoming = whole_blocks[global_rows]]
    unnamed x26 -> x44, local copies, waits for them, and re-layouts: 11.9 us -> 23.5 us
  transfers between devices with their start and end apart: 6 -> 4, of which waited for: 5 -> 4; matrix products, arithmetic and copies ran while one was open for 32% -> 0% of each run, Pallas kernels for 0% -> 11%
where the time goes in v1:
time: 150 us; the launch traced here: 149 us
  blocking collectives  30.6 us (20%)
  waiting for transfers between devices  29.4 us (20%)
  Pallas kernels  28.3 us (19%)
  local copies, waits for them, and re-layouts  23.5 us (16%)
  starting transfers between devices  22.8 us (15%)
  between operations  14.2 us (9%)
    all_to_all x3, waiting for transfers between devices, exchange(): lax.all_to_all(message, row_axes, split_axis=0, concat_axis=0, tiled=True)  28.7 us
    unnamed x44, local copies, waits for them, and re-layouts  23.5 us
    all_to_all x3, starting transfers between devices, exchange(): lax.all_to_all(message, row_axes, split_axis=0, concat_axis=0, tiled=True)  22.8 us
    all_to_all x1, blocking collectives, on_device(): part = lax.all_to_all(part, 'z', split_axis=0, concat_axis=0, tiled=True)  17.8 us
    all_to_all x1, blocking collectives, on_device(): part = lax.all_to_all(part, 'x', split_axis=0, concat_axis=0, tiled=True)  9.11 us
    pallas_call x2, Pallas kernels, local_part(): pl.pallas_call(local_product, out_shape=shape((cols, width), f32), in_spe...  8.91 us
    pallas_call x1, Pallas kernels, on_device(): pl.pallas_call(first_local_kernel, grid=(rows // STEP,), out_shape=(shape...  7.72 us
    pallas_call x2, Pallas kernels, next_step(): pl.pallas_call(lambda *refs: step_kernel(second, *refs), out_shape=(shape...  5.76 us
  transfers between devices with their start and end apart: 4, of which 4 were waited for; matrix products, arithmetic and copies ran while one was open for 0% of the time, Pallas kernels for 11%

profile of v1, /device:TPU:2, one launch (start us, length us, event | category | flops | bytes accessed | tf_op | source)
XLA Modules:
  0.0 148.8 jit_solution(8745644324625701531)
XLA Ops:
  7.2 0.8 copy.14.src_ref.refs_0_
  7.9 0.0 copy-start.6
  7.9 0.0 copy-start.15
  7.9 3.7 %copy.9.hb_ref = bf16[32,12,4096]{2,1,0:T(8,128)(2,1)S(1)} copy(bf16[32,12,4096]{2,0,1:T(8,128)(2,1)} %param.6) | data formatting | bytes 6291456 | tf_op args[1]
  11.7 0.0 copy-done.6
  11.7 0.0 copy-done.15
  11.7 3.3 %first_message.1 = (bf16[32,64,128]{2,1,0:T(8,128)(2,1)}, bf16[32,64,256]{2,1,0:T(8,128)(2,1)S(1)}) custom-call(s32[32,12]{1,0:T(8,128)S(1)} %copy.14.src_ref.refs_0_, s32[64]{0:T(128)S(1)} %copy-done.15, bf16[32,2048]{1,0:T(8,128)(2,1)S(1)} %copy-done.6, bf16[32,12,4096]{2,1,0:T(8,128)(2,1)S(1)} %copy.9.hb_ref), custom_call_target="tpu_custom_call" | custom-call | tf_op jit(solution)/shard_map/first_message/pallas_call | solution.py:263
  15.0 0.0 copy-start
  15.0 2.0 %copy-done = bf16[32,12,4096]{2,1,0:T(8,128)(2,1)} copy-done((bf16[32,12,4096]{2,1,0:T(8,128)(2,1)}, bf16[32,12,4096]{2,1,0:T(8,128)(2,1)S(1)}, u32[]{:S(2)}) %copy-start) | copy-done | bytes 3145752
  17.0 0.0 copy-start.2
  17.0 1.0 copy-done.2
  18.0 11.6 %all-to-all-start = ((bf16[32,64,128]{2,1,0:T(8,128)(2,1)}), bf16[32,64,128]{2,1,0:T(8,128)(2,1)S(1)}, u32[]{:S(2)}, u32[]{:S(2)}) async-start(bf16[32,64,128]{2,1,0:T(8,128)(2,1)} %get-tuple-element.13), calls=%async_computation | async-start | bytes 1048576 | tf_op jit(solution)/shard_map/all_to_all | solution.py:281
  29.6 0.0 copy-start.1
  29.7 2.2 %copy-done.1 = bf16[32,12,4096]{2,1,0:T(8,128)(2,1)S(1)} copy-done((bf16[32,12,4096]{2,1,0:T(8,128)(2,1)S(1)}, bf16[32,12,4096]{2,1,0:T(8,128)(2,1)}, u32[]{:S(2)}) %copy-start.1) | copy-done | bytes 3145752
  31.8 0.0 copy-start.19
  31.8 0.7 copy-done.19
  32.5 7.7 %first_local.1 = (bf16[32,64,640]{2,1,0:T(8,128)(2,1)S(1)}, f32[32,2048]{1,0:T(8,128)S(1)}) custom-call(s32[32,12]{1,0:T(8,128)S(1)} %copy.14.src_ref.refs_0_, s32[32]{0:T(128)S(1)} %copy-done.19, bf16[32,2048]{1,0:T(8,128)(2,1)S(1)} %copy-done.6, bf16[32,12,4096]{2,1,0:T(8,128)(2,1)S(1)} %copy-done.1), custom_call_target="tpu_custom_call" | custom-call | tf_op jit(solution)/shard_map/first_local/pallas_call | solution.py:285
  40.2 6.3 %all-to-all-done.refs_2_ = bf16[32,64,128]{2,1,0:T(8,128)(2,1)S(1)} async-done(((bf16[32,64,128]{2,1,0:T(8,128)(2,1)}), bf16[32,64,128]{2,1,0:T(8,128)(2,1)S(1)}, u32[]{:S(2)}, u32[]{:S(2)}) %all-to-all-start) | async-done | bytes 524320 | tf_op jit(solution)/shard_map/all_to_all | solution.py:281
  46.5 0.0 copy-start.3
  46.5 1.2 copy-done.3
  47.7 0.0 copy-start.16
  47.7 0.7 copy-done.16
  48.4 2.6 %first_step.1 = (bf16[32,2048]{1,0:T(8,128)(2,1)S(1)}, bf16[32,64,128]{2,1,0:T(8,128)(2,1)S(1)}) custom-call(s32[32,12]{1,0:T(8,128)S(1)} %copy.14.src_ref.refs_0_, s32[64]{0:T(128)S(1)} %copy-done.16, bf16[32,64,128]{2,1,0:T(8,128)(2,1)S(1)} %all-to-all-done.refs_2_, f32[32,2048]{1,0:T(8,128)S(1)} %get-tuple-element.14.refs_3_, ...), custom_call_target="tpu_custom_call" | custom-call | tf_op jit(solution)/shard_map/first_step/pallas_call | solution.py:312
  51.0 0.0 copy-start.10
  51.0 0.6 copy-done.10
  51.7 0.0 copy-start.14
  51.7 0.8 copy-done.14
  52.5 5.6 %all-to-all-start.1 = ((bf16[32,64,128]{2,1,0:T(8,128)(2,1)}), bf16[32,64,128]{2,1,0:T(8,128)(2,1)S(1)}, u32[]{:S(2)}, u32[]{:S(2)}) async-start(bf16[32,64,128]{2,1,0:T(8,128)(2,1)} %copy-done.14), calls=%async_computation.1 | async-start | bytes 1048576 | tf_op jit(solution)/shard_map/all_to_all | solution.py:281
  58.0 0.0 all-gather.2.cloned.1.call-start
  58.1 0.0 copy-start.11
  58.1 0.9 copy-done.11
  59.0 4.5 %local_product.2.refs_3_ = f32[32,2048]{1,0:T(8,128)S(1)} custom-call(s32[32,12]{1,0:T(8,128)S(1)} %copy.14.src_ref.refs_0_, bf16[32,2048]{1,0:T(8,128)(2,1)S(1)} %copy-done.11, bf16[32,64,640]{2,1,0:T(8,128)(2,1)S(1)} %get-tuple-element.18.um_ref), custom_call_target="tpu_custom_call" | custom-call | tf_op jit(solution)/shard_map/local_product/pallas_call | solution.py:301
  63.4 10.5 %all-to-all-done.1.refs_2_ = bf16[32,64,128]{2,1,0:T(8,128)(2,1)S(1)} async-done(((bf16[32,64,128]{2,1,0:T(8,128)(2,1)}), bf16[32,64,128]{2,1,0:T(8,128)(2,1)S(1)}, u32[]{:S(2)}, u32[]{:S(2)}) %all-to-all-start.1) | async-done | bytes 524320 | tf_op jit(solution)/shard_map/all_to_all | solution.py:281
  73.9 0.0 copy-start.4
  73.9 1.2 copy-done.4
  75.2 0.0 copy-start.12
  75.2 0.9 copy-done.12
  76.1 0.0 copy-start.17
  76.1 0.7 copy-done.17
  76.7 3.1 %second_step.1 = (bf16[32,2048]{1,0:T(8,128)(2,1)}, bf16[32,64,128]{2,1,0:T(8,128)(2,1)S(1)}) custom-call(s32[32,12]{1,0:T(8,128)S(1)} %copy.14.src_ref.refs_0_, s32[64]{0:T(128)S(1)} %copy-done.17, bf16[32,64,128]{2,1,0:T(8,128)(2,1)S(1)} %all-to-all-done.1.refs_2_, f32[32,2048]{1,0:T(8,128)S(1)} %local_product.2.refs_3_, bf16[32,2048]{1,0:T(8,128)(2,1)S(1)} %copy-done.6, ...), custom_call_target="tpu_custom_call" | custom-call | tf_op jit(solution)/shard_map/second_step/pallas_call | solution.py:312
  79.8 0.0 copy-start.13
  79.8 0.8 copy-done.13
  80.6 0.0 copy-start.8
  80.6 3.7 %all_gather.6 = bf16[64,2048]{1,0:T(8,128)(2,1)} all-gather(bf16[32,2048]{1,0:T(8,128)(2,1)} %get-tuple-element.23.v_ref.f_ref), channel_id=1, replica_groups=mesh['z'=8,'x'=4,'y'=4,'c'=2] {'c'}, dimensions={0}, use_global_device_ids=true | all-gather | bytes 393216 | tf_op jit(solution)/shard_map/all_gather | solution.py:328
  84.3 0.0 all-gather.2.cloned.1.call-update
  84.3 5.6 %all-to-all-start.2 = ((bf16[32,64,128]{2,1,0:T(8,128)(2,1)}), bf16[32,64,128]{2,1,0:T(8,128)(2,1)S(1)}, u32[]{:S(2)}, u32[]{:S(2)}) async-start(bf16[32,64,128]{2,1,0:T(8,128)(2,1)} %copy-done.13), calls=%async_computation.2 | async-start | bytes 1048576 | tf_op jit(solution)/shard_map/all_to_all | solution.py:281
  90.0 0.0 copy-start.7
  90.0 0.9 copy-done.7
  90.9 4.5 %local_product.3.y_ref = f32[32,2048]{1,0:T(8,128)S(1)} custom-call(s32[32,12]{1,0:T(8,128)S(1)} %copy.14.src_ref.refs_0_, bf16[32,2048]{1,0:T(8,128)(2,1)S(1)} %copy-done.7, bf16[32,64,640]{2,1,0:T(8,128)(2,1)S(1)} %get-tuple-element.18.um_ref), custom_call_target="tpu_custom_call" | custom-call | tf_op jit(solution)/shard_map/local_product/pallas_call | solution.py:301
  95.3 12.0 %all-to-all-done.2.recv_ref = bf16[32,64,128]{2,1,0:T(8,128)(2,1)S(1)} async-done(((bf16[32,64,128]{2,1,0:T(8,128)(2,1)}), bf16[32,64,128]{2,1,0:T(8,128)(2,1)S(1)}, u32[]{:S(2)}, u32[]{:S(2)}) %all-to-all-start.2) | async-done | bytes 524320 | tf_op jit(solution)/shard_map/all_to_all | solution.py:281
  107.3 0.7 all-gather.2.cloned.1.call-done.all_ref
  108.0 0.0 copy-done.8
  108.0 0.0 copy-start.5
  108.0 1.2 copy-done.5
  109.2 0.0 copy-start.9
  109.2 1.2 copy-done.9
  110.4 0.0 copy-start.18
  110.4 0.7 copy-done.18
  111.1 2.4 %image.1 = bf16[8,64,256]{2,1,0:T(8,128)(2,1)S(1)} custom-call(s32[32,12]{1,0:T(8,128)S(1)} %copy.14.src_ref.refs_0_, s32[64]{0:T(128)S(1)} %copy-done.18, bf16[32,64,128]{2,1,0:T(8,128)(2,1)S(1)} %all-to-all-done.2.recv_ref, f32[32,2048]{1,0:T(8,128)S(1)} %local_product.3.y_ref, bf16[32,2048]{1,0:T(8,128)(2,1)S(1)} %copy-done.8, ...), custom_call_target="tpu_custom_call" | custom-call | tf_op jit(solution)/shard_map/image/pallas_call | solution.py:330
  113.5 17.8 %all_to_all.25.in_ref = bf16[8,64,256]{2,1,0:T(8,128)(2,1)S(1)} all-to-all(bf16[8,64,256]{2,1,0:T(8,128)(2,1)S(1)} %image.1), channel_id=1, replica_groups=mesh['z'=8,'x'=4,'y'=4,'c'=2] {'z'}, dimensions={0} | all-to-all | bytes 524288 | tf_op jit(solution)/shard_map/all_to_all | solution.py:339
  131.4 9.1 %all_to_all.26.in_ref = bf16[4,64,256]{2,1,0:T(8,128)(2,1)S(1)} all-to-all(bf16[4,64,256]{2,1,0:T(8,128)(2,1)S(1)} %sum_z.1), channel_id=1, replica_groups=mesh['z'=8,'x'=4,'y'=4,'c'=2] {'x'}, dimensions={0} | all-to-all | bytes 262144 | tf_op jit(solution)/shard_map/all_to_all | solution.py:346
  140.5 0.1 sum_x.1
  140.6 0.7 copy.17
  141.3 0.7 copy.18
  (1 shorter events, 0.0 us)
Async XLA Ops:
  7.9 3.7 %copy-start.6 = (bf16[32,2048]{1,0:T(8,128)(2,1)S(1)}, bf16[32,2048]{1,0:T(8,128)(2,1)}, u32[]{:S(2)}) copy-start(bf16[32,2048]{1,0:T(8,128)(2,1)} %refs_4_.3) | copy-start | bytes 393220
  7.9 3.7 %copy-start.15 = (s32[64]{0:T(128)S(1)}, s32[64]{0:T(128)}, u32[]{:S(2)}) copy-start(s32[64]{0:T(128)} %send_ref.3) | copy-start | bytes 772
  15.0 2.0 %copy-start = (bf16[32,12,4096]{2,1,0:T(8,128)(2,1)}, bf16[32,12,4096]{2,1,0:T(8,128)(2,1)S(1)}, u32[]{:S(2)}) copy-start(bf16[32,12,4096]{2,1,0:T(8,128)(2,1)S(1)} %copy.9.hb_ref) | copy-start | bytes 9437188
  17.0 1.0 copy-start.2
  18.0 28.4 %all-to-all-start = ((bf16[32,64,128]{2,1,0:T(8,128)(2,1)}), bf16[32,64,128]{2,1,0:T(8,128)(2,1)S(1)}, u32[]{:S(2)}, u32[]{:S(2)}) async-start(bf16[32,64,128]{2,1,0:T(8,128)(2,1)} %get-tuple-element.13), calls=%async_computation | async-start | bytes 1048576 | tf_op jit(solution)/shard_map/all_to_all | solution.py:281
  29.6 2.2 %copy-start.1 = (bf16[32,12,4096]{2,1,0:T(8,128)(2,1)S(1)}, bf16[32,12,4096]{2,1,0:T(8,128)(2,1)}, u32[]{:S(2)}) copy-start(bf16[32,12,4096]{2,1,0:T(8,128)(2,1)} %copy-done) | copy-start | bytes 9437188
  31.8 0.7 copy-start.19
  46.5 1.2 copy-start.3
  47.7 0.7 copy-start.16
  51.0 0.7 copy-start.10
  51.7 0.8 copy-start.14
  52.5 21.5 %all-to-all-start.1 = ((bf16[32,64,128]{2,1,0:T(8,128)(2,1)}), bf16[32,64,128]{2,1,0:T(8,128)(2,1)S(1)}, u32[]{:S(2)}, u32[]{:S(2)}) async-start(bf16[32,64,128]{2,1,0:T(8,128)(2,1)} %copy-done.14), calls=%async_computation.1 | async-start | bytes 1048576 | tf_op jit(solution)/shard_map/all_to_all | solution.py:281
  58.0 50.0 %all-gather.2.cloned.1.call-start = ((), (), s32[]{:S(2)}) async-start(), calls=%async_computation.5 | async-start | bytes 1310720 | tf_op jit(solution)/shard_map/all_gather | solution.py:329
  58.1 0.9 copy-start.11
  73.9 1.2 copy-start.4
  75.2 0.9 copy-start.12
  76.1 0.7 copy-start.17
  79.8 0.8 copy-start.13
  80.6 27.3 %copy-start.8 = (bf16[32,2048]{1,0:T(8,128)(2,1)S(1)}, bf16[32,2048]{1,0:T(8,128)(2,1)}, u32[]{:S(2)}) copy-start(bf16[32,2048]{1,0:T(8,128)(2,1)} %get-tuple-element.23.v_ref.f_ref) | copy-start | bytes 393220
  84.3 22.9 %all-to-all-start.2 = ((bf16[32,64,128]{2,1,0:T(8,128)(2,1)}), bf16[32,64,128]{2,1,0:T(8,128)(2,1)S(1)}, u32[]{:S(2)}, u32[]{:S(2)}) async-start(bf16[32,64,128]{2,1,0:T(8,128)(2,1)} %copy-done.13), calls=%async_computation.2 | async-start | bytes 1048576 | tf_op jit(solution)/shard_map/all_to_all | solution.py:281
  90.0 0.9 copy-start.7
  108.0 1.2 copy-start.5
  109.2 1.2 copy-start.9
  110.4 0.7 copy-start.18
Sparse Core Ops, SparseCore 0:
  84.5 23.4 all-gather.1

commit v2 on v1

v2 whole, which is shorter than its diff:
```python
import jax
import jax.numpy as jnp
from jax import lax
from jax.experimental import pallas as pl
from jax.experimental.pallas import tpu as pltpu
from jax.sharding import Mesh, PartitionSpec as P

B = 64
K = 12
RB = 32
MC = 32
PEERS = 32
NZ, NX, NY, NC = 8, 4, 4, 2
SEND, COUNT = 12, 13
LOCAL = ((0, 3), (4, 5), (6, 7), (8, 9), (10, 11))
LW = 128 * len(LOCAL)
center_value = 0.25
half_width = 1.5
bf16 = jnp.bfloat16
f32 = jnp.float32
MIB = 1024 * 1024

NN = (((1,), (0,)), ((), ()))
NT = (((1,), (1,)), ((), ()))


def low_half(rows=MC):
    return lax.broadcasted_iota(jnp.int32, (rows, 128), 1) < B


def dot(a, b, dims):
    return lax.dot_general(a, b, dims, preferred_element_type=f32)


def store_pair(even_odd_ref, first, second, low):
    even_odd_ref[pl.ds(0, 32, stride=2), :] = jnp.where(low, first, pltpu.roll(second, B, 1))
    even_odd_ref[pl.ds(1, 32, stride=2), :] = jnp.where(low, pltpu.roll(first, B, 1), second)


def duplicate(tile, low):
    turned = pltpu.roll(tile, B, 1)
    return jnp.where(low, tile, turned), jnp.where(low, turned, tile)


def emit_picks(msg_ref, dup_ref, idx_ref, low):
    for q in range(PEERS):
        msg_ref[q, 0:MC, :] = jnp.where(
            low, dup_ref[idx_ref[SEND, 2 * q]], dup_ref[idx_ref[SEND, 2 * q + 1]]
        ).astype(bf16)


def emit_mirror(msg_ref, prod_ref, inv_ref, low):
    for q in range(PEERS):
        msg_ref[q, MC : 2 * MC, :] = jnp.where(
            low, prod_ref[inv_ref[2 * q]], prod_ref[inv_ref[2 * q + 1]]
        ).astype(bf16)


def invert_slots(inv_ref, idx_ref):
    for i in range(RB):
        for k in (1, 2):
            inv_ref[idx_ref[k, i] - RB] = 2 * i + k - 1


def unpack_rows(rows_ref, hb_ref):
    for j in range(32):
        rows_ref[32 * j : 32 * (j + 1), :] = hb_ref[0, :, 128 * j : 128 * (j + 1)].astype(f32)


def first_message_kernel(src_ref, send_ref, srcv_ref, sendv_ref, countv_ref, v_ref, hb_ref, idx_ref, msg_ref, wd_ref, rows_ref, pair_ref, dup_ref, prod_ref, inv_ref):
    step = pl.program_id(0)
    low = low_half()

    @pl.when(step == 0)
    def _():
        idx_ref[...] = jnp.zeros(idx_ref.shape, jnp.int32)
        idx_ref[0:K, 0:RB] = srcv_ref[...]
        idx_ref[SEND : SEND + 1, 0 : 2 * PEERS] = sendv_ref[...]
        idx_ref[COUNT : COUNT + 1, 0:RB] = countv_ref[...]
        for t in range(RB // 2):
            tile = v_ref[:, 128 * t : 128 * (t + 1)].astype(f32)
            dup_ref[2 * t], dup_ref[2 * t + 1] = duplicate(tile, low)
        for i in range(RB):
            for k in (1, 2):
                inv_ref[src_ref[k, i] - RB] = 2 * i + k - 1
        for q in range(PEERS):
            msg_ref[q, 0:MC, :] = jnp.where(
                low, dup_ref[send_ref[2 * q]], dup_ref[send_ref[2 * q + 1]]
            ).astype(bf16)

    unpack_rows(rows_ref, hb_ref)
    for i in range(RB):
        block = rows_ref[pl.ds(i, 32, stride=32), :]
        store_pair(pair_ref.at[i], block, block, low)

    @pl.when(step == 0)
    def _():
        for i in range(RB):
            wd_ref[i, :, 0:128] = pair_ref[i].astype(bf16)

    @pl.when(step == 1)
    def _():
        for i in range(RB):
            wd_ref[i, :, 128:256] = pair_ref[i].astype(bf16)
        mirror_products(dup_ref, wd_ref, prod_ref)
        emit_mirror(msg_ref, prod_ref, inv_ref, low)


def mirror_products(dup_ref, wd_ref, prod_ref):
    for i in range(RB):
        prod = dot(dup_ref[i][:, 0:B].astype(bf16), wd_ref[i], NN)
        prod_ref[2 * i] = prod[:, 0:128]
        prod_ref[2 * i + 1] = prod[:, 128:256]


def local_product(idx_ref, v_ref, um_ref, y_ref, dup_ref, dupb_ref, lhs_ref, mir_ref, acc_ref):
    low = low_half()
    for t in range(RB // 2):
        tile = v_ref[:, 128 * t : 128 * (t + 1)].astype(f32)
        one, two = duplicate(tile, low)
        dup_ref[2 * t], dup_ref[2 * t + 1] = one, two
        dupb_ref[2 * t], dupb_ref[2 * t + 1] = one.astype(bf16), two.astype(bf16)

    def gather(i, _):
        for t, (k0, k1) in enumerate(LOCAL):
            j0 = i if k0 == 0 else jnp.minimum(idx_ref[k0, i], RB - 1)
            j1 = jnp.minimum(idx_ref[k1, i], RB - 1)
            lhs_ref[i, :, 128 * t : 128 * (t + 1)] = jnp.where(low, dup_ref[j0], dup_ref[j1]).astype(bf16)
        return 0

    lax.fori_loop(0, RB, gather, 0, unroll=4)
    for i in range(RB):
        mir_ref[i] = dot(dupb_ref[i][:, 0:B], um_ref[i], NN)
    for i in range(RB):
        acc_ref[i, :, 0:B] = dot(lhs_ref[i], um_ref[i], NT)
        acc_ref[i, :, B:128] = jnp.zeros((MC, B), f32)

    def scatter(i, _):
        for t, (k0, k1) in enumerate(LOCAL):
            j0 = i if k0 == 0 else jnp.minimum(idx_ref[k0, i], RB - 1)
            j1 = jnp.minimum(idx_ref[k1, i], RB - 1)
            part = mir_ref[i, :, 128 * t : 128 * (t + 1)]
            acc_ref[j0] += jnp.where(low, part, 0.0)
            acc_ref[j1] += jnp.where(low, 0.0, part)
        return 0

    lax.fori_loop(0, RB, scatter, 0, unroll=4)
    for t in range(RB // 2):
        one, two = acc_ref[2 * t], acc_ref[2 * t + 1]
        y_ref[:, 128 * t : 128 * (t + 1)] = jnp.where(
            low, one + pltpu.roll(one, B, 1), two + pltpu.roll(two, B, 1)
        )


def first_local_kernel(idx_ref, v_ref, one_ref, two_ref, um_ref, y_ref, rows1_ref, rows2_ref, pair_ref, dup_ref, dupb_ref, lhs_ref, mir_ref, acc_ref):
    step = pl.program_id(0)
    low = low_half()
    unpack_rows(rows1_ref, one_ref)
    unpack_rows(rows2_ref, two_ref)
    k0, k1 = jnp.where(step == 0, 0, 2 * step + 2), 2 * step + 3
    lanes = pl.ds(pl.multiple_of(step * 128, 128), 128)
    for i in range(RB):
        count = idx_ref[COUNT, i]
        one = jnp.where(k0 < count, rows1_ref[pl.ds(i, 32, stride=32), :], 0.0)
        two = jnp.where(k1 < count, rows2_ref[pl.ds(i, 32, stride=32), :], 0.0)
        store_pair(pair_ref.at[i], one, two, low)
        um_ref[i, :, lanes] = pair_ref[i].astype(bf16)

    @pl.when(step == len(LOCAL) - 1)
    def _():
        local_product(idx_ref, v_ref, um_ref, y_ref, dup_ref, dupb_ref, lhs_ref, mir_ref, acc_ref)


def remote_sum(idx_ref, recv_ref, wd_ref, lhs_ref, acc_ref):
    low = low_half()
    lane = lax.broadcasted_iota(jnp.int32, (MC, 128), 1) // B

    def gather(i, _):
        for k in (1, 2):
            s = idx_ref[k, i] - RB
            tile = recv_ref[s // 2, 0:MC, :].astype(f32)
            lhs_ref[i, :, 128 * (k - 1) : 128 * k] = jnp.where(lane == s % 2, tile, 0.0).astype(bf16)
        return 0

    lax.fori_loop(0, RB, gather, 0, unroll=4)
    for i in range(RB):
        acc_ref[i, :, 0:B] = dot(lhs_ref[i], wd_ref[i], NT)
        acc_ref[i, :, B:128] = jnp.zeros((MC, B), f32)

    def scatter(q, _):
        tile = recv_ref[q, MC : 2 * MC, :].astype(f32)
        acc_ref[idx_ref[SEND, 2 * q]] += jnp.where(low, tile, 0.0)
        acc_ref[idx_ref[SEND, 2 * q + 1]] += jnp.where(low, 0.0, tile)
        return 0

    lax.fori_loop(0, PEERS, scatter, 0, unroll=4)


def folded(acc_ref, t, low):
    one, two = acc_ref[2 * t], acc_ref[2 * t + 1]
    return jnp.where(low, one + pltpu.roll(one, B, 1), two + pltpu.roll(two, B, 1))


def step_kernel(second, idx_ref, recv_ref, y_ref, v_ref, prev_ref, wd_ref, out_ref, msg_ref, lhs_ref, acc_ref, dup_ref, prod_ref, inv_ref):
    low = low_half()
    invert_slots(inv_ref, idx_ref)
    remote_sum(idx_ref, recv_ref, wd_ref, lhs_ref, acc_ref)
    for t in range(RB // 2):
        lanes = slice(128 * t, 128 * (t + 1))
        image = folded(acc_ref, t, low) + y_ref[:, lanes]
        if second:
            tile = 2.0 * (image - center_value * prev_ref[:, lanes].astype(f32)) / half_width - v_ref[:, lanes].astype(f32)
        else:
            tile = (image - center_value * v_ref[:, lanes].astype(f32)) / half_width
        tile = tile.astype(bf16)
        out_ref[:, lanes] = tile
        dup_ref[2 * t], dup_ref[2 * t + 1] = duplicate(tile.astype(f32), low)
    emit_picks(msg_ref, dup_ref, idx_ref, low)
    mirror_products(dup_ref, wd_ref, prod_ref)
    emit_mirror(msg_ref, prod_ref, inv_ref, low)


def image_kernel(idx_ref, recv_ref, y_ref, wd_ref, *refs):
    own, other = refs[0:NY], refs[NY : 2 * NY]
    out_ref, lhs_ref, acc_ref, stack_ref, all_ref = refs[2 * NY :]
    low = low_half()
    y, c = lax.axis_index("y"), lax.axis_index("c")
    for d in range(NY):
        from_y = lax.rem(y + NY - d, NY) * NC
        all_ref[pl.ds(pl.multiple_of((from_y + c) * MC, MC), MC), :] = own[d][...]
        all_ref[pl.ds(pl.multiple_of((from_y + 1 - c) * MC, MC), MC), :] = other[d][...]
    remote_sum(idx_ref, recv_ref, wd_ref, lhs_ref, acc_ref)
    stack_ref[0:MC, :] = own[0][...]
    for t in range(RB // 2):
        lanes = slice(128 * t, 128 * (t + 1))
        stack_ref[MC : 2 * MC, lanes] = (folded(acc_ref, t, low) + y_ref[:, lanes]).astype(bf16)
    part = dot(stack_ref[...], all_ref[...], NT).astype(bf16)
    for z in range(NZ):
        out_ref[z] = part


def sum_z_kernel(in_ref, out_ref):
    total = in_ref[0].astype(f32)
    for z in range(1, NZ):
        total = total + in_ref[z].astype(f32)
    total = total.astype(bf16)
    for x in range(NX):
        out_ref[x] = total


def sum_x_kernel(in_ref, gram_ref, proj_ref):
    total = in_ref[0].astype(f32)
    for x in range(1, NX):
        total = total + in_ref[x].astype(f32)
    gram_ref[...] = total[0:MC, :]
    proj_ref[...] = total[MC : 2 * MC, :]


SMEM = pl.BlockSpec(memory_space=pltpu.SMEM)
VM = pl.BlockSpec(memory_space=pltpu.VMEM)
shape = jax.ShapeDtypeStruct


def limit(mib):
    return pltpu.CompilerParams(vmem_limit_bytes=mib * MIB)


def on_device(vectors, hblocks, counts, sources, send_rows):
    cols, width = vectors.shape
    row_axes, rows = ("z", "x"), hblocks.shape[0]
    msg_shape = shape((PEERS, 2 * MC, 128), bf16)
    wd_shape = shape((rows, B, 256), bf16)
    dup = pltpu.VMEM((rows, MC, 128), f32)
    dupb = pltpu.VMEM((rows, MC, 128), bf16)
    acc = pltpu.VMEM((rows, MC, 128), f32)
    prod = pltpu.VMEM((2 * rows, MC, 128), f32)
    inv = pltpu.SMEM((2 * PEERS,), jnp.int32)
    lhs = pltpu.VMEM((rows, MC, LW), bf16)
    lhs_remote = pltpu.VMEM((rows, MC, 256), bf16)
    mir = pltpu.VMEM((rows, MC, LW), f32)
    unpacked = pltpu.VMEM((rows * 32, 128), f32)
    pairs = pltpu.VMEM((rows, B, 128), f32)

    def whole(shape_):
        return pl.BlockSpec(shape_, lambda g: (0,) * len(shape_))

    blocks = hblocks.transpose(1, 0, 2)
    sources = sources.T
    one_k = (1, rows, B * B)
    idx, message, wd = pl.pallas_call(
        first_message_kernel,
        grid=(2,),
        out_shape=(shape((16, 128), jnp.int32), msg_shape, wd_shape),
        in_specs=[
            SMEM,
            SMEM,
            whole((K, rows)),
            whole((1, 2 * PEERS)),
            whole((1, rows)),
            whole((cols, width)),
            pl.BlockSpec(one_k, lambda g: (g + 1, 0, 0)),
        ],
        out_specs=(whole((16, 128)), whole(msg_shape.shape), whole(wd_shape.shape)),
        scratch_shapes=[unpacked, pairs, dup, prod, inv],
        compiler_params=limit(60),
        name="first_message",
    )(sources, send_rows, sources, send_rows[None], counts[None], vectors, blocks)

    def exchange(message):
        return lax.all_to_all(message, row_axes, split_axis=0, concat_axis=0, tiled=True)

    received = exchange(message)
    local_scratch = [dup, dupb, lhs, mir, acc]
    um, local = pl.pallas_call(
        first_local_kernel,
        grid=(len(LOCAL),),
        out_shape=(shape((rows, B, LW), bf16), shape((cols, width), f32)),
        in_specs=[
            SMEM,
            whole((cols, width)),
            pl.BlockSpec(one_k, lambda g: (jnp.where(g == 0, 0, 2 * g + 2), 0, 0)),
            pl.BlockSpec(one_k, lambda g: (2 * g + 3, 0, 0)),
        ],
        out_specs=(whole((rows, B, LW)), whole((cols, width))),
        scratch_shapes=[unpacked, unpacked, pairs] + local_scratch,
        compiler_params=limit(60),
        name="first_local",
    )(idx, vectors, blocks, blocks)

    def local_part(block):
        return pl.pallas_call(
            local_product,
            out_shape=shape((cols, width), f32),
            in_specs=[SMEM, VM, VM],
            out_specs=VM,
            scratch_shapes=local_scratch,
            compiler_params=limit(60),
            name="local_product",
        )(idx, block, um)

    def next_step(second, received, local, previous):
        return pl.pallas_call(
            lambda *refs: step_kernel(second, *refs),
            out_shape=(shape((cols, width), bf16), msg_shape),
            in_specs=[SMEM] + [VM] * 5,
            out_specs=(VM, VM),
            scratch_shapes=[lhs_remote, acc, dup, prod, inv],
            compiler_params=limit(60),
            name="second_step" if second else "first_step",
        )(idx, received, local, vectors, previous, wd)

    first, message = next_step(False, received, local, vectors)
    received = exchange(message)
    local = local_part(first)
    filtered, message = next_step(True, received, local, first)
    received = exchange(message)
    local = local_part(filtered)
    own = [filtered] + [
        lax.ppermute(filtered, "y", [(y, (y + d) % NY) for y in range(NY)]) for d in range(1, NY)
    ]
    other = [lax.ppermute(block, "c", [(0, 1), (1, 0)]) for block in own]
    part = pl.pallas_call(
        image_kernel,
        out_shape=shape((NZ, 2 * MC, NY * NC * MC), bf16),
        in_specs=[SMEM] + [VM] * (3 + 2 * NY),
        out_specs=VM,
        scratch_shapes=[
            lhs_remote,
            acc,
            pltpu.VMEM((2 * MC, width), bf16),
            pltpu.VMEM((NY * NC * MC, width), bf16),
        ],
        compiler_params=limit(60),
        name="image",
    )(idx, received, local, wd, *own, *other)
    part = lax.all_to_all(part, "z", split_axis=0, concat_axis=0, tiled=True)
    part = pl.pallas_call(
        sum_z_kernel,
        out_shape=shape((NX,) + part.shape[1:], bf16),
        compiler_params=limit(4),
        name="sum_z",
    )(part)
    part = lax.all_to_all(part, "x", split_axis=0, concat_axis=0, tiled=True)
    gram, projected = pl.pallas_call(
        sum_x_kernel,
        out_shape=(shape((MC, NY * NC * MC), f32),) * 2,
        compiler_params=limit(4),
        name="sum_x",
    )(part)
    return filtered, gram.T, projected.T


def solution(mesh):
    axes = Mesh(mesh.devices.reshape(NZ, NX, NY, NC), ("z", "x", "y", "c"))
    row, col = ("z", "x"), ("y", "c")
    return jax.shard_map(
        on_device,
        mesh=axes,
        in_specs=(P(col, row), P(row, None, None), P(row), P(row, None), P(row)),
        out_specs=(P(col, row), P(None, col), P(None, col)),
        check_vma=False,
    )
```

time: 150 us -> 124 us (0.83)
  local copies, waits for them, and re-layouts: 23.5 us -> 3.14 us
  Pallas kernels: 28.3 us -> 42 us
  between operations: 14.2 us -> 0.75 us
  waiting for transfers between devices: 29.4 us -> 20.9 us
  starting transfers between devices: 22.8 us -> 27.4 us
  blocking collectives: 30.6 us -> 28.3 us
    unnamed x44 -> x20, local copies, waits for them, and re-layouts: 23.5 us -> 3.14 us
    all_to_all x3, waiting for transfers between devices: 28.7 us -> 14.4 us  [exchange(): lax.all_to_all(message, row_axes, split_axis=0, concat_axis=0, tiled=True)]
    ppermute x0 -> x7, waiting for transfers between devices: none -> 6.48 us  [the longest x3 6.47 us: on_device(): lax.ppermute(filtered, 'y', [(y, (y + d) % NY) for y in range(NY)])]
    pallas_call x3, Pallas kernels: 11.2 us -> 16.5 us  [the longest x1 12 us: on_device(): pl.pallas_call(first_local_kernel, grid=(len(LOCAL),), out_shape=(shape((...]
    ppermute x0 -> x7, starting transfers between devices: none -> 4.71 us  [the longest x3 4.69 us: on_device(): lax.ppermute(filtered, 'y', [(y, (y + d) % NY) for y in range(NY)])]
    pallas_call x2, Pallas kernels: 8.91 us -> 12.7 us  [local_part(): pl.pallas_call(local_product, out_shape=shape((cols, width), f32), in_spe...]
    all_gather x1 -> x0, blocking collectives: 3.67 us -> none  [on_device(): both = lax.all_gather(filtered, 'c', axis=0, tiled=True)]
    pallas_call x2, Pallas kernels: 5.76 us -> 8.49 us  [next_step(): pl.pallas_call(lambda *refs: step_kernel(second, *refs), out_shape=(shape...]
  transfers between devices with their start and end apart: 4 -> 10, of which waited for: 4 -> 5; matrix products, arithmetic and copies ran while one was open for 0% -> 0% of each run, Pallas kernels for 11% -> 20%
where the time goes in v2:
time: 124 us; the launch traced here: 122 us
  Pallas kernels  42 us (34%)
  blocking collectives  28.3 us (23%)
  starting transfers between devices  27.4 us (22%)
  waiting for transfers between devices  20.9 us (17%)
  local copies, waits for them, and re-layouts  3.14 us (3%)
    all_to_all x3, starting transfers between devices, exchange(): lax.all_to_all(message, row_axes, split_axis=0, concat_axis=0, tiled=True)  22.7 us
    all_to_all x1, blocking collectives, on_device(): part = lax.all_to_all(part, 'z', split_axis=0, concat_axis=0, tiled=True)  19.1 us
    all_to_all x3, waiting for transfers between devices, exchange(): lax.all_to_all(message, row_axes, split_axis=0, concat_axis=0, tiled=True)  14.4 us
    pallas_call x2, Pallas kernels, local_part(): pl.pallas_call(local_product, out_shape=shape((cols, width), f32), in_spe...  12.7 us
    pallas_call x1, Pallas kernels, on_device(): pl.pallas_call(first_local_kernel, grid=(len(LOCAL),), out_shape=(shape((...  12 us
    all_to_all x1, blocking collectives, on_device(): part = lax.all_to_all(part, 'x', split_axis=0, concat_axis=0, tiled=True)  9.12 us
    pallas_call x2, Pallas kernels, next_step(): pl.pallas_call(lambda *refs: step_kernel(second, *refs), out_shape=(shape...  8.49 us
    ppermute x3, waiting for transfers between devices, on_device(): lax.ppermute(filtered, 'y', [(y, (y + d) % NY) for y in range(NY)])  6.47 us
  transfers between devices with their start and end apart: 10, of which 5 were waited for; matrix products, arithmetic and copies ran while one was open for 0% of the time, Pallas kernels for 20%

profile of v2, /device:TPU:2, one launch (start us, length us, event | category | flops | bytes accessed | tf_op | source)
XLA Modules:
  0.0 122.5 jit_solution(9918891490016530609)
XLA Ops:
  0.6 3.8 %first_message.1 = (s32[16,128]{1,0:T(8,128)}, bf16[32,64,128]{2,1,0:T(8,128)(2,1)}, bf16[32,64,256]{2,1,0:T(8,128)(2,1)}) custom-call(s32[12,32]{1,0:T(8,128)} %bitcast.9, s32[64]{0:T(128)} %send_ref.1, s32[12,32]{1,0:T(8,128)} %bitcast.10, s32[1,64]{1,0:T(1,128)} %bitcast.11, s32[1,32]{1,0:T(1,128)} %bitcast.12, bf16[32,2048]{1,0:T(8,128)(2,1)} %refs_3_.3, ...), custom_call_target="tpu_custom_call" | custom-call | tf_op jit(solution)/shard_map/first_message/pallas_call | solution.py:290
  4.5 11.6 %all-to-all-start = ((bf16[32,64,128]{2,1,0:T(8,128)(2,1)}), bf16[32,64,128]{2,1,0:T(8,128)(2,1)S(1)}, u32[]{:S(2)}, u32[]{:S(2)}) async-start(bf16[32,64,128]{2,1,0:T(8,128)(2,1)} %get-tuple-element.15), calls=%async_computation | async-start | bytes 1048576 | tf_op jit(solution)/shard_map/all_to_all | solution.py:310
  16.1 12.0 %first_local.1 = (bf16[32,64,640]{2,1,0:T(8,128)(2,1)}, f32[32,2048]{1,0:T(8,128)}) custom-call(s32[16,128]{1,0:T(8,128)} %get-tuple-element.14.idx_ref.refs_0_, bf16[32,2048]{1,0:T(8,128)(2,1)} %refs_3_.3, bf16[12,32,4096]{2,1,0:T(8,128)(2,1)} %bitcast.7, bf16[12,32,4096]{2,1,0:T(8,128)(2,1)} %bitcast.8), custom_call_target="tpu_custom_call" | custom-call | tf_op jit(solution)/shard_map/first_local/pallas_call | solution.py:314
  28.1 4.8 %all-to-all-done.refs_1_ = bf16[32,64,128]{2,1,0:T(8,128)(2,1)S(1)} async-done(((bf16[32,64,128]{2,1,0:T(8,128)(2,1)}), bf16[32,64,128]{2,1,0:T(8,128)(2,1)S(1)}, u32[]{:S(2)}, u32[]{:S(2)}) %all-to-all-start) | async-done | bytes 524320 | tf_op jit(solution)/shard_map/all_to_all | solution.py:310
  32.9 0.0 copy-start.1
  32.9 0.8 copy-done.1
  33.7 4.3 %first_step.1 = (bf16[32,2048]{1,0:T(8,128)(2,1)}, bf16[32,64,128]{2,1,0:T(8,128)(2,1)}) custom-call(s32[16,128]{1,0:T(8,128)} %get-tuple-element.14.idx_ref.refs_0_, bf16[32,64,128]{2,1,0:T(8,128)(2,1)} %copy-done.1, f32[32,2048]{1,0:T(8,128)} %get-tuple-element.16.refs_2_, bf16[32,2048]{1,0:T(8,128)(2,1)} %refs_3_.3, bf16[32,2048]{1,0:T(8,128)(2,1)} %refs_3_.3, ...), custom_call_target="tpu_custom_call" | custom-call | tf_op jit(solution)/shard_map/first_step/pallas_call | solution.py:342
  38.0 5.6 %all-to-all-start.1 = ((bf16[32,64,128]{2,1,0:T(8,128)(2,1)}), bf16[32,64,128]{2,1,0:T(8,128)(2,1)S(1)}, u32[]{:S(2)}, u32[]{:S(2)}) async-start(bf16[32,64,128]{2,1,0:T(8,128)(2,1)} %get-tuple-element.18), calls=%async_computation.1 | async-start | bytes 1048576 | tf_op jit(solution)/shard_map/all_to_all | solution.py:310
  43.5 6.3 %local_product.2.refs_2_ = f32[32,2048]{1,0:T(8,128)} custom-call(s32[16,128]{1,0:T(8,128)} %get-tuple-element.14.idx_ref.refs_0_, bf16[32,2048]{1,0:T(8,128)(2,1)} %get-tuple-element.19.v_ref.refs_4_, bf16[32,64,640]{2,1,0:T(8,128)(2,1)} %get-tuple-element.20.um_ref), custom_call_target="tpu_custom_call" | custom-call | tf_op jit(solution)/shard_map/local_product/pallas_call | solution.py:331
  49.8 9.6 %all-to-all-done.1.refs_1_ = bf16[32,64,128]{2,1,0:T(8,128)(2,1)S(1)} async-done(((bf16[32,64,128]{2,1,0:T(8,128)(2,1)}), bf16[32,64,128]{2,1,0:T(8,128)(2,1)S(1)}, u32[]{:S(2)}, u32[]{:S(2)}) %all-to-all-start.1) | async-done | bytes 524320 | tf_op jit(solution)/shard_map/all_to_all | solution.py:310
  59.4 0.0 copy-start.2
  59.4 0.8 copy-done.2
  60.2 4.2 %second_step.1 = (bf16[32,2048]{1,0:T(8,128)(2,1)}, bf16[32,64,128]{2,1,0:T(8,128)(2,1)}) custom-call(s32[16,128]{1,0:T(8,128)} %get-tuple-element.14.idx_ref.refs_0_, bf16[32,64,128]{2,1,0:T(8,128)(2,1)} %copy-done.2, f32[32,2048]{1,0:T(8,128)} %local_product.2.refs_2_, bf16[32,2048]{1,0:T(8,128)(2,1)} %refs_3_.3, ...), custom_call_target="tpu_custom_call" | custom-call | tf_op jit(solution)/shard_map/second_step/pallas_call | solution.py:342
  64.5 5.6 %all-to-all-start.2 = ((bf16[32,64,128]{2,1,0:T(8,128)(2,1)}), bf16[32,64,128]{2,1,0:T(8,128)(2,1)S(1)}, u32[]{:S(2)}, u32[]{:S(2)}) async-start(bf16[32,64,128]{2,1,0:T(8,128)(2,1)} %get-tuple-element.22), calls=%async_computation.2 | async-start | bytes 1048576 | tf_op jit(solution)/shard_map/all_to_all | solution.py:310
  70.1 3.1 %collective-permute-start.2 = (bf16[32,2048]{1,0:T(8,128)(2,1)}, bf16[32,2048]{1,0:T(8,128)(2,1)S(1)}, u32[]{:S(2)}, u32[]{:S(2)}) collective-permute-start(bf16[32,2048]{1,0:T(8,128)(2,1)} %get-tuple-element.11.v_ref.refs_0_), channel_id=1, source_target_pairs={{0,6},{2,0},{4,2},{6,4},{1,7},{3,1},{5,3},{7,5},{8,14},{10,8},{12,... | collective-permute-start | bytes 393224 | tf_op jit(solution)/shard_map/ppermute | solution.py:359
  73.2 0.6 collective-permute-start.1
  73.8 1.0 collective-permute-start
  74.8 0.0 collective-permute-start.3
  74.8 2.9 %collective-permute-done.2.refs_3_ = bf16[32,2048]{1,0:T(8,128)(2,1)S(1)} collective-permute-done((bf16[32,2048]{1,0:T(8,128)(2,1)}, bf16[32,2048]{1,0:T(8,128)(2,1)S(1)}, u32[]{:S(2)}, u32[]{:S(2)}) %collective-permute-start.2) | collective-permute-done | bytes 131104 | tf_op jit(solution)/shard_map/ppermute | solution.py:359
  77.7 0.0 copy-start.3
  77.7 0.0 collective-permute-start.6
  77.7 2.2 %collective-permute-done.1.refs_2_ = bf16[32,2048]{1,0:T(8,128)(2,1)S(1)} collective-permute-done((bf16[32,2048]{1,0:T(8,128)(2,1)}, bf16[32,2048]{1,0:T(8,128)(2,1)S(1)}, u32[]{:S(2)}, u32[]{:S(2)}) %collective-permute-start.1) | collective-permute-done | bytes 131104 | tf_op jit(solution)/shard_map/ppermute | solution.py:359
  79.9 0.0 copy-start.4
  79.9 0.0 collective-permute-start.5
  79.9 1.3 %collective-permute-done.refs_1_ = bf16[32,2048]{1,0:T(8,128)(2,1)S(1)} collective-permute-done((bf16[32,2048]{1,0:T(8,128)(2,1)}, bf16[32,2048]{1,0:T(8,128)(2,1)S(1)}, u32[]{:S(2)}, u32[]{:S(2)}) %collective-permute-start) | collective-permute-done | bytes 131104 | tf_op jit(solution)/shard_map/ppermute | solution.py:359
  81.2 0.0 copy-start.5
  81.2 0.0 collective-permute-start.4
  81.2 6.4 %local_product.3.y_ref = f32[32,2048]{1,0:T(8,128)} custom-call(s32[16,128]{1,0:T(8,128)} %get-tuple-element.14.idx_ref.refs_0_, bf16[32,2048]{1,0:T(8,128)(2,1)} %get-tuple-element.11.v_ref.refs_0_, bf16[32,64,640]{2,1,0:T(8,128)(2,1)} %get-tuple-element.20.um_ref), custom_call_target="tpu_custom_call" | custom-call | tf_op jit(solution)/shard_map/local_product/pallas_call | solution.py:331
  87.6 0.0 collective-permute-done.3.refs_4_
  87.6 0.0 copy-start.6
  87.6 0.0 collective-permute-done.6.refs_7_
  87.6 0.0 copy-start.7
  87.6 0.0 collective-permute-done.5.refs_6_
  87.6 0.0 copy-start.8
  87.7 0.0 collective-permute-done.4.refs_5_
  87.7 0.0 copy-start.9
  87.7 0.0 all-to-all-done.2.recv_ref
  87.7 0.0 copy-done.3
  87.7 0.0 copy-done.4
  87.7 0.0 copy-done.5
  87.7 0.6 copy-done.6
  88.3 0.1 copy-done.7
  88.3 0.0 copy-done.8
  88.4 0.1 copy-done.9
  88.4 0.0 copy-start
  88.4 0.8 copy-done
  89.2 4.3 %image.1 = bf16[8,64,256]{2,1,0:T(8,128)(2,1)} custom-call(s32[16,128]{1,0:T(8,128)} %get-tuple-element.14.idx_ref.refs_0_, bf16[32,64,128]{2,1,0:T(8,128)(2,1)} %copy-done, f32[32,2048]{1,0:T(8,128)} %local_product.3.y_ref, bf16[32,64,256]{2,1,0:T(8,128)(2,1)} %get-tuple-element.17.refs_5_.wd_ref, bf16[32,2048]{1,0:T(8,128)(2,1)} %get-tuple-element.11.v_ref.refs_0_, ...), custom_call_target="tpu_custom_call" | custom-call | tf_op jit(solution)/shard_map/image/pallas_call | solution.py:362
  93.5 19.1 %all_to_all.25.in_ref = bf16[8,64,256]{2,1,0:T(8,128)(2,1)S(1)} all-to-all(bf16[8,64,256]{2,1,0:T(8,128)(2,1)} %image.1), channel_id=1, replica_groups=mesh['z'=8,'x'=4,'y'=4,'c'=2] {'z'}, dimensions={0} | all-to-all | bytes 524288 | tf_op jit(solution)/shard_map/all_to_all | solution.py:376
  112.7 9.1 %all_to_all.26.in_ref = bf16[4,64,256]{2,1,0:T(8,128)(2,1)S(1)} all-to-all(bf16[4,64,256]{2,1,0:T(8,128)(2,1)S(1)} %sum_z.1), channel_id=1, replica_groups=mesh['z'=8,'x'=4,'y'=4,'c'=2] {'x'}, dimensions={0} | all-to-all | bytes 262144 | tf_op jit(solution)/shard_map/all_to_all | solution.py:383
  121.8 0.6 sum_x.1
  (1 shorter events, 0.0 us)
Async XLA Ops:
  4.5 28.4 %all-to-all-start = ((bf16[32,64,128]{2,1,0:T(8,128)(2,1)}), bf16[32,64,128]{2,1,0:T(8,128)(2,1)S(1)}, u32[]{:S(2)}, u32[]{:S(2)}) async-start(bf16[32,64,128]{2,1,0:T(8,128)(2,1)} %get-tuple-element.15), calls=%async_computation | async-start | bytes 1048576 | tf_op jit(solution)/shard_map/all_to_all | solution.py:310
  32.9 0.8 copy-start.1
  38.0 21.5 %all-to-all-start.1 = ((bf16[32,64,128]{2,1,0:T(8,128)(2,1)}), bf16[32,64,128]{2,1,0:T(8,128)(2,1)S(1)}, u32[]{:S(2)}, u32[]{:S(2)}) async-start(bf16[32,64,128]{2,1,0:T(8,128)(2,1)} %get-tuple-element.18), calls=%async_computation.1 | async-start | bytes 1048576 | tf_op jit(solution)/shard_map/all_to_all | solution.py:310
  59.4 0.8 copy-start.2
  64.5 23.2 %all-to-all-start.2 = ((bf16[32,64,128]{2,1,0:T(8,128)(2,1)}), bf16[32,64,128]{2,1,0:T(8,128)(2,1)S(1)}, u32[]{:S(2)}, u32[]{:S(2)}) async-start(bf16[32,64,128]{2,1,0:T(8,128)(2,1)} %get-tuple-element.22), calls=%async_computation.2 | async-start | bytes 1048576 | tf_op jit(solution)/shard_map/all_to_all | solution.py:310
  70.1 7.6 %collective-permute-start.2 = (bf16[32,2048]{1,0:T(8,128)(2,1)}, bf16[32,2048]{1,0:T(8,128)(2,1)S(1)}, u32[]{:S(2)}, u32[]{:S(2)}) collective-permute-start(bf16[32,2048]{1,0:T(8,128)(2,1)} %get-tuple-element.11.v_ref.refs_0_), channel_id=1, source_target_pairs={{0,6},{2,0},{4,2},{6,4},{1,7},{3,1},{5,3},{7,5},{8,14},{10,8},{12,... | collective-permute-start | bytes 393224 | tf_op jit(solution)/shard_map/ppermute | solution.py:359
  73.2 6.8 %collective-permute-start.1 = (bf16[32,2048]{1,0:T(8,128)(2,1)}, bf16[32,2048]{1,0:T(8,128)(2,1)S(1)}, u32[]{:S(2)}, u32[]{:S(2)}) collective-permute-start(bf16[32,2048]{1,0:T(8,128)(2,1)} %get-tuple-element.11.v_ref.refs_0_), channel_id=1, source_target_pairs={{0,4},{2,6},{4,0},{6,2},{1,5},{3,7},{5,1},{7,3},{8,12},{10,14},{12... | collective-permute-start | bytes 393224 | tf_op jit(solution)/shard_map/ppermute | solution.py:359
  73.8 7.5 %collective-permute-start = (bf16[32,2048]{1,0:T(8,128)(2,1)}, bf16[32,2048]{1,0:T(8,128)(2,1)S(1)}, u32[]{:S(2)}, u32[]{:S(2)}) collective-permute-start(bf16[32,2048]{1,0:T(8,128)(2,1)} %get-tuple-element.11.v_ref.refs_0_), channel_id=1, source_target_pairs={{0,2},{2,4},{4,6},{6,0},{1,3},{3,5},{5,7},{7,1},{8,10},{10,12},{12... | collective-permute-start | bytes 393224 | tf_op jit(solution)/shard_map/ppermute | solution.py:359
  74.8 12.9 %collective-permute-start.3 = (bf16[32,2048]{1,0:T(8,128)(2,1)}, bf16[32,2048]{1,0:T(8,128)(2,1)S(1)}, u32[]{:S(2)}, u32[]{:S(2)}) collective-permute-start(bf16[32,2048]{1,0:T(8,128)(2,1)} %get-tuple-element.11.v_ref.refs_0_), channel_id=1, source_target_pairs={{0,1},{1,0},{2,3},{3,2},{4,5},{5,4},{6,7},{7,6},{8,9},{9,8},{10,11... | collective-permute-start | bytes 393224 | tf_op jit(solution)/shard_map/ppermute | solution.py:361
  77.7 10.0 %copy-start.3 = (bf16[32,2048]{1,0:T(8,128)(2,1)}, bf16[32,2048]{1,0:T(8,128)(2,1)S(1)}, u32[]{:S(2)}) copy-start(bf16[32,2048]{1,0:T(8,128)(2,1)S(1)} %collective-permute-done.2.refs_3_) | copy-start | bytes 393220
  77.7 9.9 %collective-permute-start.6 = (bf16[32,2048]{1,0:T(8,128)(2,1)S(1)}, bf16[32,2048]{1,0:T(8,128)(2,1)S(1)}, u32[]{:S(2)}, u32[]{:S(2)}) collective-permute-start(bf16[32,2048]{1,0:T(8,128)(2,1)S(1)} %collective-permute-done.2.refs_3_), channel_id=1, source_target_pairs={{0,1},{1,0},{2,3},{3,2},{4,5},{5,4},{6,7},{7,6},{8,9},{9,8},{10,11... | collective-permute-start | bytes 393224 | tf_op jit(solution)/shard_map/ppermute | solution.py:361
  79.9 7.8 %copy-start.4 = (bf16[32,2048]{1,0:T(8,128)(2,1)}, bf16[32,2048]{1,0:T(8,128)(2,1)S(1)}, u32[]{:S(2)}) copy-start(bf16[32,2048]{1,0:T(8,128)(2,1)S(1)} %collective-permute-done.1.refs_2_) | copy-start | bytes 393220
  79.9 7.7 %collective-permute-start.5 = (bf16[32,2048]{1,0:T(8,128)(2,1)S(1)}, bf16[32,2048]{1,0:T(8,128)(2,1)S(1)}, u32[]{:S(2)}, u32[]{:S(2)}) collective-permute-start(bf16[32,2048]{1,0:T(8,128)(2,1)S(1)} %collective-permute-done.1.refs_2_), channel_id=1, source_target_pairs={{0,1},{1,0},{2,3},{3,2},{4,5},{5,4},{6,7},{7,6},{8,9},{9,8},{10,11... | collective-permute-start | bytes 393224 | tf_op jit(solution)/shard_map/ppermute | solution.py:361
  81.2 6.5 %copy-start.5 = (bf16[32,2048]{1,0:T(8,128)(2,1)}, bf16[32,2048]{1,0:T(8,128)(2,1)S(1)}, u32[]{:S(2)}) copy-start(bf16[32,2048]{1,0:T(8,128)(2,1)S(1)} %collective-permute-done.refs_1_) | copy-start | bytes 393220
  81.2 6.4 %collective-permute-start.4 = (bf16[32,2048]{1,0:T(8,128)(2,1)S(1)}, bf16[32,2048]{1,0:T(8,128)(2,1)S(1)}, u32[]{:S(2)}, u32[]{:S(2)}) collective-permute-start(bf16[32,2048]{1,0:T(8,128)(2,1)S(1)} %collective-permute-done.refs_1_), channel_id=1, source_target_pairs={{0,1},{1,0},{2,3},{3,2},{4,5},{5,4},{6,7},{7,6},{8,9},{9,8},{10,11... | collective-permute-start | bytes 393224 | tf_op jit(solution)/shard_map/ppermute | solution.py:361
  87.6 0.7 copy-start.6
  87.6 0.7 copy-start.7
  87.6 0.7 copy-start.8
  87.7 0.8 copy-start.9
  88.4 0.8 copy-start

commit v3 on v2

v3 whole, which is shorter than its diff:
```python
import jax
import jax.numpy as jnp
from jax import lax
from jax.experimental import pallas as pl
from jax.experimental.pallas import tpu as pltpu
from jax.sharding import Mesh, PartitionSpec as P

B = 64
K = 12
RB = 32
MC = 32
PEERS = 32
NZ, NX, NY, NC = 8, 4, 4, 2
STRIDE = 40
ROOM = 1024
TABLE = 8192
LOCAL = ((0, 3), (4, 5), (6, 7), (8, 9), (10, 11))
LW = 128 * len(LOCAL)
center_value = 0.25
half_width = 1.5
bf16 = jnp.bfloat16
f32 = jnp.float32
MIB = 1024 * 1024

NN = (((1,), (0,)), ((), ()))
NT = (((1,), (1,)), ((), ()))


def low_half(rows=MC):
    return lax.broadcasted_iota(jnp.int32, (rows, 128), 1) < B


def dot(a, b, dims):
    return lax.dot_general(a, b, dims, preferred_element_type=f32)


def store_pair(even_odd_ref, first, second, low):
    even_odd_ref[pl.ds(0, 32, stride=2), :] = jnp.where(low, first, pltpu.roll(second, B, 1))
    even_odd_ref[pl.ds(1, 32, stride=2), :] = jnp.where(low, pltpu.roll(first, B, 1), second)


def duplicate(tile, low):
    turned = pltpu.roll(tile, B, 1)
    return jnp.where(low, tile, turned), jnp.where(low, turned, tile)


def emit_picks(msg_ref, dup_ref, send, low):
    for q in range(PEERS):
        msg_ref[q, 0:MC, :] = jnp.where(
            low, dup_ref[send(2 * q)], dup_ref[send(2 * q + 1)]
        ).astype(bf16)


def emit_mirror(msg_ref, prod_ref, inv_ref, low):
    for q in range(PEERS):
        msg_ref[q, MC : 2 * MC, :] = jnp.where(
            low, prod_ref[inv_ref[2 * q]], prod_ref[inv_ref[2 * q + 1]]
        ).astype(bf16)


def invert_slots(inv_ref, src_ref):
    for i in range(RB):
        for k in (1, 2):
            inv_ref[src_ref[k, i] - RB] = 2 * i + k - 1


def mirror_products(dup_ref, wd_ref, prod_ref):
    for i in range(RB):
        prod = dot(dup_ref[i][:, 0:B].astype(bf16), wd_ref[i], NN)
        prod_ref[2 * i] = prod[:, 0:128]
        prod_ref[2 * i + 1] = prod[:, 128:256]


def starter(sems):
    taken = iter(range(sems.shape[0]))

    def start(source, target):
        copy = pltpu.make_async_copy(source, target, sems.at[next(taken)])
        copy.start()
        return copy

    return start


def unpack_rows(rows_ref, hb_ref):
    for j in range(32):
        rows_ref[STRIDE * j : STRIDE * j + 32, :] = hb_ref[:, 128 * j : 128 * (j + 1)].astype(f32)


def unpacked_row(rows_ref, i):
    return rows_ref[pl.ds(i, 32, stride=STRIDE), :]


def first_message_kernel(src_hbm, send_hbm, v_hbm, hb_hbm, msg_hbm, wd_hbm, table_hbm, keep_hbm, src_ref, send_ref, srcv_ref, sendv_ref, table_ref, v_ref, hb_ref, msg_ref, wd_ref, rows_ref, pair_ref, dup_ref, prod_ref, inv_ref, sems):
    low = low_half()
    start = starter(sems)
    blocks = [start(hb_hbm.at[k], hb_ref.at[k - 1]) for k in (1, 2)]
    vectors = start(v_hbm, v_ref)
    send = start(send_hbm, send_ref)
    src = start(src_hbm, src_ref)
    tables = [start(src_hbm, srcv_ref), start(send_hbm, sendv_ref)]
    vectors.wait()
    keep_out = start(v_ref, keep_hbm.at[0:MC, :])
    for t in range(RB // 2):
        tile = v_ref[:, 128 * t : 128 * (t + 1)].astype(f32)
        dup_ref[2 * t], dup_ref[2 * t + 1] = duplicate(tile, low)
    send.wait()
    emit_picks(msg_ref, dup_ref, lambda c: send_ref[0, c], low)
    picks_out = start(msg_ref.at[:, 0:MC, :], msg_hbm.at[:, 0:MC, :])
    for copy in tables:
        copy.wait()
    table_ref[...] = jnp.zeros(table_ref.shape, jnp.int32)
    table_ref[0:K, 0:RB] = srcv_ref[...]
    table_ref[K : K + 1, 0 : 2 * PEERS] = sendv_ref[...]
    table_out = start(table_ref, table_hbm.at[0:16, :])
    src.wait()
    invert_slots(inv_ref, src_ref)
    for k in (1, 2):
        blocks[k - 1].wait()
        unpack_rows(rows_ref.at[k - 1], hb_ref.at[k - 1])
        for i in range(RB):
            block = unpacked_row(rows_ref.at[k - 1], i)
            pair = pair_ref.at[k - 1, i]
            store_pair(pair, block, block, low)
            wd_ref[i, :, 128 * (k - 1) : 128 * k] = pair[...].astype(bf16)
    weights_out = start(wd_ref, wd_hbm.at[0:RB])
    mirror_products(dup_ref, wd_ref, prod_ref)
    emit_mirror(msg_ref, prod_ref, inv_ref, low)
    mirror_out = start(msg_ref.at[:, MC : 2 * MC, :], msg_hbm.at[:, MC : 2 * MC, :])
    for copy in (keep_out, table_out, picks_out, weights_out, mirror_out):
        copy.wait()


def local_sums(src_ref, v_ref, um_ref, um_ready, y_ref, dup_ref, dupb_ref, lhs_ref, mir_ref, acc_ref):
    low = low_half()
    for t in range(RB // 2):
        tile = v_ref[:, 128 * t : 128 * (t + 1)].astype(f32)
        one, two = duplicate(tile, low)
        dup_ref[2 * t], dup_ref[2 * t + 1] = one, two
        dupb_ref[2 * t], dupb_ref[2 * t + 1] = one.astype(bf16), two.astype(bf16)

    def gather(i, _):
        for t, (k0, k1) in enumerate(LOCAL):
            j0 = i if k0 == 0 else jnp.minimum(src_ref[k0, i], RB - 1)
            j1 = jnp.minimum(src_ref[k1, i], RB - 1)
            lhs_ref[i, :, 128 * t : 128 * (t + 1)] = jnp.where(low, dup_ref[j0], dup_ref[j1]).astype(bf16)
        return 0

    lax.fori_loop(0, RB, gather, 0, unroll=4)
    um_ready()
    for i in range(RB):
        mir_ref[i] = dot(dupb_ref[i][:, 0:B], um_ref[i], NN)
    for i in range(RB):
        acc_ref[i, :, 0:B] = dot(lhs_ref[i], um_ref[i], NT)
        acc_ref[i, :, B:128] = jnp.zeros((MC, B), f32)

    def scatter(i, _):
        for t, (k0, k1) in enumerate(LOCAL):
            j0 = i if k0 == 0 else jnp.minimum(src_ref[k0, i], RB - 1)
            j1 = jnp.minimum(src_ref[k1, i], RB - 1)
            part = mir_ref[i, :, 128 * t : 128 * (t + 1)]
            acc_ref[j0] += jnp.where(low, part, 0.0)
            acc_ref[j1] += jnp.where(low, 0.0, part)
        return 0

    lax.fori_loop(0, RB, scatter, 0, unroll=4)
    for t in range(RB // 2):
        y_ref[:, 128 * t : 128 * (t + 1)] = folded(acc_ref, t, low)


def first_local_kernel(src_hbm, counts_hbm, v_hbm, hb_hbm, um_hbm, y_hbm, src_ref, counts_ref, v_ref, hb_ref, um_ref, y_ref, rows_ref, pair_ref, dup_ref, dupb_ref, lhs_ref, mir_ref, acc_ref, sems, hb_sems):
    low = low_half()
    start = starter(sems)
    counts = start(counts_hbm, counts_ref)

    def block_copies(t):
        k0, k1 = jnp.where(t == 0, 0, 2 * t + 2), 2 * t + 3
        return (
            pltpu.make_async_copy(hb_hbm.at[k0], hb_ref.at[2 * t], hb_sems.at[2 * t]),
            pltpu.make_async_copy(hb_hbm.at[k1], hb_ref.at[2 * t + 1], hb_sems.at[2 * t + 1]),
        )

    for t in range(len(LOCAL)):
        for copy in block_copies(t):
            copy.start()
    src = start(src_hbm, src_ref)
    vectors = start(v_hbm, v_ref)
    counts.wait()

    def relayout(t, _):
        for copy in block_copies(t):
            copy.wait()
        unpack_rows(rows_ref.at[0], hb_ref.at[2 * t])
        unpack_rows(rows_ref.at[1], hb_ref.at[2 * t + 1])
        k0, k1 = jnp.where(t == 0, 0, 2 * t + 2), 2 * t + 3
        lanes = pl.ds(pl.multiple_of(t * 128, 128), 128)
        for i in range(RB):
            count = counts_ref[i]
            one = jnp.where(k0 < count, unpacked_row(rows_ref.at[0], i), 0.0)
            two = jnp.where(k1 < count, unpacked_row(rows_ref.at[1], i), 0.0)
            store_pair(pair_ref.at[i], one, two, low)
            um_ref[i, :, lanes] = pair_ref[i].astype(bf16)
        return 0

    lax.fori_loop(0, len(LOCAL), relayout, 0)
    um_out = start(um_ref, um_hbm)
    src.wait()
    vectors.wait()
    local_sums(src_ref, v_ref, um_ref, lambda: None, y_ref, dup_ref, dupb_ref, lhs_ref, mir_ref, acc_ref)
    y_out = start(y_ref, y_hbm.at[0:MC, :])
    um_out.wait()
    y_out.wait()


def local_kernel(src_hbm, v_hbm, um_hbm, y_hbm, src_ref, v_ref, um_ref, y_ref, dup_ref, dupb_ref, lhs_ref, mir_ref, acc_ref, sems):
    start = starter(sems)
    vectors = start(v_hbm.at[0:MC, :], v_ref)
    src = start(src_hbm, src_ref)
    um = start(um_hbm, um_ref)
    vectors.wait()
    src.wait()
    local_sums(src_ref, v_ref, um_ref, um.wait, y_ref, dup_ref, dupb_ref, lhs_ref, mir_ref, acc_ref)
    start(y_ref, y_hbm.at[0:MC, :]).wait()


def remote_sum(table_ref, recv_ref, wd_ref, wd_ready, lhs_ref, acc_ref):
    low = low_half()
    lane = lax.broadcasted_iota(jnp.int32, (MC, 128), 1) // B

    def gather(i, _):
        for k in (1, 2):
            s = table_ref[k, i] - RB
            tile = recv_ref[s // 2, 0:MC, :].astype(f32)
            lhs_ref[i, :, 128 * (k - 1) : 128 * k] = jnp.where(lane == s % 2, tile, 0.0).astype(bf16)
        return 0

    lax.fori_loop(0, RB, gather, 0, unroll=4)
    wd_ready()
    for i in range(RB):
        acc_ref[i, :, 0:B] = dot(lhs_ref[i], wd_ref[i], NT)
        acc_ref[i, :, B:128] = jnp.zeros((MC, B), f32)

    def scatter(q, _):
        tile = recv_ref[q, MC : 2 * MC, :].astype(f32)
        acc_ref[table_ref[K, 2 * q]] += jnp.where(low, tile, 0.0)
        acc_ref[table_ref[K, 2 * q + 1]] += jnp.where(low, 0.0, tile)
        return 0

    lax.fori_loop(0, PEERS, scatter, 0, unroll=4)


def folded(acc_ref, t, low):
    one, two = acc_ref[2 * t], acc_ref[2 * t + 1]
    return jnp.where(low, one + pltpu.roll(one, B, 1), two + pltpu.roll(two, B, 1))


def step_kernel(second, table_hbm, recv_ref, y_hbm, v_hbm, prev_hbm, wd_hbm, out_hbm, msg_hbm, table_ref, y_ref, v_ref, prev_ref, wd_ref, out_ref, msg_ref, lhs_ref, acc_ref, dup_ref, prod_ref, inv_ref, sems):
    low = low_half()
    start = starter(sems)
    table = start(table_hbm.at[0:16, :], table_ref)
    wd = start(wd_hbm.at[0:RB], wd_ref)
    terms = [start(y_hbm.at[0:MC, :], y_ref), start(v_hbm.at[0:MC, :], v_ref)]
    if second:
        terms.append(start(prev_hbm.at[0:MC, :], prev_ref))
    table.wait()
    invert_slots(inv_ref, table_ref)
    remote_sum(table_ref, recv_ref, wd_ref, wd.wait, lhs_ref, acc_ref)
    for copy in terms:
        copy.wait()
    for t in range(RB // 2):
        lanes = slice(128 * t, 128 * (t + 1))
        image = folded(acc_ref, t, low) + y_ref[:, lanes]
        if second:
            tile = 2.0 * (image - center_value * prev_ref[:, lanes].astype(f32)) / half_width - v_ref[:, lanes].astype(f32)
        else:
            tile = (image - center_value * v_ref[:, lanes].astype(f32)) / half_width
        tile = tile.astype(bf16)
        out_ref[:, lanes] = tile
        dup_ref[2 * t], dup_ref[2 * t + 1] = duplicate(tile.astype(f32), low)
    result_out = start(out_ref, out_hbm.at[0:MC, :])
    emit_picks(msg_ref, dup_ref, lambda c: table_ref[K, c], low)
    picks_out = start(msg_ref.at[:, 0:MC, :], msg_hbm.at[:, 0:MC, :])
    mirror_products(dup_ref, wd_ref, prod_ref)
    emit_mirror(msg_ref, prod_ref, inv_ref, low)
    mirror_out = start(msg_ref.at[:, MC : 2 * MC, :], msg_hbm.at[:, MC : 2 * MC, :])
    result_out.wait()
    picks_out.wait()
    mirror_out.wait()


def image_kernel(table_hbm, recv_ref, y_hbm, wd_hbm, *refs):
    own, other = refs[0:NY], refs[NY : 2 * NY]
    out_ref, table_ref, y_ref, wd_ref, lhs_ref, acc_ref, stack_ref, all_ref, sems = refs[2 * NY :]
    low = low_half()
    start = starter(sems)
    table = start(table_hbm.at[0:16, :], table_ref)
    wd = start(wd_hbm.at[0:RB], wd_ref)
    y_sum = start(y_hbm.at[0:MC, :], y_ref)
    y, c = lax.axis_index("y"), lax.axis_index("c")
    moves = [start(own[0], stack_ref.at[0:MC, :])]
    for d in range(NY):
        from_y = lax.rem(y + NY - d, NY) * NC
        for block, core in ((own[d], c), (other[d], 1 - c)):
            moves.append(start(block, all_ref.at[pl.ds(pl.multiple_of((from_y + core) * MC, MC), MC), :]))
    table.wait()
    remote_sum(table_ref, recv_ref, wd_ref, wd.wait, lhs_ref, acc_ref)
    y_sum.wait()
    for t in range(RB // 2):
        lanes = slice(128 * t, 128 * (t + 1))
        stack_ref[MC : 2 * MC, lanes] = (folded(acc_ref, t, low) + y_ref[:, lanes]).astype(bf16)
    for copy in moves:
        copy.wait()
    part = dot(stack_ref[...], all_ref[...], NT).astype(bf16)
    for z in range(NZ):
        out_ref[z] = part


def sum_z_kernel(in_ref, out_ref):
    total = in_ref[0].astype(f32)
    for z in range(1, NZ):
        total = total + in_ref[z].astype(f32)
    total = total.astype(bf16)
    for x in range(NX):
        out_ref[x] = total


def sum_x_kernel(in_ref, gram_ref, proj_ref):
    total = in_ref[0].astype(f32)
    for x in range(1, NX):
        total = total + in_ref[x].astype(f32)
    gram_ref[...] = total[0:MC, :]
    proj_ref[...] = total[MC : 2 * MC, :]


VM = pl.BlockSpec(memory_space=pltpu.VMEM)
ANY = pl.BlockSpec(memory_space=pl.ANY)
HBM = pl.BlockSpec(memory_space=pltpu.HBM)
shape = jax.ShapeDtypeStruct


def limit(mib):
    return pltpu.CompilerParams(vmem_limit_bytes=int(mib * MIB))


def semaphores(count):
    return pltpu.SemaphoreType.DMA((count,))


def on_device(vectors, hblocks, counts, sources, send_rows):
    cols, width = vectors.shape
    row_axes, rows = ("z", "x"), hblocks.shape[0]
    msg_shape = shape((PEERS, 2 * MC, 128), bf16)
    um_shape = shape((rows, B, LW), bf16)
    vec = pltpu.VMEM((cols, width), bf16)
    vec_sum = pltpu.VMEM((cols, width), f32)
    msg = pltpu.VMEM(msg_shape.shape, bf16)
    wd_scratch = pltpu.VMEM((rows, B, 256), bf16)
    um_scratch = pltpu.VMEM(um_shape.shape, bf16)
    dup = pltpu.VMEM((rows, MC, 128), f32)
    dupb = pltpu.VMEM((rows, MC, 128), bf16)
    acc = pltpu.VMEM((rows, MC, 128), f32)
    prod = pltpu.VMEM((2 * rows, MC, 128), f32)
    inv = pltpu.SMEM((2 * PEERS,), jnp.int32)
    src = pltpu.SMEM((K, rows), jnp.int32)
    table_scratch = pltpu.SMEM((16, 128), jnp.int32)
    lhs = pltpu.VMEM((rows, MC, LW), bf16)
    lhs_remote = pltpu.VMEM((rows, MC, 256), bf16)
    mir = pltpu.VMEM((rows, MC, LW), f32)
    unpacked = pltpu.VMEM((2, STRIDE * 32, 128), f32)

    blocks = hblocks.transpose(1, 0, 2)
    sources = sources.T
    message, wd, table, kept = pl.pallas_call(
        first_message_kernel,
        out_shape=(
            msg_shape,
            shape((4 * rows, B, 256), bf16),
            shape((TABLE, 128), jnp.int32),
            shape((ROOM, width), bf16),
        ),
        in_specs=[HBM] * 4,
        out_specs=(HBM,) * 4,
        scratch_shapes=[
            src,
            pltpu.SMEM((1, 2 * PEERS), jnp.int32),
            pltpu.VMEM((K, rows), jnp.int32),
            pltpu.VMEM((1, 2 * PEERS), jnp.int32),
            pltpu.VMEM((16, 128), jnp.int32),
            vec,
            pltpu.VMEM((2, rows, B * B), bf16),
            msg,
            wd_scratch,
            unpacked,
            pltpu.VMEM((2, rows, B, 128), f32),
            dup,
            prod,
            inv,
            semaphores(12),
        ],
        compiler_params=limit(60),
        name="first_message",
    )(sources, send_rows[None], vectors, blocks)

    def exchange(message):
        return lax.all_to_all(message, row_axes, split_axis=0, concat_axis=0, tiled=True)

    received = exchange(message)
    local_scratch = [dup, dupb, lhs, mir, acc]
    um, local = pl.pallas_call(
        first_local_kernel,
        out_shape=(um_shape, shape((ROOM, width), f32)),
        in_specs=[HBM] * 4,
        out_specs=(HBM, HBM),
        scratch_shapes=[
            src,
            pltpu.SMEM((rows,), jnp.int32),
            vec,
            pltpu.VMEM((2 * len(LOCAL), rows, B * B), bf16),
            um_scratch,
            vec_sum,
            unpacked,
            pltpu.VMEM((rows, B, 128), f32),
        ]
        + local_scratch
        + [semaphores(5), semaphores(2 * len(LOCAL))],
        compiler_params=limit(60),
        name="first_local",
    )(sources, counts, vectors, blocks)

    def local_part(block):
        return pl.pallas_call(
            local_kernel,
            out_shape=shape((ROOM, width), f32),
            in_specs=[HBM] * 3,
            out_specs=HBM,
            scratch_shapes=[src, vec, um_scratch, vec_sum] + local_scratch + [semaphores(4)],
            compiler_params=limit(60),
            name="local_product",
        )(sources, block, um)

    def next_step(second, received, local, previous):
        return pl.pallas_call(
            lambda *refs: step_kernel(second, *refs),
            out_shape=(shape((cols if second else ROOM, width), bf16), msg_shape),
            in_specs=[HBM, VM] + [HBM] * 4,
            out_specs=(HBM, HBM),
            scratch_shapes=[table_scratch, vec_sum, vec, vec, wd_scratch, vec, msg, lhs_remote, acc, dup, prod, inv]
            + [semaphores(9)],
            compiler_params=limit(51.6),
            name="second_step" if second else "first_step",
        )(table, received, local, kept, previous, wd)

    first, message = next_step(False, received, local, kept)
    received = exchange(message)
    local = local_part(first)
    filtered, message = next_step(True, received, local, first)
    received = exchange(message)
    local = local_part(filtered)
    own = [filtered] + [
        lax.ppermute(filtered, "y", [(y, (y + d) % NY) for y in range(NY)]) for d in range(1, NY)
    ]
    other = [lax.ppermute(block, "c", [(0, 1), (1, 0)]) for block in own]
    part = pl.pallas_call(
        image_kernel,
        out_shape=shape((NZ, 2 * MC, NY * NC * MC), bf16),
        in_specs=[HBM, VM, HBM, HBM, HBM] + [ANY] * (2 * NY - 1),
        out_specs=VM,
        scratch_shapes=[
            table_scratch,
            vec_sum,
            wd_scratch,
            lhs_remote,
            acc,
            pltpu.VMEM((2 * MC, width), bf16),
            pltpu.VMEM((NY * NC * MC, width), bf16),
            semaphores(5 + 2 * NY),
        ],
        compiler_params=limit(51.6),
        name="image",
    )(table, received, local, wd, *own, *other)
    part = lax.all_to_all(part, "z", split_axis=0, concat_axis=0, tiled=True)
    part = pl.pallas_call(
        sum_z_kernel,
        out_shape=shape((NX,) + part.shape[1:], bf16),
        compiler_params=limit(4),
        name="sum_z",
    )(part)
    part = lax.all_to_all(part, "x", split_axis=0, concat_axis=0, tiled=True)
    gram, projected = pl.pallas_call(
        sum_x_kernel,
        out_shape=(shape((MC, NY * NC * MC), f32),) * 2,
        compiler_params=limit(4),
        name="sum_x",
    )(part)
    return filtered, gram.T, projected.T


def solution(mesh):
    axes = Mesh(mesh.devices.reshape(NZ, NX, NY, NC), ("z", "x", "y", "c"))
    row, col = ("z", "x"), ("y", "c")
    return jax.shard_map(
        on_device,
        mesh=axes,
        in_specs=(P(col, row), P(row, None, None), P(row), P(row, None), P(row)),
        out_specs=(P(col, row), P(None, col), P(None, col)),
        check_vma=False,
    )
```

time: 124 us -> 117 us (0.944)
  Pallas kernels: 42 us -> 33.6 us
  waiting for transfers between devices: 20.9 us -> 25.6 us
  local copies, waits for them, and re-layouts: 3.14 us -> 0.01 us
    pallas_call x4, Pallas kernels: 28.5 us -> 22.4 us  [the longest x2 11.2 us: local_part(): pl.pallas_call(local_kernel, out_shape=shape((ROOM, width), f32), in_spec...]
    all_to_all x3, waiting for transfers between devices: 14.4 us -> 19.1 us  [exchange(): lax.all_to_all(message, row_axes, split_axis=0, concat_axis=0, tiled=True)]
    unnamed x20 -> x2, local copies, waits for them, and re-layouts: 3.14 us -> 0.01 us
    pallas_call x2, Pallas kernels: 8.49 us -> 6.94 us  [next_step(): pl.pallas_call(lambda *refs: step_kernel(second, *refs), out_shape=(shape...]
  transfers between devices with their start and end apart: 10 -> 10, of which waited for: 5 -> 5; matrix products, arithmetic and copies ran while one was open for 0% -> 0% of each run, Pallas kernels for 20% -> 17%
where the time goes in v3:
time: 117 us; the launch traced here: 116 us
  Pallas kernels  33.6 us (29%)
  blocking collectives  28.1 us (24%)
  starting transfers between devices  27.5 us (24%)
  waiting for transfers between devices  25.6 us (22%)
    all_to_all x3, starting transfers between devices, exchange(): lax.all_to_all(message, row_axes, split_axis=0, concat_axis=0, tiled=True)  22.8 us
    all_to_all x3, waiting for transfers between devices, exchange(): lax.all_to_all(message, row_axes, split_axis=0, concat_axis=0, tiled=True)  19.1 us
    all_to_all x1, blocking collectives, on_device(): part = lax.all_to_all(part, 'z', split_axis=0, concat_axis=0, tiled=True)  19 us
    pallas_call x2, Pallas kernels, local_part(): pl.pallas_call(local_kernel, out_shape=shape((ROOM, width), f32), in_spec...  11.2 us
    all_to_all x1, blocking collectives, on_device(): part = lax.all_to_all(part, 'x', split_axis=0, concat_axis=0, tiled=True)  9.12 us
    pallas_call x1, Pallas kernels, on_device(): pl.pallas_call(first_local_kernel, out_shape=(um_shape, shape((ROOM, widt...  8.03 us
    pallas_call x2, Pallas kernels, next_step(): pl.pallas_call(lambda *refs: step_kernel(second, *refs), out_shape=(shape...  6.94 us
    ppermute x3, waiting for transfers between devices, on_device(): lax.ppermute(filtered, 'y', [(y, (y + d) % NY) for y in range(NY)])  6.47 us
  transfers between devices with their start and end apart: 10, of which 5 were waited for; matrix products, arithmetic and copies ran while one was open for 0% of the time, Pallas kernels for 17%

profile of v3, /device:TPU:2, one launch (start us, length us, event | category | flops | bytes accessed | tf_op | source)
XLA Modules:
  0.0 115.6 jit_solution(1119448671162806661)
XLA Ops:
  0.6 3.2 %first_message.1 = (bf16[32,64,128]{2,1,0:T(8,128)(2,1)}, bf16[128,64,256]{2,1,0:T(8,128)(2,1)}, s32[8192,128]{1,0:T(8,128)}, bf16[1024,2048]{1,0:T(8,128)(2,1)}) custom-call(s32[12,32]{1,0:T(8,128)} %bitcast.7, s32[1,64]{1,0:T(1,128)} %bitcast.11, bf16[32,2048]{1,0:T(8,128)(2,1)} %v_hbm.3, bf16[12,32,4096]{2,1,0:T(8,128)(2,1)} %bitcast.5), custom_call_target="tpu_custom_call" | custom-call | tf_op jit(solution)/shard_map/first_message/pallas_call | solution.py:373
  3.9 11.6 %all-to-all-start = ((bf16[32,64,128]{2,1,0:T(8,128)(2,1)}), bf16[32,64,128]{2,1,0:T(8,128)(2,1)S(1)}, u32[]{:S(2)}, u32[]{:S(2)}) async-start(bf16[32,64,128]{2,1,0:T(8,128)(2,1)} %get-tuple-element.16), calls=%async_computation | async-start | bytes 1048576 | tf_op jit(solution)/shard_map/all_to_all | solution.py:405
  15.5 8.0 %first_local.1 = (bf16[32,64,640]{2,1,0:T(8,128)(2,1)}, f32[1024,2048]{1,0:T(8,128)}) custom-call(s32[12,32]{1,0:T(8,128)} %bitcast.8, s32[32]{0:T(128)} %counts_hbm.1, bf16[32,2048]{1,0:T(8,128)(2,1)} %v_hbm.3, bf16[12,32,4096]{2,1,0:T(8,128)(2,1)} %bitcast.6), custom_call_target="tpu_custom_call" | custom-call | tf_op jit(solution)/shard_map/first_local/pallas_call | solution.py:409
  23.5 8.8 %all-to-all-done.refs_1_ = bf16[32,64,128]{2,1,0:T(8,128)(2,1)S(1)} async-done(((bf16[32,64,128]{2,1,0:T(8,128)(2,1)}), bf16[32,64,128]{2,1,0:T(8,128)(2,1)S(1)}, u32[]{:S(2)}, u32[]{:S(2)}) %all-to-all-start) | async-done | bytes 524320 | tf_op jit(solution)/shard_map/all_to_all | solution.py:405
  32.3 3.5 %first_step.1 = (bf16[1024,2048]{1,0:T(8,128)(2,1)}, bf16[32,64,128]{2,1,0:T(8,128)(2,1)}) custom-call(s32[8192,128]{1,0:T(8,128)} %get-tuple-element.15.refs_0_.table_hbm, bf16[32,64,128]{2,1,0:T(8,128)(2,1)S(1)} %all-to-all-done.refs_1_, f32[1024,2048]{1,0:T(8,128)} %get-tuple-element.17.refs_2_, bf16[1024,2048]{1,0:T(8,128)(2,1)} %get-tuple-element.18.refs_3_.refs_4_, ...), custom_call_target="tpu_custom_call" | custom-call | tf_op jit(solution)/shard_map/first_step/pallas_call | solution.py:442
  35.8 5.6 %all-to-all-start.1 = ((bf16[32,64,128]{2,1,0:T(8,128)(2,1)}), bf16[32,64,128]{2,1,0:T(8,128)(2,1)S(1)}, u32[]{:S(2)}, u32[]{:S(2)}) async-start(bf16[32,64,128]{2,1,0:T(8,128)(2,1)} %get-tuple-element.20), calls=%async_computation.1 | async-start | bytes 1048576 | tf_op jit(solution)/shard_map/all_to_all | solution.py:405
  41.4 5.6 %local_product.2.refs_2_ = f32[1024,2048]{1,0:T(8,128)} custom-call(s32[12,32]{1,0:T(8,128)} %bitcast.9, bf16[1024,2048]{1,0:T(8,128)(2,1)} %get-tuple-element.21.v_hbm.refs_4_, bf16[32,64,640]{2,1,0:T(8,128)(2,1)} %get-tuple-element.22.um_hbm), custom_call_target="tpu_custom_call" | custom-call | tf_op jit(solution)/shard_map/local_product/pallas_call | solution.py:431
  47.0 10.3 %all-to-all-done.1.refs_1_ = bf16[32,64,128]{2,1,0:T(8,128)(2,1)S(1)} async-done(((bf16[32,64,128]{2,1,0:T(8,128)(2,1)}), bf16[32,64,128]{2,1,0:T(8,128)(2,1)S(1)}, u32[]{:S(2)}, u32[]{:S(2)}) %all-to-all-start.1) | async-done | bytes 524320 | tf_op jit(solution)/shard_map/all_to_all | solution.py:405
  57.3 3.5 %second_step.1 = (bf16[32,2048]{1,0:T(8,128)(2,1)}, bf16[32,64,128]{2,1,0:T(8,128)(2,1)}) custom-call(s32[8192,128]{1,0:T(8,128)} %get-tuple-element.15.refs_0_.table_hbm, bf16[32,64,128]{2,1,0:T(8,128)(2,1)S(1)} %all-to-all-done.1.refs_1_, f32[1024,2048]{1,0:T(8,128)} %local_product.2.refs_2_, bf16[1024,2048]{1,0:T(8,128)(2,1)} %get-tuple-element.18.refs_3_.refs_4_, ...), custom_call_target="tpu_custom_call" | custom-call | tf_op jit(solution)/shard_map/second_step/pallas_call | solution.py:442
  60.8 5.6 %all-to-all-start.2 = ((bf16[32,64,128]{2,1,0:T(8,128)(2,1)}), bf16[32,64,128]{2,1,0:T(8,128)(2,1)S(1)}, u32[]{:S(2)}, u32[]{:S(2)}) async-start(bf16[32,64,128]{2,1,0:T(8,128)(2,1)} %get-tuple-element.24), calls=%async_computation.2 | async-start | bytes 1048576 | tf_op jit(solution)/shard_map/all_to_all | solution.py:405
  66.3 0.0 copy-start
  66.4 3.1 %collective-permute-start.2 = (bf16[32,2048]{1,0:T(8,128)(2,1)}, bf16[32,2048]{1,0:T(8,128)(2,1)S(1)}, u32[]{:S(2)}, u32[]{:S(2)}) collective-permute-start(bf16[32,2048]{1,0:T(8,128)(2,1)} %get-tuple-element.12.v_hbm.refs_0_), channel_id=1, source_target_pairs={{0,6},{2,0},{4,2},{6,4},{1,7},{3,1},{5,3},{7,5},{8,14},{10,8},{12,... | collective-permute-start | bytes 393224 | tf_op jit(solution)/shard_map/ppermute | solution.py:460
  69.4 0.6 collective-permute-start.1
  70.1 1.0 collective-permute-start
  71.1 0.0 collective-permute-start.3
  71.1 2.9 %collective-permute-done.2.refs_3_ = bf16[32,2048]{1,0:T(8,128)(2,1)S(1)} collective-permute-done((bf16[32,2048]{1,0:T(8,128)(2,1)}, bf16[32,2048]{1,0:T(8,128)(2,1)S(1)}, u32[]{:S(2)}, u32[]{:S(2)}) %collective-permute-start.2) | collective-permute-done | bytes 131104 | tf_op jit(solution)/shard_map/ppermute | solution.py:460
  74.0 0.0 collective-permute-start.6
  74.0 2.2 %collective-permute-done.1.refs_2_ = bf16[32,2048]{1,0:T(8,128)(2,1)S(1)} collective-permute-done((bf16[32,2048]{1,0:T(8,128)(2,1)}, bf16[32,2048]{1,0:T(8,128)(2,1)S(1)}, u32[]{:S(2)}, u32[]{:S(2)}) %collective-permute-start.1) | collective-permute-done | bytes 131104 | tf_op jit(solution)/shard_map/ppermute | solution.py:460
  76.2 0.0 collective-permute-start.5
  76.2 1.3 %collective-permute-done.refs_1_ = bf16[32,2048]{1,0:T(8,128)(2,1)S(1)} collective-permute-done((bf16[32,2048]{1,0:T(8,128)(2,1)}, bf16[32,2048]{1,0:T(8,128)(2,1)S(1)}, u32[]{:S(2)}, u32[]{:S(2)}) %collective-permute-start) | collective-permute-done | bytes 131104 | tf_op jit(solution)/shard_map/ppermute | solution.py:460
  77.5 0.0 collective-permute-start.4
  77.5 5.6 %local_product.3.y_hbm = f32[1024,2048]{1,0:T(8,128)} custom-call(s32[12,32]{1,0:T(8,128)} %bitcast.10, bf16[32,2048]{1,0:T(8,128)(2,1)} %get-tuple-element.12.v_hbm.refs_0_, bf16[32,64,640]{2,1,0:T(8,128)(2,1)} %get-tuple-element.22.um_hbm), custom_call_target="tpu_custom_call" | custom-call | tf_op jit(solution)/shard_map/local_product/pallas_call | solution.py:431
  83.1 0.0 collective-permute-done.3.refs_4_
  83.1 0.0 collective-permute-done.6.refs_7_
  83.2 0.0 collective-permute-done.5.refs_6_
  83.2 0.0 collective-permute-done.4.refs_5_
  83.2 0.0 all-to-all-done.2.recv_ref
  83.2 0.0 copy-done
  83.2 3.6 %image.1 = bf16[8,64,256]{2,1,0:T(8,128)(2,1)S(1)} custom-call(s32[8192,128]{1,0:T(8,128)} %get-tuple-element.15.refs_0_.table_hbm, bf16[32,64,128]{2,1,0:T(8,128)(2,1)S(1)} %all-to-all-done.2.recv_ref, f32[1024,2048]{1,0:T(8,128)} %local_product.3.y_hbm, bf16[128,64,256]{2,1,0:T(8,128)(2,1)} %get-tuple-element.19.refs_5_.wd_hbm, ...), custom_call_target="tpu_custom_call" | custom-call | tf_op jit(solution)/shard_map/image/pallas_call | solution.py:463
  86.8 19.0 %all_to_all.25.in_ref = bf16[8,64,256]{2,1,0:T(8,128)(2,1)S(1)} all-to-all(bf16[8,64,256]{2,1,0:T(8,128)(2,1)S(1)} %image.1), channel_id=1, replica_groups=mesh['z'=8,'x'=4,'y'=4,'c'=2] {'z'}, dimensions={0} | all-to-all | bytes 524288 | tf_op jit(solution)/shard_map/all_to_all | solution.py:481
  105.8 9.1 %all_to_all.26.in_ref = bf16[4,64,256]{2,1,0:T(8,128)(2,1)S(1)} all-to-all(bf16[4,64,256]{2,1,0:T(8,128)(2,1)S(1)} %sum_z.1), channel_id=1, replica_groups=mesh['z'=8,'x'=4,'y'=4,'c'=2] {'x'}, dimensions={0} | all-to-all | bytes 262144 | tf_op jit(solution)/shard_map/all_to_all | solution.py:488
  114.9 0.6 sum_x.1
  (1 shorter events, 0.0 us)
Async XLA Ops:
  3.9 28.5 %all-to-all-start = ((bf16[32,64,128]{2,1,0:T(8,128)(2,1)}), bf16[32,64,128]{2,1,0:T(8,128)(2,1)S(1)}, u32[]{:S(2)}, u32[]{:S(2)}) async-start(bf16[32,64,128]{2,1,0:T(8,128)(2,1)} %get-tuple-element.16), calls=%async_computation | async-start | bytes 1048576 | tf_op jit(solution)/shard_map/all_to_all | solution.py:405
  35.8 21.5 %all-to-all-start.1 = ((bf16[32,64,128]{2,1,0:T(8,128)(2,1)}), bf16[32,64,128]{2,1,0:T(8,128)(2,1)S(1)}, u32[]{:S(2)}, u32[]{:S(2)}) async-start(bf16[32,64,128]{2,1,0:T(8,128)(2,1)} %get-tuple-element.20), calls=%async_computation.1 | async-start | bytes 1048576 | tf_op jit(solution)/shard_map/all_to_all | solution.py:405
  60.8 22.4 %all-to-all-start.2 = ((bf16[32,64,128]{2,1,0:T(8,128)(2,1)}), bf16[32,64,128]{2,1,0:T(8,128)(2,1)S(1)}, u32[]{:S(2)}, u32[]{:S(2)}) async-start(bf16[32,64,128]{2,1,0:T(8,128)(2,1)} %get-tuple-element.24), calls=%async_computation.2 | async-start | bytes 1048576 | tf_op jit(solution)/shard_map/all_to_all | solution.py:405
  66.3 16.8 %copy-start = (bf16[32,2048]{1,0:T(8,128)(2,1)S(1)}, bf16[32,2048]{1,0:T(8,128)(2,1)}, u32[]{:S(2)}) copy-start(bf16[32,2048]{1,0:T(8,128)(2,1)} %get-tuple-element.12.v_hbm.refs_0_) | copy-start | bytes 393220
  66.4 7.6 %collective-permute-start.2 = (bf16[32,2048]{1,0:T(8,128)(2,1)}, bf16[32,2048]{1,0:T(8,128)(2,1)S(1)}, u32[]{:S(2)}, u32[]{:S(2)}) collective-permute-start(bf16[32,2048]{1,0:T(8,128)(2,1)} %get-tuple-element.12.v_hbm.refs_0_), channel_id=1, source_target_pairs={{0,6},{2,0},{4,2},{6,4},{1,7},{3,1},{5,3},{7,5},{8,14},{10,8},{12,... | collective-permute-start | bytes 393224 | tf_op jit(solution)/shard_map/ppermute | solution.py:460
  69.4 6.8 %collective-permute-start.1 = (bf16[32,2048]{1,0:T(8,128)(2,1)}, bf16[32,2048]{1,0:T(8,128)(2,1)S(1)}, u32[]{:S(2)}, u32[]{:S(2)}) collective-permute-start(bf16[32,2048]{1,0:T(8,128)(2,1)} %get-tuple-element.12.v_hbm.refs_0_), channel_id=1, source_target_pairs={{0,4},{2,6},{4,0},{6,2},{1,5},{3,7},{5,1},{7,3},{8,12},{10,14},{12... | collective-permute-start | bytes 393224 | tf_op jit(solution)/shard_map/ppermute | solution.py:460
  70.1 7.5 %collective-permute-start = (bf16[32,2048]{1,0:T(8,128)(2,1)}, bf16[32,2048]{1,0:T(8,128)(2,1)S(1)}, u32[]{:S(2)}, u32[]{:S(2)}) collective-permute-start(bf16[32,2048]{1,0:T(8,128)(2,1)} %get-tuple-element.12.v_hbm.refs_0_), channel_id=1, source_target_pairs={{0,2},{2,4},{4,6},{6,0},{1,3},{3,5},{5,7},{7,1},{8,10},{10,12},{12... | collective-permute-start | bytes 393224 | tf_op jit(solution)/shard_map/ppermute | solution.py:460
  71.1 12.1 %collective-permute-start.3 = (bf16[32,2048]{1,0:T(8,128)(2,1)}, bf16[32,2048]{1,0:T(8,128)(2,1)S(1)}, u32[]{:S(2)}, u32[]{:S(2)}) collective-permute-start(bf16[32,2048]{1,0:T(8,128)(2,1)} %get-tuple-element.12.v_hbm.refs_0_), channel_id=1, source_target_pairs={{0,1},{1,0},{2,3},{3,2},{4,5},{5,4},{6,7},{7,6},{8,9},{9,8},{10,11... | collective-permute-start | bytes 393224 | tf_op jit(solution)/shard_map/ppermute | solution.py:462
  74.0 9.1 %collective-permute-start.6 = (bf16[32,2048]{1,0:T(8,128)(2,1)S(1)}, bf16[32,2048]{1,0:T(8,128)(2,1)S(1)}, u32[]{:S(2)}, u32[]{:S(2)}) collective-permute-start(bf16[32,2048]{1,0:T(8,128)(2,1)S(1)} %collective-permute-done.2.refs_3_), channel_id=1, source_target_pairs={{0,1},{1,0},{2,3},{3,2},{4,5},{5,4},{6,7},{7,6},{8,9},{9,8},{10,11... | collective-permute-start | bytes 393224 | tf_op jit(solution)/shard_map/ppermute | solution.py:462
  76.2 6.9 %collective-permute-start.5 = (bf16[32,2048]{1,0:T(8,128)(2,1)S(1)}, bf16[32,2048]{1,0:T(8,128)(2,1)S(1)}, u32[]{:S(2)}, u32[]{:S(2)}) collective-permute-start(bf16[32,2048]{1,0:T(8,128)(2,1)S(1)} %collective-permute-done.1.refs_2_), channel_id=1, source_target_pairs={{0,1},{1,0},{2,3},{3,2},{4,5},{5,4},{6,7},{7,6},{8,9},{9,8},{10,11... | collective-permute-start | bytes 393224 | tf_op jit(solution)/shard_map/ppermute | solution.py:462
  77.5 5.6 %collective-permute-start.4 = (bf16[32,2048]{1,0:T(8,128)(2,1)S(1)}, bf16[32,2048]{1,0:T(8,128)(2,1)S(1)}, u32[]{:S(2)}, u32[]{:S(2)}) collective-permute-start(bf16[32,2048]{1,0:T(8,128)(2,1)S(1)} %collective-permute-done.refs_1_), channel_id=1, source_target_pairs={{0,1},{1,0},{2,3},{3,2},{4,5},{5,4},{6,7},{7,6},{8,9},{9,8},{10,11... | collective-permute-start | bytes 393224 | tf_op jit(solution)/shard_map/ppermute | solution.py:462

commit v4 on v3

--- a/solution.py
+++ b/solution.py
@@ -342,6 +342,9 @@
     return pltpu.CompilerParams(vmem_limit_bytes=int(mib * MIB))
 
 
+LOCAL_COST = pl.CostEstimate(flops=2 * 2 * RB * 10 * MC * B * B, bytes_accessed=20 * MIB, transcendentals=0)
+
+
 def semaphores(count):
     return pltpu.SemaphoreType.DMA((count,))
 
@@ -435,6 +438,7 @@
             out_specs=HBM,
             scratch_shapes=[src, vec, um_scratch, vec_sum] + local_scratch + [semaphores(4)],
             compiler_params=limit(60),
+            cost_estimate=LOCAL_COST,
             name="local_product",
         )(sources, block, um)
 
@@ -459,6 +463,8 @@
     own = [filtered] + [
         lax.ppermute(filtered, "y", [(y, (y + d) % NY) for y in range(NY)]) for d in range(1, NY)
     ]
+    local, *passed = lax.optimization_barrier((local, *own[1:]))
+    own = own[:1] + passed
     other = [lax.ppermute(block, "c", [(0, 1), (1, 0)]) for block in own]
     part = pl.pallas_call(
         image_kernel,

time: 117 us -> 113 us (0.966)
  blocking collectives: 28.1 us -> 25 us
  waiting for transfers between devices: 25.6 us -> 24.1 us
    ppermute x3, waiting for transfers between devices: 6.47 us -> 0.88 us  [on_device(): lax.ppermute(filtered, 'y', [(y, (y + d) % NY) for y in range(NY)])]
    all_to_all x1, blocking collectives: 19 us -> 15.9 us  [on_device(): part = lax.all_to_all(part, 'z', split_axis=0, concat_axis=0, tiled=True)]
    all_to_all x3, waiting for transfers between devices: 19.1 us -> 21.9 us  [exchange(): lax.all_to_all(message, row_axes, split_axis=0, concat_axis=0, tiled=True)]
    ppermute x4, waiting for transfers between devices: 0.01 us -> 1.34 us  [on_device(): other = [lax.ppermute(block, 'c', [(0, 1), (1, 0)]) for block in own]]
  transfers between devices with their start and end apart: 10 -> 10, of which waited for: 5 -> 7; matrix products, arithmetic and copies ran while one was open for 0% -> 0% of each run, Pallas kernels for 17% -> 17%
where the time goes in v4:
time: 113 us; the launch traced here: 111 us
  Pallas kernels  33.6 us (30%)
  starting transfers between devices  28 us (25%)
  blocking collectives  25 us (22%)
  waiting for transfers between devices  24.1 us (21%)
    all_to_all x3, starting transfers between devices, exchange(): lax.all_to_all(message, row_axes, split_axis=0, concat_axis=0, tiled=True)  22.8 us
    all_to_all x3, waiting for transfers between devices, exchange(): lax.all_to_all(message, row_axes, split_axis=0, concat_axis=0, tiled=True)  21.9 us
    all_to_all x1, blocking collectives, on_device(): part = lax.all_to_all(part, 'z', split_axis=0, concat_axis=0, tiled=True)  15.9 us
    pallas_call x2, Pallas kernels, local_part(): pl.pallas_call(local_kernel, out_shape=shape((ROOM, width), f32), in_spec...  11.2 us
    all_to_all x1, blocking collectives, on_device(): part = lax.all_to_all(part, 'x', split_axis=0, concat_axis=0, tiled=True)  9.12 us
    pallas_call x1, Pallas kernels, on_device(): pl.pallas_call(first_local_kernel, out_shape=(um_shape, shape((ROOM, widt...  8.03 us
    pallas_call x2, Pallas kernels, next_step(): pl.pallas_call(lambda *refs: step_kernel(second, *refs), out_shape=(shape...  6.93 us
    ppermute x3, starting transfers between devices, on_device(): lax.ppermute(filtered, 'y', [(y, (y + d) % NY) for y in range(NY)])  4.69 us
  transfers between devices with their start and end apart: 10, of which 7 were waited for; matrix products, arithmetic and copies ran while one was open for 0% of the time, Pallas kernels for 17%

profile of v4, /device:TPU:2, one launch (start us, length us, event | category | flops | bytes accessed | tf_op | source)
XLA Modules:
  0.0 111.4 jit_solution(13706729155092507515)
XLA Ops:
  0.6 3.2 %first_message.1 = (bf16[32,64,128]{2,1,0:T(8,128)(2,1)}, bf16[128,64,256]{2,1,0:T(8,128)(2,1)}, s32[8192,128]{1,0:T(8,128)}, bf16[1024,2048]{1,0:T(8,128)(2,1)}) custom-call(s32[12,32]{1,0:T(8,128)} %bitcast.7, s32[1,64]{1,0:T(1,128)} %bitcast.11, bf16[32,2048]{1,0:T(8,128)(2,1)} %v_hbm.3, bf16[12,32,4096]{2,1,0:T(8,128)(2,1)} %bitcast.5), custom_call_target="tpu_custom_call" | custom-call | tf_op jit(solution)/shard_map/first_message/pallas_call | solution.py:376
  3.9 11.6 %all-to-all-start = ((bf16[32,64,128]{2,1,0:T(8,128)(2,1)}), bf16[32,64,128]{2,1,0:T(8,128)(2,1)S(1)}, u32[]{:S(2)}, u32[]{:S(2)}) async-start(bf16[32,64,128]{2,1,0:T(8,128)(2,1)} %get-tuple-element.20), calls=%async_computation | async-start | bytes 1048576 | tf_op jit(solution)/shard_map/all_to_all | solution.py:408
  15.5 8.0 %first_local.1 = (bf16[32,64,640]{2,1,0:T(8,128)(2,1)}, f32[1024,2048]{1,0:T(8,128)}) custom-call(s32[12,32]{1,0:T(8,128)} %bitcast.8, s32[32]{0:T(128)} %counts_hbm.1, bf16[32,2048]{1,0:T(8,128)(2,1)} %v_hbm.3, bf16[12,32,4096]{2,1,0:T(8,128)(2,1)} %bitcast.6), custom_call_target="tpu_custom_call" | custom-call | tf_op jit(solution)/shard_map/first_local/pallas_call | solution.py:412
  23.5 8.8 %all-to-all-done.refs_1_ = bf16[32,64,128]{2,1,0:T(8,128)(2,1)S(1)} async-done(((bf16[32,64,128]{2,1,0:T(8,128)(2,1)}), bf16[32,64,128]{2,1,0:T(8,128)(2,1)S(1)}, u32[]{:S(2)}, u32[]{:S(2)}) %all-to-all-start) | async-done | bytes 524320 | tf_op jit(solution)/shard_map/all_to_all | solution.py:408
  32.3 3.5 %first_step.1 = (bf16[1024,2048]{1,0:T(8,128)(2,1)}, bf16[32,64,128]{2,1,0:T(8,128)(2,1)}) custom-call(s32[8192,128]{1,0:T(8,128)} %get-tuple-element.19.refs_0_.table_hbm, bf16[32,64,128]{2,1,0:T(8,128)(2,1)S(1)} %all-to-all-done.refs_1_, f32[1024,2048]{1,0:T(8,128)} %get-tuple-element.21.refs_2_, bf16[1024,2048]{1,0:T(8,128)(2,1)} %get-tuple-element.22.refs_3_.refs_4_, ...), custom_call_target="tpu_custom_call" | custom-call | tf_op jit(solution)/shard_map/first_step/pallas_call | solution.py:446
  35.8 5.6 %all-to-all-start.1 = ((bf16[32,64,128]{2,1,0:T(8,128)(2,1)}), bf16[32,64,128]{2,1,0:T(8,128)(2,1)S(1)}, u32[]{:S(2)}, u32[]{:S(2)}) async-start(bf16[32,64,128]{2,1,0:T(8,128)(2,1)} %get-tuple-element.24), calls=%async_computation.1 | async-start | bytes 1048576 | tf_op jit(solution)/shard_map/all_to_all | solution.py:408
  41.4 5.6 %local_product.2.refs_2_ = f32[1024,2048]{1,0:T(8,128)} custom-call(s32[12,32]{1,0:T(8,128)} %bitcast.9, bf16[1024,2048]{1,0:T(8,128)(2,1)} %get-tuple-element.25.v_hbm.refs_4_, bf16[32,64,640]{2,1,0:T(8,128)(2,1)} %get-tuple-element.26.um_hbm), custom_call_target="tpu_custom_call" | custom-call | flops 167772160 | bytes 20971520 | tf_op jit(solution)/shard_map/local_product/pallas_call | solution.py:434
  47.0 10.3 %all-to-all-done.1.refs_1_ = bf16[32,64,128]{2,1,0:T(8,128)(2,1)S(1)} async-done(((bf16[32,64,128]{2,1,0:T(8,128)(2,1)}), bf16[32,64,128]{2,1,0:T(8,128)(2,1)S(1)}, u32[]{:S(2)}, u32[]{:S(2)}) %all-to-all-start.1) | async-done | bytes 524320 | tf_op jit(solution)/shard_map/all_to_all | solution.py:408
  57.3 3.5 %second_step.1 = (bf16[32,2048]{1,0:T(8,128)(2,1)}, bf16[32,64,128]{2,1,0:T(8,128)(2,1)}) custom-call(s32[8192,128]{1,0:T(8,128)} %get-tuple-element.19.refs_0_.table_hbm, bf16[32,64,128]{2,1,0:T(8,128)(2,1)S(1)} %all-to-all-done.1.refs_1_, f32[1024,2048]{1,0:T(8,128)} %local_product.2.refs_2_, bf16[1024,2048]{1,0:T(8,128)(2,1)} %get-tuple-element.22.refs_3_.refs_4_, ...), custom_call_target="tpu_custom_call" | custom-call | tf_op jit(solution)/shard_map/second_step/pallas_call | solution.py:446
  60.8 5.6 %all-to-all-start.2 = ((bf16[32,64,128]{2,1,0:T(8,128)(2,1)}), bf16[32,64,128]{2,1,0:T(8,128)(2,1)S(1)}, u32[]{:S(2)}, u32[]{:S(2)}) async-start(bf16[32,64,128]{2,1,0:T(8,128)(2,1)} %get-tuple-element.28), calls=%async_computation.2 | async-start | bytes 1048576 | tf_op jit(solution)/shard_map/all_to_all | solution.py:408
  66.3 0.0 copy-start
  66.4 3.1 %collective-permute-start.2 = (bf16[32,2048]{1,0:T(8,128)(2,1)}, bf16[32,2048]{1,0:T(8,128)(2,1)S(1)}, u32[]{:S(2)}, u32[]{:S(2)}) collective-permute-start(bf16[32,2048]{1,0:T(8,128)(2,1)} %get-tuple-element.16.v_hbm.refs_0_), channel_id=1, source_target_pairs={{0,6},{2,0},{4,2},{6,4},{1,7},{3,1},{5,3},{7,5},{8,14},{10,8},{12,... | collective-permute-start | bytes 393224 | tf_op jit(solution)/shard_map/ppermute | solution.py:464
  69.4 0.6 collective-permute-start.1
  70.1 1.0 collective-permute-start
  71.0 0.0 collective-permute-start.3
  71.1 5.6 %local_product.3.y_hbm = f32[1024,2048]{1,0:T(8,128)} custom-call(s32[12,32]{1,0:T(8,128)} %bitcast.10, bf16[32,2048]{1,0:T(8,128)(2,1)} %get-tuple-element.16.v_hbm.refs_0_, bf16[32,64,640]{2,1,0:T(8,128)(2,1)} %get-tuple-element.26.um_hbm), custom_call_target="tpu_custom_call" | custom-call | flops 167772160 | bytes 20971520 | tf_op jit(solution)/shard_map/local_product/pallas_call | solution.py:434
  76.6 0.0 collective-permute-done.2.refs_3_
  76.7 0.0 collective-permute-done.1.refs_2_
  76.7 0.9 collective-permute-done.refs_1_
  77.5 0.0 collective-permute-start.4
  77.5 0.5 collective-permute-start.5
  78.0 0.0 collective-permute-start.6
  78.1 0.0 collective-permute-done.3.refs_4_
  78.1 0.8 collective-permute-done.4.refs_5_
  78.9 0.2 collective-permute-done.5.refs_6_
  79.1 0.3 collective-permute-done.6.refs_7_
  79.4 2.8 %all-to-all-done.2.recv_ref = bf16[32,64,128]{2,1,0:T(8,128)(2,1)S(1)} async-done(((bf16[32,64,128]{2,1,0:T(8,128)(2,1)}), bf16[32,64,128]{2,1,0:T(8,128)(2,1)S(1)}, u32[]{:S(2)}, u32[]{:S(2)}) %all-to-all-start.2) | async-done | bytes 524320 | tf_op jit(solution)/shard_map/all_to_all | solution.py:408
  82.2 0.0 copy-done
  82.2 3.5 %image.1 = bf16[8,64,256]{2,1,0:T(8,128)(2,1)S(1)} custom-call(s32[8192,128]{1,0:T(8,128)} %get-tuple-element.19.refs_0_.table_hbm, bf16[32,64,128]{2,1,0:T(8,128)(2,1)S(1)} %all-to-all-done.2.recv_ref, f32[1024,2048]{1,0:T(8,128)} %local_product.3.y_hbm, bf16[128,64,256]{2,1,0:T(8,128)(2,1)} %get-tuple-element.23.refs_5_.wd_hbm, ...), custom_call_target="tpu_custom_call" | custom-call | tf_op jit(solution)/shard_map/image/pallas_call | solution.py:469
  85.7 15.9 %all_to_all.25.in_ref = bf16[8,64,256]{2,1,0:T(8,128)(2,1)S(1)} all-to-all(bf16[8,64,256]{2,1,0:T(8,128)(2,1)S(1)} %image.1), channel_id=1, replica_groups=mesh['z'=8,'x'=4,'y'=4,'c'=2] {'z'}, dimensions={0} | all-to-all | bytes 524288 | tf_op jit(solution)/shard_map/all_to_all | solution.py:487
  101.7 9.1 %all_to_all.26.in_ref = bf16[4,64,256]{2,1,0:T(8,128)(2,1)S(1)} all-to-all(bf16[4,64,256]{2,1,0:T(8,128)(2,1)S(1)} %sum_z.1), channel_id=1, replica_groups=mesh['z'=8,'x'=4,'y'=4,'c'=2] {'x'}, dimensions={0} | all-to-all | bytes 262144 | tf_op jit(solution)/shard_map/all_to_all | solution.py:494
  110.8 0.6 sum_x.1
  (1 shorter events, 0.0 us)
Async XLA Ops:
  3.9 28.5 %all-to-all-start = ((bf16[32,64,128]{2,1,0:T(8,128)(2,1)}), bf16[32,64,128]{2,1,0:T(8,128)(2,1)S(1)}, u32[]{:S(2)}, u32[]{:S(2)}) async-start(bf16[32,64,128]{2,1,0:T(8,128)(2,1)} %get-tuple-element.20), calls=%async_computation | async-start | bytes 1048576 | tf_op jit(solution)/shard_map/all_to_all | solution.py:408
  35.8 21.5 %all-to-all-start.1 = ((bf16[32,64,128]{2,1,0:T(8,128)(2,1)}), bf16[32,64,128]{2,1,0:T(8,128)(2,1)S(1)}, u32[]{:S(2)}, u32[]{:S(2)}) async-start(bf16[32,64,128]{2,1,0:T(8,128)(2,1)} %get-tuple-element.24), calls=%async_computation.1 | async-start | bytes 1048576 | tf_op jit(solution)/shard_map/all_to_all | solution.py:408
  60.8 21.4 %all-to-all-start.2 = ((bf16[32,64,128]{2,1,0:T(8,128)(2,1)}), bf16[32,64,128]{2,1,0:T(8,128)(2,1)S(1)}, u32[]{:S(2)}, u32[]{:S(2)}) async-start(bf16[32,64,128]{2,1,0:T(8,128)(2,1)} %get-tuple-element.28), calls=%async_computation.2 | async-start | bytes 1048576 | tf_op jit(solution)/shard_map/all_to_all | solution.py:408
  66.3 15.9 %copy-start = (bf16[32,2048]{1,0:T(8,128)(2,1)S(1)}, bf16[32,2048]{1,0:T(8,128)(2,1)}, u32[]{:S(2)}) copy-start(bf16[32,2048]{1,0:T(8,128)(2,1)} %get-tuple-element.16.v_hbm.refs_0_) | copy-start | bytes 393220
  66.4 10.3 %collective-permute-start.2 = (bf16[32,2048]{1,0:T(8,128)(2,1)}, bf16[32,2048]{1,0:T(8,128)(2,1)S(1)}, u32[]{:S(2)}, u32[]{:S(2)}) collective-permute-start(bf16[32,2048]{1,0:T(8,128)(2,1)} %get-tuple-element.16.v_hbm.refs_0_), channel_id=1, source_target_pairs={{0,6},{2,0},{4,2},{6,4},{1,7},{3,1},{5,3},{7,5},{8,14},{10,8},{12,... | collective-permute-start | bytes 393224 | tf_op jit(solution)/shard_map/ppermute | solution.py:464
  69.4 7.2 %collective-permute-start.1 = (bf16[32,2048]{1,0:T(8,128)(2,1)}, bf16[32,2048]{1,0:T(8,128)(2,1)S(1)}, u32[]{:S(2)}, u32[]{:S(2)}) collective-permute-start(bf16[32,2048]{1,0:T(8,128)(2,1)} %get-tuple-element.16.v_hbm.refs_0_), channel_id=1, source_target_pairs={{0,4},{2,6},{4,0},{6,2},{1,5},{3,7},{5,1},{7,3},{8,12},{10,14},{12... | collective-permute-start | bytes 393224 | tf_op jit(solution)/shard_map/ppermute | solution.py:464
  70.1 7.5 %collective-permute-start = (bf16[32,2048]{1,0:T(8,128)(2,1)}, bf16[32,2048]{1,0:T(8,128)(2,1)S(1)}, u32[]{:S(2)}, u32[]{:S(2)}) collective-permute-start(bf16[32,2048]{1,0:T(8,128)(2,1)} %get-tuple-element.16.v_hbm.refs_0_), channel_id=1, source_target_pairs={{0,2},{2,4},{4,6},{6,0},{1,3},{3,5},{5,7},{7,1},{8,10},{10,12},{12... | collective-permute-start | bytes 393224 | tf_op jit(solution)/shard_map/ppermute | solution.py:464
  71.0 7.0 %collective-permute-start.3 = (bf16[32,2048]{1,0:T(8,128)(2,1)}, bf16[32,2048]{1,0:T(8,128)(2,1)S(1)}, u32[]{:S(2)}, u32[]{:S(2)}) collective-permute-start(bf16[32,2048]{1,0:T(8,128)(2,1)} %get-tuple-element.16.v_hbm.refs_0_), channel_id=1, source_target_pairs={{0,1},{1,0},{2,3},{3,2},{4,5},{5,4},{6,7},{7,6},{8,9},{9,8},{10,11... | collective-permute-start | bytes 393224 | tf_op jit(solution)/shard_map/ppermute | solution.py:468
  77.5 1.3 %collective-permute-start.4 = (bf16[32,2048]{1,0:T(8,128)(2,1)S(1)}, bf16[32,2048]{1,0:T(8,128)(2,1)S(1)}, u32[]{:S(2)}, u32[]{:S(2)}) collective-permute-start(bf16[32,2048]{1,0:T(8,128)(2,1)S(1)} %collective-permute-done.refs_1_), channel_id=1, source_target_pairs={{0,1},{1,0},{2,3},{3,2},{4,5},{5,4},{6,7},{7,6},{8,9},{9,8},{10,11... | collective-permute-start | bytes 393224 | tf_op jit(solution)/shard_map/ppermute | solution.py:468
  77.5 1.5 %collective-permute-start.5 = (bf16[32,2048]{1,0:T(8,128)(2,1)S(1)}, bf16[32,2048]{1,0:T(8,128)(2,1)S(1)}, u32[]{:S(2)}, u32[]{:S(2)}) collective-permute-start(bf16[32,2048]{1,0:T(8,128)(2,1)S(1)} %collective-permute-done.1.refs_2_), channel_id=1, source_target_pairs={{0,1},{1,0},{2,3},{3,2},{4,5},{5,4},{6,7},{7,6},{8,9},{9,8},{10,11... | collective-permute-start | bytes 393224 | tf_op jit(solution)/shard_map/ppermute | solution.py:468
  78.0 1.3 %collective-permute-start.6 = (bf16[32,2048]{1,0:T(8,128)(2,1)S(1)}, bf16[32,2048]{1,0:T(8,128)(2,1)S(1)}, u32[]{:S(2)}, u32[]{:S(2)}) collective-permute-start(bf16[32,2048]{1,0:T(8,128)(2,1)S(1)} %collective-permute-done.2.refs_3_), channel_id=1, source_target_pairs={{0,1},{1,0},{2,3},{3,2},{4,5},{5,4},{6,7},{7,6},{8,9},{9,8},{10,11... | collective-permute-start | bytes 393224 | tf_op jit(solution)/shard_map/ppermute | solution.py:468

commit v5 on v4

--- a/solution.py
+++ b/solution.py
@@ -131,7 +131,7 @@
         copy.wait()
 
 
-def local_sums(src_ref, v_ref, um_ref, um_ready, y_ref, dup_ref, dupb_ref, lhs_ref, mir_ref, acc_ref):
+def local_sums(src_ref, v_ref, um_ref, um_ready, y_ref, dup_ref, dupb_ref, lhs_ref, mir_ref, *acc_refs):
     low = low_half()
     for t in range(RB // 2):
         tile = v_ref[:, 128 * t : 128 * (t + 1)].astype(f32)
@@ -146,29 +146,30 @@
             lhs_ref[i, :, 128 * t : 128 * (t + 1)] = jnp.where(low, dup_ref[j0], dup_ref[j1]).astype(bf16)
         return 0
 
-    lax.fori_loop(0, RB, gather, 0, unroll=4)
+    lax.fori_loop(0, RB, gather, 0, unroll=8)
     um_ready()
     for i in range(RB):
         mir_ref[i] = dot(dupb_ref[i][:, 0:B], um_ref[i], NN)
     for i in range(RB):
-        acc_ref[i, :, 0:B] = dot(lhs_ref[i], um_ref[i], NT)
-        acc_ref[i, :, B:128] = jnp.zeros((MC, B), f32)
+        acc_refs[0][i, :, 0:B] = dot(lhs_ref[i], um_ref[i], NT)
+    for acc_ref in acc_refs[1:]:
+        acc_ref[...] = jnp.zeros(acc_ref.shape, f32)
 
     def scatter(i, _):
         for t, (k0, k1) in enumerate(LOCAL):
             j0 = i if k0 == 0 else jnp.minimum(src_ref[k0, i], RB - 1)
             j1 = jnp.minimum(src_ref[k1, i], RB - 1)
             part = mir_ref[i, :, 128 * t : 128 * (t + 1)]
-            acc_ref[j0] += jnp.where(low, part, 0.0)
-            acc_ref[j1] += jnp.where(low, 0.0, part)
+            acc_refs[2 * (t % 2)][j0] += part
+            acc_refs[2 * (t % 2) + 1][j1] += part
         return 0
 
-    lax.fori_loop(0, RB, scatter, 0, unroll=4)
+    lax.fori_loop(0, RB, scatter, 0, unroll=8)
     for t in range(RB // 2):
-        y_ref[:, 128 * t : 128 * (t + 1)] = folded(acc_ref, t, low)
-
-
-def first_local_kernel(src_hbm, counts_hbm, v_hbm, hb_hbm, um_hbm, y_hbm, src_ref, counts_ref, v_ref, hb_ref, um_ref, y_ref, rows_ref, pair_ref, dup_ref, dupb_ref, lhs_ref, mir_ref, acc_ref, sems, hb_sems):
+        y_ref[:, 128 * t : 128 * (t + 1)] = folded(acc_refs[0], acc_refs[1], t, low) + folded(acc_refs[2], acc_refs[3], t, low)
+
+
+def first_local_kernel(src_hbm, counts_hbm, v_hbm, hb_hbm, um_hbm, y_hbm, src_ref, counts_ref, v_ref, hb_ref, um_ref, y_ref, rows_ref, pair_ref, dup_ref, dupb_ref, lhs_ref, mir_ref, acc0_ref, acc1_ref, acc2_ref, acc3_ref, sems, hb_sems):
     low = low_half()
     start = starter(sems)
     counts = start(counts_hbm, counts_ref)
@@ -206,25 +207,24 @@
     um_out = start(um_ref, um_hbm)
     src.wait()
     vectors.wait()
-    local_sums(src_ref, v_ref, um_ref, lambda: None, y_ref, dup_ref, dupb_ref, lhs_ref, mir_ref, acc_ref)
+    local_sums(src_ref, v_ref, um_ref, lambda: None, y_ref, dup_ref, dupb_ref, lhs_ref, mir_ref, acc0_ref, acc1_ref, acc2_ref, acc3_ref)
     y_out = start(y_ref, y_hbm.at[0:MC, :])
     um_out.wait()
     y_out.wait()
 
 
-def local_kernel(src_hbm, v_hbm, um_hbm, y_hbm, src_ref, v_ref, um_ref, y_ref, dup_ref, dupb_ref, lhs_ref, mir_ref, acc_ref, sems):
+def local_kernel(src_hbm, v_hbm, um_hbm, y_hbm, src_ref, v_ref, um_ref, y_ref, dup_ref, dupb_ref, lhs_ref, mir_ref, acc0_ref, acc1_ref, acc2_ref, acc3_ref, sems):
     start = starter(sems)
     vectors = start(v_hbm.at[0:MC, :], v_ref)
     src = start(src_hbm, src_ref)
     um = start(um_hbm, um_ref)
     vectors.wait()
     src.wait()
-    local_sums(src_ref, v_ref, um_ref, um.wait, y_ref, dup_ref, dupb_ref, lhs_ref, mir_ref, acc_ref)
+    local_sums(src_ref, v_ref, um_ref, um.wait, y_ref, dup_ref, dupb_ref, lhs_ref, mir_ref, acc0_ref, acc1_ref, acc2_ref, acc3_ref)
     start(y_ref, y_hbm.at[0:MC, :]).wait()
 
 
-def remote_sum(table_ref, recv_ref, wd_ref, wd_ready, lhs_ref, acc_ref):
-    low = low_half()
+def remote_sum(table_ref, recv_ref, wd_ref, wd_ready, lhs_ref, low_ref, high_ref):
     lane = lax.broadcasted_iota(jnp.int32, (MC, 128), 1) // B
 
     def gather(i, _):
@@ -234,27 +234,29 @@
             lhs_ref[i, :, 128 * (k - 1) : 128 * k] = jnp.where(lane == s % 2, tile, 0.0).astype(bf16)
         return 0
 
-    lax.fori_loop(0, RB, gather, 0, unroll=4)
+    lax.fori_loop(0, RB, gather, 0, unroll=8)
     wd_ready()
     for i in range(RB):
-        acc_ref[i, :, 0:B] = dot(lhs_ref[i], wd_ref[i], NT)
-        acc_ref[i, :, B:128] = jnp.zeros((MC, B), f32)
+        low_ref[i, :, 0:B] = dot(lhs_ref[i], wd_ref[i], NT)
+    high_ref[...] = jnp.zeros(high_ref.shape, f32)
 
     def scatter(q, _):
         tile = recv_ref[q, MC : 2 * MC, :].astype(f32)
-        acc_ref[table_ref[K, 2 * q]] += jnp.where(low, tile, 0.0)
-        acc_ref[table_ref[K, 2 * q + 1]] += jnp.where(low, 0.0, tile)
+        low_ref[table_ref[K, 2 * q]] += tile
+        high_ref[table_ref[K, 2 * q + 1]] += tile
         return 0
 
-    lax.fori_loop(0, PEERS, scatter, 0, unroll=4)
-
-
-def folded(acc_ref, t, low):
-    one, two = acc_ref[2 * t], acc_ref[2 * t + 1]
-    return jnp.where(low, one + pltpu.roll(one, B, 1), two + pltpu.roll(two, B, 1))
-
-
-def step_kernel(second, table_hbm, recv_ref, y_hbm, v_hbm, prev_hbm, wd_hbm, out_hbm, msg_hbm, table_ref, y_ref, v_ref, prev_ref, wd_ref, out_ref, msg_ref, lhs_ref, acc_ref, dup_ref, prod_ref, inv_ref, sems):
+    lax.fori_loop(0, PEERS, scatter, 0, unroll=8)
+
+
+def folded(low_ref, high_ref, t, low):
+    one, two = 2 * t, 2 * t + 1
+    return jnp.where(
+        low, low_ref[one] + pltpu.roll(high_ref[one], B, 1), pltpu.roll(low_ref[two], B, 1) + high_ref[two]
+    )
+
+
+def step_kernel(second, table_hbm, recv_ref, y_hbm, v_hbm, prev_hbm, wd_hbm, out_hbm, msg_hbm, table_ref, y_ref, v_ref, prev_ref, wd_ref, out_ref, msg_ref, lhs_ref, low_ref, high_ref, dup_ref, prod_ref, inv_ref, sems):
     low = low_half()
     start = starter(sems)
     table = start(table_hbm.at[0:16, :], table_ref)
@@ -264,12 +266,12 @@
         terms.append(start(prev_hbm.at[0:MC, :], prev_ref))
     table.wait()
     invert_slots(inv_ref, table_ref)
-    remote_sum(table_ref, recv_ref, wd_ref, wd.wait, lhs_ref, acc_ref)
+    remote_sum(table_ref, recv_ref, wd_ref, wd.wait, lhs_ref, low_ref, high_ref)
     for copy in terms:
         copy.wait()
     for t in range(RB // 2):
         lanes = slice(128 * t, 128 * (t + 1))
-        image = folded(acc_ref, t, low) + y_ref[:, lanes]
+        image = folded(low_ref, high_ref, t, low) + y_ref[:, lanes]
         if second:
             tile = 2.0 * (image - center_value * prev_ref[:, lanes].astype(f32)) / half_width - v_ref[:, lanes].astype(f32)
         else:
@@ -290,7 +292,7 @@
 
 def image_kernel(table_hbm, recv_ref, y_hbm, wd_hbm, *refs):
     own, other = refs[0:NY], refs[NY : 2 * NY]
-    out_ref, table_ref, y_ref, wd_ref, lhs_ref, acc_ref, stack_ref, all_ref, sems = refs[2 * NY :]
+    out_ref, table_ref, y_ref, wd_ref, lhs_ref, low_ref, high_ref, stack_ref, all_ref, sems = refs[2 * NY :]
     low = low_half()
     start = starter(sems)
     table = start(table_hbm.at[0:16, :], table_ref)
@@ -303,11 +305,11 @@
         for block, core in ((own[d], c), (other[d], 1 - c)):
             moves.append(start(block, all_ref.at[pl.ds(pl.multiple_of((from_y + core) * MC, MC), MC), :]))
     table.wait()
-    remote_sum(table_ref, recv_ref, wd_ref, wd.wait, lhs_ref, acc_ref)
+    remote_sum(table_ref, recv_ref, wd_ref, wd.wait, lhs_ref, low_ref, high_ref)
     y_sum.wait()
     for t in range(RB // 2):
         lanes = slice(128 * t, 128 * (t + 1))
-        stack_ref[MC : 2 * MC, lanes] = (folded(acc_ref, t, low) + y_ref[:, lanes]).astype(bf16)
+        stack_ref[MC : 2 * MC, lanes] = (folded(low_ref, high_ref, t, low) + y_ref[:, lanes]).astype(bf16)
     for copy in moves:
         copy.wait()
     part = dot(stack_ref[...], all_ref[...], NT).astype(bf16)
@@ -408,7 +410,7 @@
         return lax.all_to_all(message, row_axes, split_axis=0, concat_axis=0, tiled=True)
 
     received = exchange(message)
-    local_scratch = [dup, dupb, lhs, mir, acc]
+    local_scratch = [dup, dupb, lhs, mir, acc, acc, acc, acc]
     um, local = pl.pallas_call(
         first_local_kernel,
         out_shape=(um_shape, shape((ROOM, width), f32)),
@@ -448,7 +450,7 @@
             out_shape=(shape((cols if second else ROOM, width), bf16), msg_shape),
             in_specs=[HBM, VM] + [HBM] * 4,
             out_specs=(HBM, HBM),
-            scratch_shapes=[table_scratch, vec_sum, vec, vec, wd_scratch, vec, msg, lhs_remote, acc, dup, prod, inv]
+            scratch_shapes=[table_scratch, vec_sum, vec, vec, wd_scratch, vec, msg, lhs_remote, acc, acc, dup, prod, inv]
             + [semaphores(9)],
             compiler_params=limit(51.6),
             name="second_step" if second else "first_step",
@@ -477,6 +479,7 @@
             wd_scratch,
             lhs_remote,
             acc,
+            acc,
             pltpu.VMEM((2 * MC, width), bf16),
             pltpu.VMEM((NY * NC * MC, width), bf16),
             semaphores(5 + 2 * NY),

time: 113 us -> 112 us (level)
  Pallas kernels: 33.6 us -> 31.1 us
  waiting for transfers between devices: 24.1 us -> 26.2 us
    all_to_all x3, waiting for transfers between devices: 21.9 us -> 23.3 us  [exchange(): lax.all_to_all(message, row_axes, split_axis=0, concat_axis=0, tiled=True)]
    pallas_call x2, Pallas kernels: 11.2 us -> 9.88 us  [local_part(): pl.pallas_call(local_kernel, out_shape=shape((ROOM, width), f32), in_spec...]
  transfers between devices with their start and end apart: 10 -> 10, of which waited for: 7 -> 8; matrix products, arithmetic and copies ran while one was open for 0% -> 0% of each run, Pallas kernels for 17% -> 15%
where the time goes in v5:
time: 112 us; the launch traced here: 111 us
  Pallas kernels  31.1 us (28%)
  starting transfers between devices  28 us (25%)
  waiting for transfers between devices  26.2 us (23%)
  blocking collectives  25 us (22%)
    all_to_all x3, waiting for transfers between devices, exchange(): lax.all_to_all(message, row_axes, split_axis=0, concat_axis=0, tiled=True)  23.3 us
    all_to_all x3, starting transfers between devices, exchange(): lax.all_to_all(message, row_axes, split_axis=0, concat_axis=0, tiled=True)  22.8 us
    all_to_all x1, blocking collectives, on_device(): part = lax.all_to_all(part, 'z', split_axis=0, concat_axis=0, tiled=True)  15.9 us
    pallas_call x2, Pallas kernels, local_part(): pl.pallas_call(local_kernel, out_shape=shape((ROOM, width), f32), in_spec...  9.88 us
    all_to_all x1, blocking collectives, on_device(): part = lax.all_to_all(part, 'x', split_axis=0, concat_axis=0, tiled=True)  9.12 us
    pallas_call x1, Pallas kernels, on_device(): pl.pallas_call(first_local_kernel, out_shape=(um_shape, shape((ROOM, widt...  7.26 us
    pallas_call x2, Pallas kernels, next_step(): pl.pallas_call(lambda *refs: step_kernel(second, *refs), out_shape=(shape...  6.66 us
    ppermute x3, starting transfers between devices, on_device(): lax.ppermute(filtered, 'y', [(y, (y + d) % NY) for y in range(NY)])  4.69 us
  transfers between devices with their start and end apart: 10, of which 8 were waited for; matrix products, arithmetic and copies ran while one was open for 0% of the time, Pallas kernels for 15%

profile of v5, /device:TPU:2, one launch (start us, length us, event | category | flops | bytes accessed | tf_op | source)
XLA Modules:
  0.0 111.1 jit_solution(10159538668786834524)
XLA Ops:
  0.6 3.2 %first_message.1 = (bf16[32,64,128]{2,1,0:T(8,128)(2,1)}, bf16[128,64,256]{2,1,0:T(8,128)(2,1)}, s32[8192,128]{1,0:T(8,128)}, bf16[1024,2048]{1,0:T(8,128)(2,1)}) custom-call(s32[12,32]{1,0:T(8,128)} %bitcast.7, s32[1,64]{1,0:T(1,128)} %bitcast.11, bf16[32,2048]{1,0:T(8,128)(2,1)} %v_hbm.3, bf16[12,32,4096]{2,1,0:T(8,128)(2,1)} %bitcast.5), custom_call_target="tpu_custom_call" | custom-call | tf_op jit(solution)/shard_map/first_message/pallas_call | solution.py:378
  3.9 11.6 %all-to-all-start = ((bf16[32,64,128]{2,1,0:T(8,128)(2,1)}), bf16[32,64,128]{2,1,0:T(8,128)(2,1)S(1)}, u32[]{:S(2)}, u32[]{:S(2)}) async-start(bf16[32,64,128]{2,1,0:T(8,128)(2,1)} %get-tuple-element.20), calls=%async_computation | async-start | bytes 1048576 | tf_op jit(solution)/shard_map/all_to_all | solution.py:410
  15.5 7.3 %first_local.1 = (bf16[32,64,640]{2,1,0:T(8,128)(2,1)}, f32[1024,2048]{1,0:T(8,128)}) custom-call(s32[12,32]{1,0:T(8,128)} %bitcast.8, s32[32]{0:T(128)} %counts_hbm.1, bf16[32,2048]{1,0:T(8,128)(2,1)} %v_hbm.3, bf16[12,32,4096]{2,1,0:T(8,128)(2,1)} %bitcast.6), custom_call_target="tpu_custom_call" | custom-call | tf_op jit(solution)/shard_map/first_local/pallas_call | solution.py:414
  22.8 9.6 %all-to-all-done.refs_1_ = bf16[32,64,128]{2,1,0:T(8,128)(2,1)S(1)} async-done(((bf16[32,64,128]{2,1,0:T(8,128)(2,1)}), bf16[32,64,128]{2,1,0:T(8,128)(2,1)S(1)}, u32[]{:S(2)}, u32[]{:S(2)}) %all-to-all-start) | async-done | bytes 524320 | tf_op jit(solution)/shard_map/all_to_all | solution.py:410
  32.3 3.3 %first_step.1 = (bf16[1024,2048]{1,0:T(8,128)(2,1)}, bf16[32,64,128]{2,1,0:T(8,128)(2,1)}) custom-call(s32[8192,128]{1,0:T(8,128)} %get-tuple-element.19.refs_0_.table_hbm, bf16[32,64,128]{2,1,0:T(8,128)(2,1)S(1)} %all-to-all-done.refs_1_, f32[1024,2048]{1,0:T(8,128)} %get-tuple-element.21.refs_2_, bf16[1024,2048]{1,0:T(8,128)(2,1)} %get-tuple-element.22.refs_3_.refs_4_, ...), custom_call_target="tpu_custom_call" | custom-call | tf_op jit(solution)/shard_map/first_step/pallas_call | solution.py:448
  35.7 5.6 %all-to-all-start.1 = ((bf16[32,64,128]{2,1,0:T(8,128)(2,1)}), bf16[32,64,128]{2,1,0:T(8,128)(2,1)S(1)}, u32[]{:S(2)}, u32[]{:S(2)}) async-start(bf16[32,64,128]{2,1,0:T(8,128)(2,1)} %get-tuple-element.24), calls=%async_computation.1 | async-start | bytes 1048576 | tf_op jit(solution)/shard_map/all_to_all | solution.py:410
  41.2 4.9 %local_product.2.refs_2_ = f32[1024,2048]{1,0:T(8,128)} custom-call(s32[12,32]{1,0:T(8,128)} %bitcast.9, bf16[1024,2048]{1,0:T(8,128)(2,1)} %get-tuple-element.25.v_hbm.refs_4_, bf16[32,64,640]{2,1,0:T(8,128)(2,1)} %get-tuple-element.26.um_hbm), custom_call_target="tpu_custom_call" | custom-call | flops 167772160 | bytes 20971520 | tf_op jit(solution)/shard_map/local_product/pallas_call | solution.py:436
  46.2 11.0 %all-to-all-done.1.refs_1_ = bf16[32,64,128]{2,1,0:T(8,128)(2,1)S(1)} async-done(((bf16[32,64,128]{2,1,0:T(8,128)(2,1)}), bf16[32,64,128]{2,1,0:T(8,128)(2,1)S(1)}, u32[]{:S(2)}, u32[]{:S(2)}) %all-to-all-start.1) | async-done | bytes 524320 | tf_op jit(solution)/shard_map/all_to_all | solution.py:410
  57.2 3.3 %second_step.1 = (bf16[32,2048]{1,0:T(8,128)(2,1)}, bf16[32,64,128]{2,1,0:T(8,128)(2,1)}) custom-call(s32[8192,128]{1,0:T(8,128)} %get-tuple-element.19.refs_0_.table_hbm, bf16[32,64,128]{2,1,0:T(8,128)(2,1)S(1)} %all-to-all-done.1.refs_1_, f32[1024,2048]{1,0:T(8,128)} %local_product.2.refs_2_, bf16[1024,2048]{1,0:T(8,128)(2,1)} %get-tuple-element.22.refs_3_.refs_4_, ...), custom_call_target="tpu_custom_call" | custom-call | tf_op jit(solution)/shard_map/second_step/pallas_call | solution.py:448
  60.5 5.6 %all-to-all-start.2 = ((bf16[32,64,128]{2,1,0:T(8,128)(2,1)}), bf16[32,64,128]{2,1,0:T(8,128)(2,1)S(1)}, u32[]{:S(2)}, u32[]{:S(2)}) async-start(bf16[32,64,128]{2,1,0:T(8,128)(2,1)} %get-tuple-element.28), calls=%async_computation.2 | async-start | bytes 1048576 | tf_op jit(solution)/shard_map/all_to_all | solution.py:410
  66.1 0.0 copy-start
  66.1 3.1 %collective-permute-start.2 = (bf16[32,2048]{1,0:T(8,128)(2,1)}, bf16[32,2048]{1,0:T(8,128)(2,1)S(1)}, u32[]{:S(2)}, u32[]{:S(2)}) collective-permute-start(bf16[32,2048]{1,0:T(8,128)(2,1)} %get-tuple-element.16.v_hbm.refs_0_), channel_id=1, source_target_pairs={{0,6},{2,0},{4,2},{6,4},{1,7},{3,1},{5,3},{7,5},{8,14},{10,8},{12,... | collective-permute-start | bytes 393224 | tf_op jit(solution)/shard_map/ppermute | solution.py:466
  69.2 0.6 collective-permute-start.1
  69.8 1.0 collective-permute-start
  70.8 0.0 collective-permute-start.3
  70.8 4.9 %local_product.3.y_hbm = f32[1024,2048]{1,0:T(8,128)} custom-call(s32[12,32]{1,0:T(8,128)} %bitcast.10, bf16[32,2048]{1,0:T(8,128)(2,1)} %get-tuple-element.16.v_hbm.refs_0_, bf16[32,64,640]{2,1,0:T(8,128)(2,1)} %get-tuple-element.26.um_hbm), custom_call_target="tpu_custom_call" | custom-call | flops 167772160 | bytes 20971520 | tf_op jit(solution)/shard_map/local_product/pallas_call | solution.py:436
  75.7 0.0 collective-permute-done.2.refs_3_
  75.8 0.2 collective-permute-done.1.refs_2_
  76.0 1.3 %collective-permute-done.refs_1_ = bf16[32,2048]{1,0:T(8,128)(2,1)S(1)} collective-permute-done((bf16[32,2048]{1,0:T(8,128)(2,1)}, bf16[32,2048]{1,0:T(8,128)(2,1)S(1)}, u32[]{:S(2)}, u32[]{:S(2)}) %collective-permute-start) | collective-permute-done | bytes 131104 | tf_op jit(solution)/shard_map/ppermute | solution.py:466
  77.3 0.0 collective-permute-start.4
  77.3 0.5 collective-permute-start.5
  77.8 0.0 collective-permute-start.6
  77.8 0.0 collective-permute-done.3.refs_4_
  77.8 0.8 collective-permute-done.4.refs_5_
  78.6 0.2 collective-permute-done.5.refs_6_
  78.8 0.3 collective-permute-done.6.refs_7_
  79.1 2.8 %all-to-all-done.2.recv_ref = bf16[32,64,128]{2,1,0:T(8,128)(2,1)S(1)} async-done(((bf16[32,64,128]{2,1,0:T(8,128)(2,1)}), bf16[32,64,128]{2,1,0:T(8,128)(2,1)S(1)}, u32[]{:S(2)}, u32[]{:S(2)}) %all-to-all-start.2) | async-done | bytes 524320 | tf_op jit(solution)/shard_map/all_to_all | solution.py:410
  81.9 0.0 copy-done
  81.9 3.4 %image.1 = bf16[8,64,256]{2,1,0:T(8,128)(2,1)S(1)} custom-call(s32[8192,128]{1,0:T(8,128)} %get-tuple-element.19.refs_0_.table_hbm, bf16[32,64,128]{2,1,0:T(8,128)(2,1)S(1)} %all-to-all-done.2.recv_ref, f32[1024,2048]{1,0:T(8,128)} %local_product.3.y_hbm, bf16[128,64,256]{2,1,0:T(8,128)(2,1)} %get-tuple-element.23.refs_5_.wd_hbm, ...), custom_call_target="tpu_custom_call" | custom-call | tf_op jit(solution)/shard_map/image/pallas_call | solution.py:471
  85.4 15.9 %all_to_all.25.in_ref = bf16[8,64,256]{2,1,0:T(8,128)(2,1)S(1)} all-to-all(bf16[8,64,256]{2,1,0:T(8,128)(2,1)S(1)} %image.1), channel_id=1, replica_groups=mesh['z'=8,'x'=4,'y'=4,'c'=2] {'z'}, dimensions={0} | all-to-all | bytes 524288 | tf_op jit(solution)/shard_map/all_to_all | solution.py:490
  101.3 9.1 %all_to_all.26.in_ref = bf16[4,64,256]{2,1,0:T(8,128)(2,1)S(1)} all-to-all(bf16[4,64,256]{2,1,0:T(8,128)(2,1)S(1)} %sum_z.1), channel_id=1, replica_groups=mesh['z'=8,'x'=4,'y'=4,'c'=2] {'x'}, dimensions={0} | all-to-all | bytes 262144 | tf_op jit(solution)/shard_map/all_to_all | solution.py:497
  110.4 0.6 sum_x.1
  (1 shorter events, 0.0 us)
Async XLA Ops:
  3.9 28.5 %all-to-all-start = ((bf16[32,64,128]{2,1,0:T(8,128)(2,1)}), bf16[32,64,128]{2,1,0:T(8,128)(2,1)S(1)}, u32[]{:S(2)}, u32[]{:S(2)}) async-start(bf16[32,64,128]{2,1,0:T(8,128)(2,1)} %get-tuple-element.20), calls=%async_computation | async-start | bytes 1048576 | tf_op jit(solution)/shard_map/all_to_all | solution.py:410
  35.7 21.5 %all-to-all-start.1 = ((bf16[32,64,128]{2,1,0:T(8,128)(2,1)}), bf16[32,64,128]{2,1,0:T(8,128)(2,1)S(1)}, u32[]{:S(2)}, u32[]{:S(2)}) async-start(bf16[32,64,128]{2,1,0:T(8,128)(2,1)} %get-tuple-element.24), calls=%async_computation.1 | async-start | bytes 1048576 | tf_op jit(solution)/shard_map/all_to_all | solution.py:410
  60.5 21.4 %all-to-all-start.2 = ((bf16[32,64,128]{2,1,0:T(8,128)(2,1)}), bf16[32,64,128]{2,1,0:T(8,128)(2,1)S(1)}, u32[]{:S(2)}, u32[]{:S(2)}) async-start(bf16[32,64,128]{2,1,0:T(8,128)(2,1)} %get-tuple-element.28), calls=%async_computation.2 | async-start | bytes 1048576 | tf_op jit(solution)/shard_map/all_to_all | solution.py:410
  66.1 15.9 %copy-start = (bf16[32,2048]{1,0:T(8,128)(2,1)S(1)}, bf16[32,2048]{1,0:T(8,128)(2,1)}, u32[]{:S(2)}) copy-start(bf16[32,2048]{1,0:T(8,128)(2,1)} %get-tuple-element.16.v_hbm.refs_0_) | copy-start | bytes 393220
  66.1 9.6 %collective-permute-start.2 = (bf16[32,2048]{1,0:T(8,128)(2,1)}, bf16[32,2048]{1,0:T(8,128)(2,1)S(1)}, u32[]{:S(2)}, u32[]{:S(2)}) collective-permute-start(bf16[32,2048]{1,0:T(8,128)(2,1)} %get-tuple-element.16.v_hbm.refs_0_), channel_id=1, source_target_pairs={{0,6},{2,0},{4,2},{6,4},{1,7},{3,1},{5,3},{7,5},{8,14},{10,8},{12,... | collective-permute-start | bytes 393224 | tf_op jit(solution)/shard_map/ppermute | solution.py:466
  69.2 6.8 %collective-permute-start.1 = (bf16[32,2048]{1,0:T(8,128)(2,1)}, bf16[32,2048]{1,0:T(8,128)(2,1)S(1)}, u32[]{:S(2)}, u32[]{:S(2)}) collective-permute-start(bf16[32,2048]{1,0:T(8,128)(2,1)} %get-tuple-element.16.v_hbm.refs_0_), channel_id=1, source_target_pairs={{0,4},{2,6},{4,0},{6,2},{1,5},{3,7},{5,1},{7,3},{8,12},{10,14},{12... | collective-permute-start | bytes 393224 | tf_op jit(solution)/shard_map/ppermute | solution.py:466
  69.8 7.5 %collective-permute-start = (bf16[32,2048]{1,0:T(8,128)(2,1)}, bf16[32,2048]{1,0:T(8,128)(2,1)S(1)}, u32[]{:S(2)}, u32[]{:S(2)}) collective-permute-start(bf16[32,2048]{1,0:T(8,128)(2,1)} %get-tuple-element.16.v_hbm.refs_0_), channel_id=1, source_target_pairs={{0,2},{2,4},{4,6},{6,0},{1,3},{3,5},{5,7},{7,1},{8,10},{10,12},{12... | collective-permute-start | bytes 393224 | tf_op jit(solution)/shard_map/ppermute | solution.py:466
  70.8 7.0 %collective-permute-start.3 = (bf16[32,2048]{1,0:T(8,128)(2,1)}, bf16[32,2048]{1,0:T(8,128)(2,1)S(1)}, u32[]{:S(2)}, u32[]{:S(2)}) collective-permute-start(bf16[32,2048]{1,0:T(8,128)(2,1)} %get-tuple-element.16.v_hbm.refs_0_), channel_id=1, source_target_pairs={{0,1},{1,0},{2,3},{3,2},{4,5},{5,4},{6,7},{7,6},{8,9},{9,8},{10,11... | collective-permute-start | bytes 393224 | tf_op jit(solution)/shard_map/ppermute | solution.py:470
  77.3 1.3 %collective-permute-start.4 = (bf16[32,2048]{1,0:T(8,128)(2,1)S(1)}, bf16[32,2048]{1,0:T(8,128)(2,1)S(1)}, u32[]{:S(2)}, u32[]{:S(2)}) collective-permute-start(bf16[32,2048]{1,0:T(8,128)(2,1)S(1)} %collective-permute-done.refs_1_), channel_id=1, source_target_pairs={{0,1},{1,0},{2,3},{3,2},{4,5},{5,4},{6,7},{7,6},{8,9},{9,8},{10,11... | collective-permute-start | bytes 393224 | tf_op jit(solution)/shard_map/ppermute | solution.py:470
  77.3 1.5 %collective-permute-start.5 = (bf16[32,2048]{1,0:T(8,128)(2,1)S(1)}, bf16[32,2048]{1,0:T(8,128)(2,1)S(1)}, u32[]{:S(2)}, u32[]{:S(2)}) collective-permute-start(bf16[32,2048]{1,0:T(8,128)(2,1)S(1)} %collective-permute-done.1.refs_2_), channel_id=1, source_target_pairs={{0,1},{1,0},{2,3},{3,2},{4,5},{5,4},{6,7},{7,6},{8,9},{9,8},{10,11... | collective-permute-start | bytes 393224 | tf_op jit(solution)/shard_map/ppermute | solution.py:470
  77.8 1.3 %collective-permute-start.6 = (bf16[32,2048]{1,0:T(8,128)(2,1)S(1)}, bf16[32,2048]{1,0:T(8,128)(2,1)S(1)}, u32[]{:S(2)}, u32[]{:S(2)}) collective-permute-start(bf16[32,2048]{1,0:T(8,128)(2,1)S(1)} %collective-permute-done.2.refs_3_), channel_id=1, source_target_pairs={{0,1},{1,0},{2,3},{3,2},{4,5},{5,4},{6,7},{7,6},{8,9},{9,8},{10,11... | collective-permute-start | bytes 393224 | tf_op jit(solution)/shard_map/ppermute | solution.py:470

commit v6 on v5

--- a/solution.py
+++ b/solution.py
@@ -94,27 +94,21 @@
 def first_message_kernel(src_hbm, send_hbm, v_hbm, hb_hbm, msg_hbm, wd_hbm, table_hbm, keep_hbm, src_ref, send_ref, srcv_ref, sendv_ref, table_ref, v_ref, hb_ref, msg_ref, wd_ref, rows_ref, pair_ref, dup_ref, prod_ref, inv_ref, sems):
     low = low_half()
     start = starter(sems)
-    blocks = [start(hb_hbm.at[k], hb_ref.at[k - 1]) for k in (1, 2)]
     vectors = start(v_hbm, v_ref)
     send = start(send_hbm, send_ref)
     src = start(src_hbm, src_ref)
+    blocks = [start(hb_hbm.at[k], hb_ref.at[k - 1]) for k in (1, 2)]
     tables = [start(src_hbm, srcv_ref), start(send_hbm, sendv_ref)]
     vectors.wait()
-    keep_out = start(v_ref, keep_hbm.at[0:MC, :])
     for t in range(RB // 2):
         tile = v_ref[:, 128 * t : 128 * (t + 1)].astype(f32)
         dup_ref[2 * t], dup_ref[2 * t + 1] = duplicate(tile, low)
     send.wait()
     emit_picks(msg_ref, dup_ref, lambda c: send_ref[0, c], low)
     picks_out = start(msg_ref.at[:, 0:MC, :], msg_hbm.at[:, 0:MC, :])
-    for copy in tables:
-        copy.wait()
-    table_ref[...] = jnp.zeros(table_ref.shape, jnp.int32)
-    table_ref[0:K, 0:RB] = srcv_ref[...]
-    table_ref[K : K + 1, 0 : 2 * PEERS] = sendv_ref[...]
-    table_out = start(table_ref, table_hbm.at[0:16, :])
     src.wait()
     invert_slots(inv_ref, src_ref)
+    weights_out = []
     for k in (1, 2):
         blocks[k - 1].wait()
         unpack_rows(rows_ref.at[k - 1], hb_ref.at[k - 1])
@@ -123,11 +117,19 @@
             pair = pair_ref.at[k - 1, i]
             store_pair(pair, block, block, low)
             wd_ref[i, :, 128 * (k - 1) : 128 * k] = pair[...].astype(bf16)
-    weights_out = start(wd_ref, wd_hbm.at[0:RB])
+        half = slice(128 * (k - 1), 128 * k)
+        weights_out.append(start(wd_ref.at[:, :, half], wd_hbm.at[0:RB, :, half]))
+    keep_out = start(v_ref, keep_hbm.at[0:MC, :])
+    for copy in tables:
+        copy.wait()
+    table_ref[...] = jnp.zeros(table_ref.shape, jnp.int32)
+    table_ref[0:K, 0:RB] = srcv_ref[...]
+    table_ref[K : K + 1, 0 : 2 * PEERS] = sendv_ref[...]
+    table_out = start(table_ref, table_hbm.at[0:16, :])
     mirror_products(dup_ref, wd_ref, prod_ref)
     emit_mirror(msg_ref, prod_ref, inv_ref, low)
     mirror_out = start(msg_ref.at[:, MC : 2 * MC, :], msg_hbm.at[:, MC : 2 * MC, :])
-    for copy in (keep_out, table_out, picks_out, weights_out, mirror_out):
+    for copy in (keep_out, table_out, picks_out, *weights_out, mirror_out):
         copy.wait()
 
 
@@ -400,7 +402,7 @@
             dup,
             prod,
             inv,
-            semaphores(12),
+            semaphores(13),
         ],
         compiler_params=limit(60),
         name="first_message",

time: 112 us -> 112 us (level)
  no operation moved by 1% of the time
where the time goes in v6:
time: 112 us; the launch traced here: 111 us
  Pallas kernels  30.9 us (28%)
  starting transfers between devices  28 us (25%)
  waiting for transfers between devices  26.2 us (23%)
  blocking collectives  25 us (22%)
    all_to_all x3, waiting for transfers between devices, exchange(): lax.all_to_all(message, row_axes, split_axis=0, concat_axis=0, tiled=True)  23.3 us
    all_to_all x3, starting transfers between devices, exchange(): lax.all_to_all(message, row_axes, split_axis=0, concat_axis=0, tiled=True)  22.8 us
    all_to_all x1, blocking collectives, on_device(): part = lax.all_to_all(part, 'z', split_axis=0, concat_axis=0, tiled=True)  15.9 us
    pallas_call x2, Pallas kernels, local_part(): pl.pallas_call(local_kernel, out_shape=shape((ROOM, width), f32), in_spec...  9.88 us
    all_to_all x1, blocking collectives, on_device(): part = lax.all_to_all(part, 'x', split_axis=0, concat_axis=0, tiled=True)  9.12 us
    pallas_call x1, Pallas kernels, on_device(): pl.pallas_call(first_local_kernel, out_shape=(um_shape, shape((ROOM, widt...  7.27 us
    pallas_call x2, Pallas kernels, next_step(): pl.pallas_call(lambda *refs: step_kernel(second, *refs), out_shape=(shape...  6.66 us
    ppermute x3, starting transfers between devices, on_device(): lax.ppermute(filtered, 'y', [(y, (y + d) % NY) for y in range(NY)])  4.69 us
  transfers between devices with their start and end apart: 10, of which 8 were waited for; matrix products, arithmetic and copies ran while one was open for 0% of the time, Pallas kernels for 15%

profile of v6, /device:TPU:2, one launch (start us, length us, event | category | flops | bytes accessed | tf_op | source)
XLA Modules:
  0.0 110.8 jit_solution(5064333909871530936)
XLA Ops:
  0.6 3.0 %first_message.1 = (bf16[32,64,128]{2,1,0:T(8,128)(2,1)}, bf16[128,64,256]{2,1,0:T(8,128)(2,1)}, s32[8192,128]{1,0:T(8,128)}, bf16[1024,2048]{1,0:T(8,128)(2,1)}) custom-call(s32[12,32]{1,0:T(8,128)} %bitcast.7, s32[1,64]{1,0:T(1,128)} %bitcast.11, bf16[32,2048]{1,0:T(8,128)(2,1)} %v_hbm.3, bf16[12,32,4096]{2,1,0:T(8,128)(2,1)} %bitcast.5), custom_call_target="tpu_custom_call" | custom-call | tf_op jit(solution)/shard_map/first_message/pallas_call | solution.py:380
  3.6 11.6 %all-to-all-start = ((bf16[32,64,128]{2,1,0:T(8,128)(2,1)}), bf16[32,64,128]{2,1,0:T(8,128)(2,1)S(1)}, u32[]{:S(2)}, u32[]{:S(2)}) async-start(bf16[32,64,128]{2,1,0:T(8,128)(2,1)} %get-tuple-element.20), calls=%async_computation | async-start | bytes 1048576 | tf_op jit(solution)/shard_map/all_to_all | solution.py:412
  15.2 7.3 %first_local.1 = (bf16[32,64,640]{2,1,0:T(8,128)(2,1)}, f32[1024,2048]{1,0:T(8,128)}) custom-call(s32[12,32]{1,0:T(8,128)} %bitcast.8, s32[32]{0:T(128)} %counts_hbm.1, bf16[32,2048]{1,0:T(8,128)(2,1)} %v_hbm.3, bf16[12,32,4096]{2,1,0:T(8,128)(2,1)} %bitcast.6), custom_call_target="tpu_custom_call" | custom-call | tf_op jit(solution)/shard_map/first_local/pallas_call | solution.py:416
  22.5 9.6 %all-to-all-done.refs_1_ = bf16[32,64,128]{2,1,0:T(8,128)(2,1)S(1)} async-done(((bf16[32,64,128]{2,1,0:T(8,128)(2,1)}), bf16[32,64,128]{2,1,0:T(8,128)(2,1)S(1)}, u32[]{:S(2)}, u32[]{:S(2)}) %all-to-all-start) | async-done | bytes 524320 | tf_op jit(solution)/shard_map/all_to_all | solution.py:412
  32.1 3.3 %first_step.1 = (bf16[1024,2048]{1,0:T(8,128)(2,1)}, bf16[32,64,128]{2,1,0:T(8,128)(2,1)}) custom-call(s32[8192,128]{1,0:T(8,128)} %get-tuple-element.19.refs_0_.table_hbm, bf16[32,64,128]{2,1,0:T(8,128)(2,1)S(1)} %all-to-all-done.refs_1_, f32[1024,2048]{1,0:T(8,128)} %get-tuple-element.21.refs_2_, bf16[1024,2048]{1,0:T(8,128)(2,1)} %get-tuple-element.22.refs_3_.refs_4_, ...), custom_call_target="tpu_custom_call" | custom-call | tf_op jit(solution)/shard_map/first_step/pallas_call | solution.py:450
  35.4 5.6 %all-to-all-start.1 = ((bf16[32,64,128]{2,1,0:T(8,128)(2,1)}), bf16[32,64,128]{2,1,0:T(8,128)(2,1)S(1)}, u32[]{:S(2)}, u32[]{:S(2)}) async-start(bf16[32,64,128]{2,1,0:T(8,128)(2,1)} %get-tuple-element.24), calls=%async_computation.1 | async-start | bytes 1048576 | tf_op jit(solution)/shard_map/all_to_all | solution.py:412
  41.0 4.9 %local_product.2.refs_2_ = f32[1024,2048]{1,0:T(8,128)} custom-call(s32[12,32]{1,0:T(8,128)} %bitcast.9, bf16[1024,2048]{1,0:T(8,128)(2,1)} %get-tuple-element.25.v_hbm.refs_4_, bf16[32,64,640]{2,1,0:T(8,128)(2,1)} %get-tuple-element.26.um_hbm), custom_call_target="tpu_custom_call" | custom-call | flops 167772160 | bytes 20971520 | tf_op jit(solution)/shard_map/local_product/pallas_call | solution.py:438
  46.0 11.0 %all-to-all-done.1.refs_1_ = bf16[32,64,128]{2,1,0:T(8,128)(2,1)S(1)} async-done(((bf16[32,64,128]{2,1,0:T(8,128)(2,1)}), bf16[32,64,128]{2,1,0:T(8,128)(2,1)S(1)}, u32[]{:S(2)}, u32[]{:S(2)}) %all-to-all-start.1) | async-done | bytes 524320 | tf_op jit(solution)/shard_map/all_to_all | solution.py:412
  56.9 3.3 %second_step.1 = (bf16[32,2048]{1,0:T(8,128)(2,1)}, bf16[32,64,128]{2,1,0:T(8,128)(2,1)}) custom-call(s32[8192,128]{1,0:T(8,128)} %get-tuple-element.19.refs_0_.table_hbm, bf16[32,64,128]{2,1,0:T(8,128)(2,1)S(1)} %all-to-all-done.1.refs_1_, f32[1024,2048]{1,0:T(8,128)} %local_product.2.refs_2_, bf16[1024,2048]{1,0:T(8,128)(2,1)} %get-tuple-element.22.refs_3_.refs_4_, ...), custom_call_target="tpu_custom_call" | custom-call | tf_op jit(solution)/shard_map/second_step/pallas_call | solution.py:450
  60.3 5.6 %all-to-all-start.2 = ((bf16[32,64,128]{2,1,0:T(8,128)(2,1)}), bf16[32,64,128]{2,1,0:T(8,128)(2,1)S(1)}, u32[]{:S(2)}, u32[]{:S(2)}) async-start(bf16[32,64,128]{2,1,0:T(8,128)(2,1)} %get-tuple-element.28), calls=%async_computation.2 | async-start | bytes 1048576 | tf_op jit(solution)/shard_map/all_to_all | solution.py:412
  65.8 0.0 copy-start
  65.9 3.1 %collective-permute-start.2 = (bf16[32,2048]{1,0:T(8,128)(2,1)}, bf16[32,2048]{1,0:T(8,128)(2,1)S(1)}, u32[]{:S(2)}, u32[]{:S(2)}) collective-permute-start(bf16[32,2048]{1,0:T(8,128)(2,1)} %get-tuple-element.16.v_hbm.refs_0_), channel_id=1, source_target_pairs={{0,6},{2,0},{4,2},{6,4},{1,7},{3,1},{5,3},{7,5},{8,14},{10,8},{12,... | collective-permute-start | bytes 393224 | tf_op jit(solution)/shard_map/ppermute | solution.py:468
  68.9 0.6 collective-permute-start.1
  69.6 1.0 collective-permute-start
  70.5 0.0 collective-permute-start.3
  70.6 4.9 %local_product.3.y_hbm = f32[1024,2048]{1,0:T(8,128)} custom-call(s32[12,32]{1,0:T(8,128)} %bitcast.10, bf16[32,2048]{1,0:T(8,128)(2,1)} %get-tuple-element.16.v_hbm.refs_0_, bf16[32,64,640]{2,1,0:T(8,128)(2,1)} %get-tuple-element.26.um_hbm), custom_call_target="tpu_custom_call" | custom-call | flops 167772160 | bytes 20971520 | tf_op jit(solution)/shard_map/local_product/pallas_call | solution.py:438
  75.5 0.0 collective-permute-done.2.refs_3_
  75.5 0.2 collective-permute-done.1.refs_2_
  75.7 1.3 %collective-permute-done.refs_1_ = bf16[32,2048]{1,0:T(8,128)(2,1)S(1)} collective-permute-done((bf16[32,2048]{1,0:T(8,128)(2,1)}, bf16[32,2048]{1,0:T(8,128)(2,1)S(1)}, u32[]{:S(2)}, u32[]{:S(2)}) %collective-permute-start) | collective-permute-done | bytes 131104 | tf_op jit(solution)/shard_map/ppermute | solution.py:468
  77.0 0.0 collective-permute-start.4
  77.0 0.5 collective-permute-start.5
  77.5 0.0 collective-permute-start.6
  77.5 0.0 collective-permute-done.3.refs_4_
  77.6 0.8 collective-permute-done.4.refs_5_
  78.4 0.2 collective-permute-done.5.refs_6_
  78.6 0.3 collective-permute-done.6.refs_7_
  78.9 2.8 %all-to-all-done.2.recv_ref = bf16[32,64,128]{2,1,0:T(8,128)(2,1)S(1)} async-done(((bf16[32,64,128]{2,1,0:T(8,128)(2,1)}), bf16[32,64,128]{2,1,0:T(8,128)(2,1)S(1)}, u32[]{:S(2)}, u32[]{:S(2)}) %all-to-all-start.2) | async-done | bytes 524320 | tf_op jit(solution)/shard_map/all_to_all | solution.py:412
  81.7 0.0 copy-done
  81.7 3.4 %image.1 = bf16[8,64,256]{2,1,0:T(8,128)(2,1)S(1)} custom-call(s32[8192,128]{1,0:T(8,128)} %get-tuple-element.19.refs_0_.table_hbm, bf16[32,64,128]{2,1,0:T(8,128)(2,1)S(1)} %all-to-all-done.2.recv_ref, f32[1024,2048]{1,0:T(8,128)} %local_product.3.y_hbm, bf16[128,64,256]{2,1,0:T(8,128)(2,1)} %get-tuple-element.23.refs_5_.wd_hbm, ...), custom_call_target="tpu_custom_call" | custom-call | tf_op jit(solution)/shard_map/image/pallas_call | solution.py:473
  85.1 15.9 %all_to_all.25.in_ref = bf16[8,64,256]{2,1,0:T(8,128)(2,1)S(1)} all-to-all(bf16[8,64,256]{2,1,0:T(8,128)(2,1)S(1)} %image.1), channel_id=1, replica_groups=mesh['z'=8,'x'=4,'y'=4,'c'=2] {'z'}, dimensions={0} | all-to-all | bytes 524288 | tf_op jit(solution)/shard_map/all_to_all | solution.py:492
  101.1 9.1 %all_to_all.26.in_ref = bf16[4,64,256]{2,1,0:T(8,128)(2,1)S(1)} all-to-all(bf16[4,64,256]{2,1,0:T(8,128)(2,1)S(1)} %sum_z.1), channel_id=1, replica_groups=mesh['z'=8,'x'=4,'y'=4,'c'=2] {'x'}, dimensions={0} | all-to-all | bytes 262144 | tf_op jit(solution)/shard_map/all_to_all | solution.py:499
  110.2 0.6 sum_x.1
  (1 shorter events, 0.0 us)
Async XLA Ops:
  3.6 28.5 %all-to-all-start = ((bf16[32,64,128]{2,1,0:T(8,128)(2,1)}), bf16[32,64,128]{2,1,0:T(8,128)(2,1)S(1)}, u32[]{:S(2)}, u32[]{:S(2)}) async-start(bf16[32,64,128]{2,1,0:T(8,128)(2,1)} %get-tuple-element.20), calls=%async_computation | async-start | bytes 1048576 | tf_op jit(solution)/shard_map/all_to_all | solution.py:412
  35.4 21.5 %all-to-all-start.1 = ((bf16[32,64,128]{2,1,0:T(8,128)(2,1)}), bf16[32,64,128]{2,1,0:T(8,128)(2,1)S(1)}, u32[]{:S(2)}, u32[]{:S(2)}) async-start(bf16[32,64,128]{2,1,0:T(8,128)(2,1)} %get-tuple-element.24), calls=%async_computation.1 | async-start | bytes 1048576 | tf_op jit(solution)/shard_map/all_to_all | solution.py:412
  60.3 21.4 %all-to-all-start.2 = ((bf16[32,64,128]{2,1,0:T(8,128)(2,1)}), bf16[32,64,128]{2,1,0:T(8,128)(2,1)S(1)}, u32[]{:S(2)}, u32[]{:S(2)}) async-start(bf16[32,64,128]{2,1,0:T(8,128)(2,1)} %get-tuple-element.28), calls=%async_computation.2 | async-start | bytes 1048576 | tf_op jit(solution)/shard_map/all_to_all | solution.py:412
  65.8 15.9 %copy-start = (bf16[32,2048]{1,0:T(8,128)(2,1)S(1)}, bf16[32,2048]{1,0:T(8,128)(2,1)}, u32[]{:S(2)}) copy-start(bf16[32,2048]{1,0:T(8,128)(2,1)} %get-tuple-element.16.v_hbm.refs_0_) | copy-start | bytes 393220
  65.9 9.6 %collective-permute-start.2 = (bf16[32,2048]{1,0:T(8,128)(2,1)}, bf16[32,2048]{1,0:T(8,128)(2,1)S(1)}, u32[]{:S(2)}, u32[]{:S(2)}) collective-permute-start(bf16[32,2048]{1,0:T(8,128)(2,1)} %get-tuple-element.16.v_hbm.refs_0_), channel_id=1, source_target_pairs={{0,6},{2,0},{4,2},{6,4},{1,7},{3,1},{5,3},{7,5},{8,14},{10,8},{12,... | collective-permute-start | bytes 393224 | tf_op jit(solution)/shard_map/ppermute | solution.py:468
  68.9 6.8 %collective-permute-start.1 = (bf16[32,2048]{1,0:T(8,128)(2,1)}, bf16[32,2048]{1,0:T(8,128)(2,1)S(1)}, u32[]{:S(2)}, u32[]{:S(2)}) collective-permute-start(bf16[32,2048]{1,0:T(8,128)(2,1)} %get-tuple-element.16.v_hbm.refs_0_), channel_id=1, source_target_pairs={{0,4},{2,6},{4,0},{6,2},{1,5},{3,7},{5,1},{7,3},{8,12},{10,14},{12... | collective-permute-start | bytes 393224 | tf_op jit(solution)/shard_map/ppermute | solution.py:468
  69.6 7.5 %collective-permute-start = (bf16[32,2048]{1,0:T(8,128)(2,1)}, bf16[32,2048]{1,0:T(8,128)(2,1)S(1)}, u32[]{:S(2)}, u32[]{:S(2)}) collective-permute-start(bf16[32,2048]{1,0:T(8,128)(2,1)} %get-tuple-element.16.v_hbm.refs_0_), channel_id=1, source_target_pairs={{0,2},{2,4},{4,6},{6,0},{1,3},{3,5},{5,7},{7,1},{8,10},{10,12},{12... | collective-permute-start | bytes 393224 | tf_op jit(solution)/shard_map/ppermute | solution.py:468
  70.5 7.0 %collective-permute-start.3 = (bf16[32,2048]{1,0:T(8,128)(2,1)}, bf16[32,2048]{1,0:T(8,128)(2,1)S(1)}, u32[]{:S(2)}, u32[]{:S(2)}) collective-permute-start(bf16[32,2048]{1,0:T(8,128)(2,1)} %get-tuple-element.16.v_hbm.refs_0_), channel_id=1, source_target_pairs={{0,1},{1,0},{2,3},{3,2},{4,5},{5,4},{6,7},{7,6},{8,9},{9,8},{10,11... | collective-permute-start | bytes 393224 | tf_op jit(solution)/shard_map/ppermute | solution.py:472
  77.0 1.3 %collective-permute-start.4 = (bf16[32,2048]{1,0:T(8,128)(2,1)S(1)}, bf16[32,2048]{1,0:T(8,128)(2,1)S(1)}, u32[]{:S(2)}, u32[]{:S(2)}) collective-permute-start(bf16[32,2048]{1,0:T(8,128)(2,1)S(1)} %collective-permute-done.refs_1_), channel_id=1, source_target_pairs={{0,1},{1,0},{2,3},{3,2},{4,5},{5,4},{6,7},{7,6},{8,9},{9,8},{10,11... | collective-permute-start | bytes 393224 | tf_op jit(solution)/shard_map/ppermute | solution.py:472
  77.0 1.5 %collective-permute-start.5 = (bf16[32,2048]{1,0:T(8,128)(2,1)S(1)}, bf16[32,2048]{1,0:T(8,128)(2,1)S(1)}, u32[]{:S(2)}, u32[]{:S(2)}) collective-permute-start(bf16[32,2048]{1,0:T(8,128)(2,1)S(1)} %collective-permute-done.1.refs_2_), channel_id=1, source_target_pairs={{0,1},{1,0},{2,3},{3,2},{4,5},{5,4},{6,7},{7,6},{8,9},{9,8},{10,11... | collective-permute-start | bytes 393224 | tf_op jit(solution)/shard_map/ppermute | solution.py:472
  77.5 1.3 %collective-permute-start.6 = (bf16[32,2048]{1,0:T(8,128)(2,1)S(1)}, bf16[32,2048]{1,0:T(8,128)(2,1)S(1)}, u32[]{:S(2)}, u32[]{:S(2)}) collective-permute-start(bf16[32,2048]{1,0:T(8,128)(2,1)S(1)} %collective-permute-done.2.refs_3_), channel_id=1, source_target_pairs={{0,1},{1,0},{2,3},{3,2},{4,5},{5,4},{6,7},{7,6},{8,9},{9,8},{10,11... | collective-permute-start | bytes 393224 | tf_op jit(solution)/shard_map/ppermute | solution.py:472

commit v7 on v6

--- a/solution.py
+++ b/solution.py
@@ -315,23 +315,23 @@
     for copy in moves:
         copy.wait()
     part = dot(stack_ref[...], all_ref[...], NT).astype(bf16)
+    for x in range(NX):
+        out_ref[x] = part
+
+
+def sum_x_kernel(in_ref, out_ref):
+    total = in_ref[0].astype(f32)
+    for x in range(1, NX):
+        total = total + in_ref[x].astype(f32)
+    total = total.astype(bf16)
     for z in range(NZ):
-        out_ref[z] = part
-
-
-def sum_z_kernel(in_ref, out_ref):
+        out_ref[z] = total
+
+
+def sum_z_kernel(in_ref, gram_ref, proj_ref):
     total = in_ref[0].astype(f32)
     for z in range(1, NZ):
         total = total + in_ref[z].astype(f32)
-    total = total.astype(bf16)
-    for x in range(NX):
-        out_ref[x] = total
-
-
-def sum_x_kernel(in_ref, gram_ref, proj_ref):
-    total = in_ref[0].astype(f32)
-    for x in range(1, NX):
-        total = total + in_ref[x].astype(f32)
     gram_ref[...] = total[0:MC, :]
     proj_ref[...] = total[MC : 2 * MC, :]
 
@@ -472,7 +472,7 @@
     other = [lax.ppermute(block, "c", [(0, 1), (1, 0)]) for block in own]
     part = pl.pallas_call(
         image_kernel,
-        out_shape=shape((NZ, 2 * MC, NY * NC * MC), bf16),
+        out_shape=shape((NX, 2 * MC, NY * NC * MC), bf16),
         in_specs=[HBM, VM, HBM, HBM, HBM] + [ANY] * (2 * NY - 1),
         out_specs=VM,
         scratch_shapes=[
@@ -489,19 +489,19 @@
         compiler_params=limit(51.6),
         name="image",
     )(table, received, local, wd, *own, *other)
+    part = lax.all_to_all(part, "x", split_axis=0, concat_axis=0, tiled=True)
+    part = pl.pallas_call(
+        sum_x_kernel,
+        out_shape=shape((NZ,) + part.shape[1:], bf16),
+        compiler_params=limit(4),
+        name="sum_x",
+    )(part)
     part = lax.all_to_all(part, "z", split_axis=0, concat_axis=0, tiled=True)
-    part = pl.pallas_call(
+    gram, projected = pl.pallas_call(
         sum_z_kernel,
-        out_shape=shape((NX,) + part.shape[1:], bf16),
+        out_shape=(shape((MC, NY * NC * MC), f32),) * 2,
         compiler_params=limit(4),
         name="sum_z",
-    )(part)
-    part = lax.all_to_all(part, "x", split_axis=0, concat_axis=0, tiled=True)
-    gram, projected = pl.pallas_call(
-        sum_x_kernel,
-        out_shape=(shape((MC, NY * NC * MC), f32),) * 2,
-        compiler_params=limit(4),
-        name="sum_x",
     )(part)
     return filtered, gram.T, projected.T
 

time: 112 us -> 110 us (0.982)
  blocking collectives: 25 us -> 23.6 us
    all_to_all x1, blocking collectives: 15.9 us -> 14.5 us  [on_device(): part = lax.all_to_all(part, 'z', split_axis=0, concat_axis=0, tiled=True)]
  transfers between devices with their start and end apart: 10 -> 10, of which waited for: 8 -> 8; matrix products, arithmetic and copies ran while one was open for 0% -> 0% of each run, Pallas kernels for 15% -> 16%
where the time goes in v7:
time: 110 us; the launch traced here: 109 us
  Pallas kernels  30.9 us (28%)
  starting transfers between devices  28 us (25%)
  waiting for transfers between devices  26.1 us (24%)
  blocking collectives  23.6 us (21%)
    all_to_all x3, waiting for transfers between devices, exchange(): lax.all_to_all(message, row_axes, split_axis=0, concat_axis=0, tiled=True)  23.3 us
    all_to_all x3, starting transfers between devices, exchange(): lax.all_to_all(message, row_axes, split_axis=0, concat_axis=0, tiled=True)  22.8 us
    all_to_all x1, blocking collectives, on_device(): part = lax.all_to_all(part, 'z', split_axis=0, concat_axis=0, tiled=True)  14.5 us
    pallas_call x2, Pallas kernels, local_part(): pl.pallas_call(local_kernel, out_shape=shape((ROOM, width), f32), in_spec...  9.95 us
    all_to_all x1, blocking collectives, on_device(): part = lax.all_to_all(part, 'x', split_axis=0, concat_axis=0, tiled=True)  9.11 us
    pallas_call x1, Pallas kernels, on_device(): pl.pallas_call(first_local_kernel, out_shape=(um_shape, shape((ROOM, widt...  7.28 us
    pallas_call x2, Pallas kernels, next_step(): pl.pallas_call(lambda *refs: step_kernel(second, *refs), out_shape=(shape...  6.65 us
    ppermute x3, starting transfers between devices, on_device(): lax.ppermute(filtered, 'y', [(y, (y + d) % NY) for y in range(NY)])  4.7 us
  transfers between devices with their start and end apart: 10, of which 8 were waited for; matrix products, arithmetic and copies ran while one was open for 0% of the time, Pallas kernels for 16%

profile of v7, /device:TPU:2, one launch (start us, length us, event | category | flops | bytes accessed | tf_op | source)
XLA Modules:
  0.0 109.4 jit_solution(2089446320853473874)
XLA Ops:
  0.6 3.0 %first_message.1 = (bf16[32,64,128]{2,1,0:T(8,128)(2,1)}, bf16[128,64,256]{2,1,0:T(8,128)(2,1)}, s32[8192,128]{1,0:T(8,128)}, bf16[1024,2048]{1,0:T(8,128)(2,1)}) custom-call(s32[12,32]{1,0:T(8,128)} %bitcast.7, s32[1,64]{1,0:T(1,128)} %bitcast.11, bf16[32,2048]{1,0:T(8,128)(2,1)} %v_hbm.3, bf16[12,32,4096]{2,1,0:T(8,128)(2,1)} %bitcast.5), custom_call_target="tpu_custom_call" | custom-call | tf_op jit(solution)/shard_map/first_message/pallas_call | solution.py:380
  3.6 11.6 %all-to-all-start = ((bf16[32,64,128]{2,1,0:T(8,128)(2,1)}), bf16[32,64,128]{2,1,0:T(8,128)(2,1)S(1)}, u32[]{:S(2)}, u32[]{:S(2)}) async-start(bf16[32,64,128]{2,1,0:T(8,128)(2,1)} %get-tuple-element.20), calls=%async_computation | async-start | bytes 1048576 | tf_op jit(solution)/shard_map/all_to_all | solution.py:412
  15.3 7.3 %first_local.1 = (bf16[32,64,640]{2,1,0:T(8,128)(2,1)}, f32[1024,2048]{1,0:T(8,128)}) custom-call(s32[12,32]{1,0:T(8,128)} %bitcast.8, s32[32]{0:T(128)} %counts_hbm.1, bf16[32,2048]{1,0:T(8,128)(2,1)} %v_hbm.3, bf16[12,32,4096]{2,1,0:T(8,128)(2,1)} %bitcast.6), custom_call_target="tpu_custom_call" | custom-call | tf_op jit(solution)/shard_map/first_local/pallas_call | solution.py:416
  22.5 9.5 %all-to-all-done.refs_1_ = bf16[32,64,128]{2,1,0:T(8,128)(2,1)S(1)} async-done(((bf16[32,64,128]{2,1,0:T(8,128)(2,1)}), bf16[32,64,128]{2,1,0:T(8,128)(2,1)S(1)}, u32[]{:S(2)}, u32[]{:S(2)}) %all-to-all-start) | async-done | bytes 524320 | tf_op jit(solution)/shard_map/all_to_all | solution.py:412
  32.1 3.3 %first_step.1 = (bf16[1024,2048]{1,0:T(8,128)(2,1)}, bf16[32,64,128]{2,1,0:T(8,128)(2,1)}) custom-call(s32[8192,128]{1,0:T(8,128)} %get-tuple-element.19.refs_0_.table_hbm, bf16[32,64,128]{2,1,0:T(8,128)(2,1)S(1)} %all-to-all-done.refs_1_, f32[1024,2048]{1,0:T(8,128)} %get-tuple-element.21.refs_2_, bf16[1024,2048]{1,0:T(8,128)(2,1)} %get-tuple-element.22.refs_3_.refs_4_, ...), custom_call_target="tpu_custom_call" | custom-call | tf_op jit(solution)/shard_map/first_step/pallas_call | solution.py:450
  35.4 5.6 %all-to-all-start.1 = ((bf16[32,64,128]{2,1,0:T(8,128)(2,1)}), bf16[32,64,128]{2,1,0:T(8,128)(2,1)S(1)}, u32[]{:S(2)}, u32[]{:S(2)}) async-start(bf16[32,64,128]{2,1,0:T(8,128)(2,1)} %get-tuple-element.24), calls=%async_computation.1 | async-start | bytes 1048576 | tf_op jit(solution)/shard_map/all_to_all | solution.py:412
  41.0 4.9 %local_product.2.refs_2_ = f32[1024,2048]{1,0:T(8,128)} custom-call(s32[12,32]{1,0:T(8,128)} %bitcast.9, bf16[1024,2048]{1,0:T(8,128)(2,1)} %get-tuple-element.25.v_hbm.refs_4_, bf16[32,64,640]{2,1,0:T(8,128)(2,1)} %get-tuple-element.26.um_hbm), custom_call_target="tpu_custom_call" | custom-call | flops 167772160 | bytes 20971520 | tf_op jit(solution)/shard_map/local_product/pallas_call | solution.py:438
  46.0 11.0 %all-to-all-done.1.refs_1_ = bf16[32,64,128]{2,1,0:T(8,128)(2,1)S(1)} async-done(((bf16[32,64,128]{2,1,0:T(8,128)(2,1)}), bf16[32,64,128]{2,1,0:T(8,128)(2,1)S(1)}, u32[]{:S(2)}, u32[]{:S(2)}) %all-to-all-start.1) | async-done | bytes 524320 | tf_op jit(solution)/shard_map/all_to_all | solution.py:412
  56.9 3.3 %second_step.1 = (bf16[32,2048]{1,0:T(8,128)(2,1)}, bf16[32,64,128]{2,1,0:T(8,128)(2,1)}) custom-call(s32[8192,128]{1,0:T(8,128)} %get-tuple-element.19.refs_0_.table_hbm, bf16[32,64,128]{2,1,0:T(8,128)(2,1)S(1)} %all-to-all-done.1.refs_1_, f32[1024,2048]{1,0:T(8,128)} %local_product.2.refs_2_, bf16[1024,2048]{1,0:T(8,128)(2,1)} %get-tuple-element.22.refs_3_.refs_4_, ...), custom_call_target="tpu_custom_call" | custom-call | tf_op jit(solution)/shard_map/second_step/pallas_call | solution.py:450
  60.3 5.6 %all-to-all-start.2 = ((bf16[32,64,128]{2,1,0:T(8,128)(2,1)}), bf16[32,64,128]{2,1,0:T(8,128)(2,1)S(1)}, u32[]{:S(2)}, u32[]{:S(2)}) async-start(bf16[32,64,128]{2,1,0:T(8,128)(2,1)} %get-tuple-element.28), calls=%async_computation.2 | async-start | bytes 1048576 | tf_op jit(solution)/shard_map/all_to_all | solution.py:412
  65.8 0.0 copy-start
  65.9 3.1 %collective-permute-start.2 = (bf16[32,2048]{1,0:T(8,128)(2,1)}, bf16[32,2048]{1,0:T(8,128)(2,1)S(1)}, u32[]{:S(2)}, u32[]{:S(2)}) collective-permute-start(bf16[32,2048]{1,0:T(8,128)(2,1)} %get-tuple-element.16.v_hbm.refs_0_), channel_id=1, source_target_pairs={{0,6},{2,0},{4,2},{6,4},{1,7},{3,1},{5,3},{7,5},{8,14},{10,8},{12,... | collective-permute-start | bytes 393224 | tf_op jit(solution)/shard_map/ppermute | solution.py:468
  68.9 0.6 collective-permute-start.1
  69.6 1.0 collective-permute-start
  70.6 0.0 collective-permute-start.3
  70.6 5.0 %local_product.3.y_hbm = f32[1024,2048]{1,0:T(8,128)} custom-call(s32[12,32]{1,0:T(8,128)} %bitcast.10, bf16[32,2048]{1,0:T(8,128)(2,1)} %get-tuple-element.16.v_hbm.refs_0_, bf16[32,64,640]{2,1,0:T(8,128)(2,1)} %get-tuple-element.26.um_hbm), custom_call_target="tpu_custom_call" | custom-call | flops 167772160 | bytes 20971520 | tf_op jit(solution)/shard_map/local_product/pallas_call | solution.py:438
  75.6 0.0 collective-permute-done.2.refs_3_
  75.6 0.2 collective-permute-done.1.refs_2_
  75.7 1.3 %collective-permute-done.refs_1_ = bf16[32,2048]{1,0:T(8,128)(2,1)S(1)} collective-permute-done((bf16[32,2048]{1,0:T(8,128)(2,1)}, bf16[32,2048]{1,0:T(8,128)(2,1)S(1)}, u32[]{:S(2)}, u32[]{:S(2)}) %collective-permute-start) | collective-permute-done | bytes 131104 | tf_op jit(solution)/shard_map/ppermute | solution.py:468
  77.0 0.0 collective-permute-start.4
  77.0 0.5 collective-permute-start.5
  77.5 0.0 collective-permute-start.6
  77.6 0.0 collective-permute-done.3.refs_4_
  77.6 0.8 collective-permute-done.4.refs_5_
  78.4 0.2 collective-permute-done.5.refs_6_
  78.6 0.3 collective-permute-done.6.refs_7_
  78.9 2.8 %all-to-all-done.2.recv_ref = bf16[32,64,128]{2,1,0:T(8,128)(2,1)S(1)} async-done(((bf16[32,64,128]{2,1,0:T(8,128)(2,1)}), bf16[32,64,128]{2,1,0:T(8,128)(2,1)S(1)}, u32[]{:S(2)}, u32[]{:S(2)}) %all-to-all-start.2) | async-done | bytes 524320 | tf_op jit(solution)/shard_map/all_to_all | solution.py:412
  81.7 0.0 copy-done
  81.7 3.4 %image.1 = bf16[4,64,256]{2,1,0:T(8,128)(2,1)S(1)} custom-call(s32[8192,128]{1,0:T(8,128)} %get-tuple-element.19.refs_0_.table_hbm, bf16[32,64,128]{2,1,0:T(8,128)(2,1)S(1)} %all-to-all-done.2.recv_ref, f32[1024,2048]{1,0:T(8,128)} %local_product.3.y_hbm, bf16[128,64,256]{2,1,0:T(8,128)(2,1)} %get-tuple-element.23.refs_5_.wd_hbm, ...), custom_call_target="tpu_custom_call" | custom-call | tf_op jit(solution)/shard_map/image/pallas_call | solution.py:473
  85.1 9.1 %all_to_all.25.in_ref = bf16[4,64,256]{2,1,0:T(8,128)(2,1)S(1)} all-to-all(bf16[4,64,256]{2,1,0:T(8,128)(2,1)S(1)} %image.1), channel_id=1, replica_groups=mesh['z'=8,'x'=4,'y'=4,'c'=2] {'x'}, dimensions={0} | all-to-all | bytes 262144 | tf_op jit(solution)/shard_map/all_to_all | solution.py:492
  94.3 14.5 %all_to_all.26.in_ref = bf16[8,64,256]{2,1,0:T(8,128)(2,1)S(1)} all-to-all(bf16[8,64,256]{2,1,0:T(8,128)(2,1)S(1)} %sum_x.1), channel_id=1, replica_groups=mesh['z'=8,'x'=4,'y'=4,'c'=2] {'z'}, dimensions={0} | all-to-all | bytes 524288 | tf_op jit(solution)/shard_map/all_to_all | solution.py:499
  108.8 0.7 sum_z.1
  (1 shorter events, 0.0 us)
Async XLA Ops:
  3.6 28.5 %all-to-all-start = ((bf16[32,64,128]{2,1,0:T(8,128)(2,1)}), bf16[32,64,128]{2,1,0:T(8,128)(2,1)S(1)}, u32[]{:S(2)}, u32[]{:S(2)}) async-start(bf16[32,64,128]{2,1,0:T(8,128)(2,1)} %get-tuple-element.20), calls=%async_computation | async-start | bytes 1048576 | tf_op jit(solution)/shard_map/all_to_all | solution.py:412
  35.4 21.5 %all-to-all-start.1 = ((bf16[32,64,128]{2,1,0:T(8,128)(2,1)}), bf16[32,64,128]{2,1,0:T(8,128)(2,1)S(1)}, u32[]{:S(2)}, u32[]{:S(2)}) async-start(bf16[32,64,128]{2,1,0:T(8,128)(2,1)} %get-tuple-element.24), calls=%async_computation.1 | async-start | bytes 1048576 | tf_op jit(solution)/shard_map/all_to_all | solution.py:412
  60.3 21.4 %all-to-all-start.2 = ((bf16[32,64,128]{2,1,0:T(8,128)(2,1)}), bf16[32,64,128]{2,1,0:T(8,128)(2,1)S(1)}, u32[]{:S(2)}, u32[]{:S(2)}) async-start(bf16[32,64,128]{2,1,0:T(8,128)(2,1)} %get-tuple-element.28), calls=%async_computation.2 | async-start | bytes 1048576 | tf_op jit(solution)/shard_map/all_to_all | solution.py:412
  65.8 15.9 %copy-start = (bf16[32,2048]{1,0:T(8,128)(2,1)S(1)}, bf16[32,2048]{1,0:T(8,128)(2,1)}, u32[]{:S(2)}) copy-start(bf16[32,2048]{1,0:T(8,128)(2,1)} %get-tuple-element.16.v_hbm.refs_0_) | copy-start | bytes 393220
  65.9 9.7 %collective-permute-start.2 = (bf16[32,2048]{1,0:T(8,128)(2,1)}, bf16[32,2048]{1,0:T(8,128)(2,1)S(1)}, u32[]{:S(2)}, u32[]{:S(2)}) collective-permute-start(bf16[32,2048]{1,0:T(8,128)(2,1)} %get-tuple-element.16.v_hbm.refs_0_), channel_id=1, source_target_pairs={{0,6},{2,0},{4,2},{6,4},{1,7},{3,1},{5,3},{7,5},{8,14},{10,8},{12,... | collective-permute-start | bytes 393224 | tf_op jit(solution)/shard_map/ppermute | solution.py:468
  68.9 6.8 %collective-permute-start.1 = (bf16[32,2048]{1,0:T(8,128)(2,1)}, bf16[32,2048]{1,0:T(8,128)(2,1)S(1)}, u32[]{:S(2)}, u32[]{:S(2)}) collective-permute-start(bf16[32,2048]{1,0:T(8,128)(2,1)} %get-tuple-element.16.v_hbm.refs_0_), channel_id=1, source_target_pairs={{0,4},{2,6},{4,0},{6,2},{1,5},{3,7},{5,1},{7,3},{8,12},{10,14},{12... | collective-permute-start | bytes 393224 | tf_op jit(solution)/shard_map/ppermute | solution.py:468
  69.6 7.5 %collective-permute-start = (bf16[32,2048]{1,0:T(8,128)(2,1)}, bf16[32,2048]{1,0:T(8,128)(2,1)S(1)}, u32[]{:S(2)}, u32[]{:S(2)}) collective-permute-start(bf16[32,2048]{1,0:T(8,128)(2,1)} %get-tuple-element.16.v_hbm.refs_0_), channel_id=1, source_target_pairs={{0,2},{2,4},{4,6},{6,0},{1,3},{3,5},{5,7},{7,1},{8,10},{10,12},{12... | collective-permute-start | bytes 393224 | tf_op jit(solution)/shard_map/ppermute | solution.py:468
  70.6 7.0 %collective-permute-start.3 = (bf16[32,2048]{1,0:T(8,128)(2,1)}, bf16[32,2048]{1,0:T(8,128)(2,1)S(1)}, u32[]{:S(2)}, u32[]{:S(2)}) collective-permute-start(bf16[32,2048]{1,0:T(8,128)(2,1)} %get-tuple-element.16.v_hbm.refs_0_), channel_id=1, source_target_pairs={{0,1},{1,0},{2,3},{3,2},{4,5},{5,4},{6,7},{7,6},{8,9},{9,8},{10,11... | collective-permute-start | bytes 393224 | tf_op jit(solution)/shard_map/ppermute | solution.py:472
  77.0 1.3 %collective-permute-start.4 = (bf16[32,2048]{1,0:T(8,128)(2,1)S(1)}, bf16[32,2048]{1,0:T(8,128)(2,1)S(1)}, u32[]{:S(2)}, u32[]{:S(2)}) collective-permute-start(bf16[32,2048]{1,0:T(8,128)(2,1)S(1)} %collective-permute-done.refs_1_), channel_id=1, source_target_pairs={{0,1},{1,0},{2,3},{3,2},{4,5},{5,4},{6,7},{7,6},{8,9},{9,8},{10,11... | collective-permute-start | bytes 393224 | tf_op jit(solution)/shard_map/ppermute | solution.py:472
  77.0 1.5 %collective-permute-start.5 = (bf16[32,2048]{1,0:T(8,128)(2,1)S(1)}, bf16[32,2048]{1,0:T(8,128)(2,1)S(1)}, u32[]{:S(2)}, u32[]{:S(2)}) collective-permute-start(bf16[32,2048]{1,0:T(8,128)(2,1)S(1)} %collective-permute-done.1.refs_2_), channel_id=1, source_target_pairs={{0,1},{1,0},{2,3},{3,2},{4,5},{5,4},{6,7},{7,6},{8,9},{9,8},{10,11... | collective-permute-start | bytes 393224 | tf_op jit(solution)/shard_map/ppermute | solution.py:472
  77.5 1.3 %collective-permute-start.6 = (bf16[32,2048]{1,0:T(8,128)(2,1)S(1)}, bf16[32,2048]{1,0:T(8,128)(2,1)S(1)}, u32[]{:S(2)}, u32[]{:S(2)}) collective-permute-start(bf16[32,2048]{1,0:T(8,128)(2,1)S(1)} %collective-permute-done.2.refs_3_), channel_id=1, source_target_pairs={{0,1},{1,0},{2,3},{3,2},{4,5},{5,4},{6,7},{7,6},{8,9},{9,8},{10,11... | collective-permute-start | bytes 393224 | tf_op jit(solution)/shard_map/ppermute | solution.py:472

commit v8 on v7

--- a/solution.py
+++ b/solution.py
@@ -12,6 +12,7 @@
 PEERS = 32
 NZ, NX, NY, NC = 8, 4, 4, 2
 STRIDE = 40
+SHIFTS = (0, 1, 3, 2)
 ROOM = 1024
 TABLE = 8192
 LOCAL = ((0, 3), (4, 5), (6, 7), (8, 9), (10, 11))
@@ -303,7 +304,7 @@
     y, c = lax.axis_index("y"), lax.axis_index("c")
     moves = [start(own[0], stack_ref.at[0:MC, :])]
     for d in range(NY):
-        from_y = lax.rem(y + NY - d, NY) * NC
+        from_y = lax.rem(y + NY - SHIFTS[d], NY) * NC
         for block, core in ((own[d], c), (other[d], 1 - c)):
             moves.append(start(block, all_ref.at[pl.ds(pl.multiple_of((from_y + core) * MC, MC), MC), :]))
     table.wait()
@@ -465,7 +466,7 @@
     received = exchange(message)
     local = local_part(filtered)
     own = [filtered] + [
-        lax.ppermute(filtered, "y", [(y, (y + d) % NY) for y in range(NY)]) for d in range(1, NY)
+        lax.ppermute(filtered, "y", [(y, (y + d) % NY) for y in range(NY)]) for d in SHIFTS[1:]
     ]
     local, *passed = lax.optimization_barrier((local, *own[1:]))
     own = own[:1] + passed

time: 110 us -> 110 us (level)
  transfers between devices with their start and end apart: 10 -> 10, of which waited for: 8 -> 7; matrix products, arithmetic and copies ran while one was open for 0% -> 0% of each run, Pallas kernels for 16% -> 16%
where the time goes in v8:
time: 110 us; the launch traced here: 109 us
  Pallas kernels  30.9 us (28%)
  starting transfers between devices  28.8 us (26%)
  waiting for transfers between devices  25.4 us (23%)
  blocking collectives  23.2 us (21%)
    all_to_all x3, waiting for transfers between devices, exchange(): lax.all_to_all(message, row_axes, split_axis=0, concat_axis=0, tiled=True)  23.8 us
    all_to_all x3, starting transfers between devices, exchange(): lax.all_to_all(message, row_axes, split_axis=0, concat_axis=0, tiled=True)  22.8 us
    all_to_all x1, blocking collectives, on_device(): part = lax.all_to_all(part, 'z', split_axis=0, concat_axis=0, tiled=True)  14 us
    pallas_call x2, Pallas kernels, local_part(): pl.pallas_call(local_kernel, out_shape=shape((ROOM, width), f32), in_spec...  9.88 us
    all_to_all x1, blocking collectives, on_device(): part = lax.all_to_all(part, 'x', split_axis=0, concat_axis=0, tiled=True)  9.12 us
    pallas_call x1, Pallas kernels, on_device(): pl.pallas_call(first_local_kernel, out_shape=(um_shape, shape((ROOM, widt...  7.28 us
    pallas_call x2, Pallas kernels, next_step(): pl.pallas_call(lambda *refs: step_kernel(second, *refs), out_shape=(shape...  6.65 us
    ppermute x3, starting transfers between devices, on_device(): lax.ppermute(filtered, 'y', [(y, (y + d) % NY) for y in range(NY)])  5.3 us
  transfers between devices with their start and end apart: 10, of which 7 were waited for; matrix products, arithmetic and copies ran while one was open for 0% of the time, Pallas kernels for 16%

profile of v8, /device:TPU:2, one launch (start us, length us, event | category | flops | bytes accessed | tf_op | source)
XLA Modules:
  0.0 109.0 jit_solution(15459259967151970503)
XLA Ops:
  0.6 3.0 %first_message.1 = (bf16[32,64,128]{2,1,0:T(8,128)(2,1)}, bf16[128,64,256]{2,1,0:T(8,128)(2,1)}, s32[8192,128]{1,0:T(8,128)}, bf16[1024,2048]{1,0:T(8,128)(2,1)}) custom-call(s32[12,32]{1,0:T(8,128)} %bitcast.7, s32[1,64]{1,0:T(1,128)} %bitcast.11, bf16[32,2048]{1,0:T(8,128)(2,1)} %v_hbm.3, bf16[12,32,4096]{2,1,0:T(8,128)(2,1)} %bitcast.5), custom_call_target="tpu_custom_call" | custom-call | tf_op jit(solution)/shard_map/first_message/pallas_call | solution.py:381
  3.6 11.6 %all-to-all-start = ((bf16[32,64,128]{2,1,0:T(8,128)(2,1)}), bf16[32,64,128]{2,1,0:T(8,128)(2,1)S(1)}, u32[]{:S(2)}, u32[]{:S(2)}) async-start(bf16[32,64,128]{2,1,0:T(8,128)(2,1)} %get-tuple-element.20), calls=%async_computation | async-start | bytes 1048576 | tf_op jit(solution)/shard_map/all_to_all | solution.py:413
  15.3 7.3 %first_local.1 = (bf16[32,64,640]{2,1,0:T(8,128)(2,1)}, f32[1024,2048]{1,0:T(8,128)}) custom-call(s32[12,32]{1,0:T(8,128)} %bitcast.8, s32[32]{0:T(128)} %counts_hbm.1, bf16[32,2048]{1,0:T(8,128)(2,1)} %v_hbm.3, bf16[12,32,4096]{2,1,0:T(8,128)(2,1)} %bitcast.6), custom_call_target="tpu_custom_call" | custom-call | tf_op jit(solution)/shard_map/first_local/pallas_call | solution.py:417
  22.5 9.5 %all-to-all-done.refs_1_ = bf16[32,64,128]{2,1,0:T(8,128)(2,1)S(1)} async-done(((bf16[32,64,128]{2,1,0:T(8,128)(2,1)}), bf16[32,64,128]{2,1,0:T(8,128)(2,1)S(1)}, u32[]{:S(2)}, u32[]{:S(2)}) %all-to-all-start) | async-done | bytes 524320 | tf_op jit(solution)/shard_map/all_to_all | solution.py:413
  32.1 3.3 %first_step.1 = (bf16[1024,2048]{1,0:T(8,128)(2,1)}, bf16[32,64,128]{2,1,0:T(8,128)(2,1)}) custom-call(s32[8192,128]{1,0:T(8,128)} %get-tuple-element.19.refs_0_.table_hbm, bf16[32,64,128]{2,1,0:T(8,128)(2,1)S(1)} %all-to-all-done.refs_1_, f32[1024,2048]{1,0:T(8,128)} %get-tuple-element.21.refs_2_, bf16[1024,2048]{1,0:T(8,128)(2,1)} %get-tuple-element.22.refs_3_.refs_4_, ...), custom_call_target="tpu_custom_call" | custom-call | tf_op jit(solution)/shard_map/first_step/pallas_call | solution.py:451
  35.4 5.6 %all-to-all-start.1 = ((bf16[32,64,128]{2,1,0:T(8,128)(2,1)}), bf16[32,64,128]{2,1,0:T(8,128)(2,1)S(1)}, u32[]{:S(2)}, u32[]{:S(2)}) async-start(bf16[32,64,128]{2,1,0:T(8,128)(2,1)} %get-tuple-element.24), calls=%async_computation.1 | async-start | bytes 1048576 | tf_op jit(solution)/shard_map/all_to_all | solution.py:413
  41.0 4.9 %local_product.2.refs_2_ = f32[1024,2048]{1,0:T(8,128)} custom-call(s32[12,32]{1,0:T(8,128)} %bitcast.9, bf16[1024,2048]{1,0:T(8,128)(2,1)} %get-tuple-element.25.v_hbm.refs_4_, bf16[32,64,640]{2,1,0:T(8,128)(2,1)} %get-tuple-element.26.um_hbm), custom_call_target="tpu_custom_call" | custom-call | flops 167772160 | bytes 20971520 | tf_op jit(solution)/shard_map/local_product/pallas_call | solution.py:439
  46.0 11.0 %all-to-all-done.1.refs_1_ = bf16[32,64,128]{2,1,0:T(8,128)(2,1)S(1)} async-done(((bf16[32,64,128]{2,1,0:T(8,128)(2,1)}), bf16[32,64,128]{2,1,0:T(8,128)(2,1)S(1)}, u32[]{:S(2)}, u32[]{:S(2)}) %all-to-all-start.1) | async-done | bytes 524320 | tf_op jit(solution)/shard_map/all_to_all | solution.py:413
  56.9 3.3 %second_step.1 = (bf16[32,2048]{1,0:T(8,128)(2,1)}, bf16[32,64,128]{2,1,0:T(8,128)(2,1)}) custom-call(s32[8192,128]{1,0:T(8,128)} %get-tuple-element.19.refs_0_.table_hbm, bf16[32,64,128]{2,1,0:T(8,128)(2,1)S(1)} %all-to-all-done.1.refs_1_, f32[1024,2048]{1,0:T(8,128)} %local_product.2.refs_2_, bf16[1024,2048]{1,0:T(8,128)(2,1)} %get-tuple-element.22.refs_3_.refs_4_, ...), custom_call_target="tpu_custom_call" | custom-call | tf_op jit(solution)/shard_map/second_step/pallas_call | solution.py:451
  60.3 5.6 %all-to-all-start.2 = ((bf16[32,64,128]{2,1,0:T(8,128)(2,1)}), bf16[32,64,128]{2,1,0:T(8,128)(2,1)S(1)}, u32[]{:S(2)}, u32[]{:S(2)}) async-start(bf16[32,64,128]{2,1,0:T(8,128)(2,1)} %get-tuple-element.28), calls=%async_computation.2 | async-start | bytes 1048576 | tf_op jit(solution)/shard_map/all_to_all | solution.py:413
  65.8 0.0 copy-start
  65.9 3.3 %collective-permute-start.2 = (bf16[32,2048]{1,0:T(8,128)(2,1)}, bf16[32,2048]{1,0:T(8,128)(2,1)S(1)}, u32[]{:S(2)}, u32[]{:S(2)}) collective-permute-start(bf16[32,2048]{1,0:T(8,128)(2,1)} %get-tuple-element.16.v_hbm.refs_0_), channel_id=1, source_target_pairs={{0,4},{2,6},{4,0},{6,2},{1,5},{3,7},{5,1},{7,3},{8,12},{10,14},{12... | collective-permute-start | bytes 393224 | tf_op jit(solution)/shard_map/ppermute | solution.py:469
  69.1 1.1 collective-permute-start.1
  70.2 1.0 collective-permute-start
  71.2 0.0 collective-permute-start.3
  71.2 4.9 %local_product.3.y_hbm = f32[1024,2048]{1,0:T(8,128)} custom-call(s32[12,32]{1,0:T(8,128)} %bitcast.10, bf16[32,2048]{1,0:T(8,128)(2,1)} %get-tuple-element.16.v_hbm.refs_0_, bf16[32,64,640]{2,1,0:T(8,128)(2,1)} %get-tuple-element.26.um_hbm), custom_call_target="tpu_custom_call" | custom-call | flops 167772160 | bytes 20971520 | tf_op jit(solution)/shard_map/local_product/pallas_call | solution.py:439
  76.1 0.0 collective-permute-done.2.refs_3_
  76.1 0.0 collective-permute-done.1.refs_2_
  76.1 0.4 collective-permute-done.refs_1_
  76.6 0.2 collective-permute-start.4
  76.7 0.3 collective-permute-start.5
  77.1 0.2 collective-permute-start.6
  77.3 0.0 collective-permute-done.3.refs_4_
  77.3 0.7 collective-permute-done.4.refs_5_
  77.9 0.2 collective-permute-done.5.refs_6_
  78.1 0.3 collective-permute-done.6.refs_7_
  78.4 3.3 %all-to-all-done.2.recv_ref = bf16[32,64,128]{2,1,0:T(8,128)(2,1)S(1)} async-done(((bf16[32,64,128]{2,1,0:T(8,128)(2,1)}), bf16[32,64,128]{2,1,0:T(8,128)(2,1)S(1)}, u32[]{:S(2)}, u32[]{:S(2)}) %all-to-all-start.2) | async-done | bytes 524320 | tf_op jit(solution)/shard_map/all_to_all | solution.py:413
  81.7 0.0 copy-done
  81.7 3.4 %image.1 = bf16[4,64,256]{2,1,0:T(8,128)(2,1)S(1)} custom-call(s32[8192,128]{1,0:T(8,128)} %get-tuple-element.19.refs_0_.table_hbm, bf16[32,64,128]{2,1,0:T(8,128)(2,1)S(1)} %all-to-all-done.2.recv_ref, f32[1024,2048]{1,0:T(8,128)} %local_product.3.y_hbm, bf16[128,64,256]{2,1,0:T(8,128)(2,1)} %get-tuple-element.23.refs_5_.wd_hbm, ...), custom_call_target="tpu_custom_call" | custom-call | tf_op jit(solution)/shard_map/image/pallas_call | solution.py:474
  85.1 9.1 %all_to_all.25.in_ref = bf16[4,64,256]{2,1,0:T(8,128)(2,1)S(1)} all-to-all(bf16[4,64,256]{2,1,0:T(8,128)(2,1)S(1)} %image.1), channel_id=1, replica_groups=mesh['z'=8,'x'=4,'y'=4,'c'=2] {'x'}, dimensions={0} | all-to-all | bytes 262144 | tf_op jit(solution)/shard_map/all_to_all | solution.py:493
  94.3 14.0 %all_to_all.26.in_ref = bf16[8,64,256]{2,1,0:T(8,128)(2,1)S(1)} all-to-all(bf16[8,64,256]{2,1,0:T(8,128)(2,1)S(1)} %sum_x.1), channel_id=1, replica_groups=mesh['z'=8,'x'=4,'y'=4,'c'=2] {'z'}, dimensions={0} | all-to-all | bytes 524288 | tf_op jit(solution)/shard_map/all_to_all | solution.py:500
  108.3 0.7 sum_z.1
  (1 shorter events, 0.0 us)
Async XLA Ops:
  3.6 28.5 %all-to-all-start = ((bf16[32,64,128]{2,1,0:T(8,128)(2,1)}), bf16[32,64,128]{2,1,0:T(8,128)(2,1)S(1)}, u32[]{:S(2)}, u32[]{:S(2)}) async-start(bf16[32,64,128]{2,1,0:T(8,128)(2,1)} %get-tuple-element.20), calls=%async_computation | async-start | bytes 1048576 | tf_op jit(solution)/shard_map/all_to_all | solution.py:413
  35.4 21.5 %all-to-all-start.1 = ((bf16[32,64,128]{2,1,0:T(8,128)(2,1)}), bf16[32,64,128]{2,1,0:T(8,128)(2,1)S(1)}, u32[]{:S(2)}, u32[]{:S(2)}) async-start(bf16[32,64,128]{2,1,0:T(8,128)(2,1)} %get-tuple-element.24), calls=%async_computation.1 | async-start | bytes 1048576 | tf_op jit(solution)/shard_map/all_to_all | solution.py:413
  60.3 21.4 %all-to-all-start.2 = ((bf16[32,64,128]{2,1,0:T(8,128)(2,1)}), bf16[32,64,128]{2,1,0:T(8,128)(2,1)S(1)}, u32[]{:S(2)}, u32[]{:S(2)}) async-start(bf16[32,64,128]{2,1,0:T(8,128)(2,1)} %get-tuple-element.28), calls=%async_computation.2 | async-start | bytes 1048576 | tf_op jit(solution)/shard_map/all_to_all | solution.py:413
  65.8 15.9 %copy-start = (bf16[32,2048]{1,0:T(8,128)(2,1)S(1)}, bf16[32,2048]{1,0:T(8,128)(2,1)}, u32[]{:S(2)}) copy-start(bf16[32,2048]{1,0:T(8,128)(2,1)} %get-tuple-element.16.v_hbm.refs_0_) | copy-start | bytes 393220
  65.9 10.3 %collective-permute-start.2 = (bf16[32,2048]{1,0:T(8,128)(2,1)}, bf16[32,2048]{1,0:T(8,128)(2,1)S(1)}, u32[]{:S(2)}, u32[]{:S(2)}) collective-permute-start(bf16[32,2048]{1,0:T(8,128)(2,1)} %get-tuple-element.16.v_hbm.refs_0_), channel_id=1, source_target_pairs={{0,4},{2,6},{4,0},{6,2},{1,5},{3,7},{5,1},{7,3},{8,12},{10,14},{12... | collective-permute-start | bytes 393224 | tf_op jit(solution)/shard_map/ppermute | solution.py:469
  69.1 7.0 %collective-permute-start.1 = (bf16[32,2048]{1,0:T(8,128)(2,1)}, bf16[32,2048]{1,0:T(8,128)(2,1)S(1)}, u32[]{:S(2)}, u32[]{:S(2)}) collective-permute-start(bf16[32,2048]{1,0:T(8,128)(2,1)} %get-tuple-element.16.v_hbm.refs_0_), channel_id=1, source_target_pairs={{0,6},{2,0},{4,2},{6,4},{1,7},{3,1},{5,3},{7,5},{8,14},{10,8},{12,... | collective-permute-start | bytes 393224 | tf_op jit(solution)/shard_map/ppermute | solution.py:469
  70.2 6.4 %collective-permute-start = (bf16[32,2048]{1,0:T(8,128)(2,1)}, bf16[32,2048]{1,0:T(8,128)(2,1)S(1)}, u32[]{:S(2)}, u32[]{:S(2)}) collective-permute-start(bf16[32,2048]{1,0:T(8,128)(2,1)} %get-tuple-element.16.v_hbm.refs_0_), channel_id=1, source_target_pairs={{0,2},{2,4},{4,6},{6,0},{1,3},{3,5},{5,7},{7,1},{8,10},{10,12},{12... | collective-permute-start | bytes 393224 | tf_op jit(solution)/shard_map/ppermute | solution.py:469
  71.2 6.1 %collective-permute-start.3 = (bf16[32,2048]{1,0:T(8,128)(2,1)}, bf16[32,2048]{1,0:T(8,128)(2,1)S(1)}, u32[]{:S(2)}, u32[]{:S(2)}) collective-permute-start(bf16[32,2048]{1,0:T(8,128)(2,1)} %get-tuple-element.16.v_hbm.refs_0_), channel_id=1, source_target_pairs={{0,1},{1,0},{2,3},{3,2},{4,5},{5,4},{6,7},{7,6},{8,9},{9,8},{10,11... | collective-permute-start | bytes 393224 | tf_op jit(solution)/shard_map/ppermute | solution.py:473
  76.6 1.3 %collective-permute-start.4 = (bf16[32,2048]{1,0:T(8,128)(2,1)S(1)}, bf16[32,2048]{1,0:T(8,128)(2,1)S(1)}, u32[]{:S(2)}, u32[]{:S(2)}) collective-permute-start(bf16[32,2048]{1,0:T(8,128)(2,1)S(1)} %collective-permute-done.refs_1_), channel_id=1, source_target_pairs={{0,1},{1,0},{2,3},{3,2},{4,5},{5,4},{6,7},{7,6},{8,9},{9,8},{10,11... | collective-permute-start | bytes 393224 | tf_op jit(solution)/shard_map/ppermute | solution.py:473
  76.7 1.4 %collective-permute-start.5 = (bf16[32,2048]{1,0:T(8,128)(2,1)S(1)}, bf16[32,2048]{1,0:T(8,128)(2,1)S(1)}, u32[]{:S(2)}, u32[]{:S(2)}) collective-permute-start(bf16[32,2048]{1,0:T(8,128)(2,1)S(1)} %collective-permute-done.1.refs_2_), channel_id=1, source_target_pairs={{0,1},{1,0},{2,3},{3,2},{4,5},{5,4},{6,7},{7,6},{8,9},{9,8},{10,11... | collective-permute-start | bytes 393224 | tf_op jit(solution)/shard_map/ppermute | solution.py:473
  77.1 1.3 %collective-permute-start.6 = (bf16[32,2048]{1,0:T(8,128)(2,1)S(1)}, bf16[32,2048]{1,0:T(8,128)(2,1)S(1)}, u32[]{:S(2)}, u32[]{:S(2)}) collective-permute-start(bf16[32,2048]{1,0:T(8,128)(2,1)S(1)} %collective-permute-done.2.refs_3_), channel_id=1, source_target_pairs={{0,1},{1,0},{2,3},{3,2},{4,5},{5,4},{6,7},{7,6},{8,9},{9,8},{10,11... | collective-permute-start | bytes 393224 | tf_op jit(solution)/shard_map/ppermute | solution.py:473
